TPU v7x, 32 devices: a whole 2x2x4 slice. The times are simulated.
32 devices in a mesh: rows: 8 (over z, y), width: 4 (over x, core).
Axes of the slice: x: 2, y: 2, z: 4, core: 2. Of those that a mesh axis runs over, the one named last changes fastest.
Arguments:
- inputs: bfloat16 [16384, 512], P('rows'), may hold values from -6 to 6
- w_first: bfloat16 [8, 512, 256], P('width'), may hold values from -0.25 to 0.25
- w_second: bfloat16 [8, 256, 256], P('width'), may hold values from -0.375 to 0.375
- w_gate: bfloat16 [3, 512, 8], replicated, may hold values from -0.1875 to 0.1875
- w_tower: bfloat16 [3, 256, 128], replicated, may hold values from -0.375 to 0.375
- norm_scale: float32 [3, 128], replicated, may hold values from 0.5 to 1.5
- norm_shift: float32 [3, 128], replicated, may hold values from -1 to 1
- w_head: float32 [3, 128], replicated, may hold values from -1 to 1
- domains: int32 [16384], P(('rows', 'width')), may hold values from 0 to 2
- labels: int32 [16384], P(('rows', 'width')), may hold values 0 or 1
Outputs:
- mean_loss: float32 [], replicated
- grad_inputs: float32 [16384, 512], P(('rows', 'width'))
- grad_first: float32 [8, 512, 256], P('width')
- grad_second: float32 [8, 256, 256], P('width')
- grad_gate: float32 [3, 512, 8], replicated
- grad_tower: float32 [3, 256, 128], replicated
- grad_scale: float32 [3, 128], replicated
- grad_shift: float32 [3, 128], replicated
- grad_head: float32 [3, 128], replicated
Inputs may be any that keep to these rules, and one draw needn't show every extreme that they name: `domains`: a domain number.
All inputs are finite; a program needn't handle non-finite values. No bound on the sum of `labels` on one device may be relied on, other than what follows from the above.
Results may differ from a plain program's by a relative error of at most 0.0074.
Values may be sent and summed in bfloat16 or wider, within the bound.
No kernel may reach another device: no remote copies, remote signals or barrier semaphores. Data moves between devices by JAX's collectives and lax.ppermute only.
A program may use at most 64 MiB of HBM per device.

v0:
```python
import math

import jax
import jax.numpy as jnp
from jax import lax
from jax.experimental import pallas as pl
from jax.experimental.pallas import tpu as pltpu
from jax.sharding import PartitionSpec as P

F32 = jnp.float32
BF16 = jnp.bfloat16
EPS = 1e-05
LANE = 128
MIB = 1 << 20
ROWS = "rows"
WIDTH = "width"
BOTH = (ROWS, WIDTH)


def mm(a, b):
    return jnp.dot(a, b, preferred_element_type=F32)


def mm_t(a, b):
    return lax.dot_general(a, b, (((1,), (1,)), ((), ())), preferred_element_type=F32)


def sigmoid(v):
    return 0.5 * jnp.tanh(0.5 * v) + 0.5


class Source:
    def __init__(self, buf, copies):
        self.buf = buf
        self.waiting = copies
        for copy in copies:
            copy.start()

    def get(self):
        for copy in self.waiting:
            copy.wait()
        self.waiting = []
        return self.buf


class Target:
    def __init__(self, ref, buf, sems):
        self.ref, self.buf, self.sems = ref, buf, sems
        self.waiting = []

    def flush(self, *at):
        if self.ref is None:
            return
        src = self.buf.at[at] if at else self.buf
        dst = self.ref.at[at] if at else self.ref
        copy = pltpu.make_async_copy(src, dst, next(self.sems))
        copy.start()
        self.waiting.append(copy)


class Near:
    def __init__(self, what):
        self.what = what


class Far:
    def __init__(self, arrays, shape=None, pairs=None, moved=False, into=None):
        self.moved = moved
        self.into = into
        self.arrays = arrays if isinstance(arrays, (list, tuple)) else [arrays]
        self.shape = shape or self.arrays[0].shape
        self.dtype = self.arrays[0].dtype
        self.pairs = pairs or (lambda refs, buf: [(refs[0], buf)])


def staged(body, ins, outs, scratch, name, limit, n_sems=64):
    far_in = [i for i, s in enumerate(ins) if isinstance(s, Far) and s.into is None]
    far_out = [i for i, s in enumerate(outs) if not isinstance(s, Near)]
    args, specs, spans = [], [], []
    hbm = pl.BlockSpec(memory_space=pltpu.HBM)
    vmem = pl.BlockSpec(memory_space=pltpu.VMEM)
    anywhere = pl.BlockSpec(memory_space=pl.ANY)
    for s in ins:
        if isinstance(s, Far):
            spans.append((len(args), len(args) + len(s.arrays)))
            if s.moved:
                args += s.arrays
                specs += [anywhere] * len(s.arrays)
                continue
            args += [pltpu.with_memory_space_constraint(a, pltpu.HBM) for a in s.arrays]
            specs += [hbm] * len(s.arrays)
        else:
            spans.append((len(args), len(args) + 1))
            args.append(s.what)
            specs.append(vmem)
    n_in, n_out = len(args), len(outs)

    def kernel(*refs):
        refs_in, refs_out = refs[:n_in], refs[n_in : n_in + n_out]
        bufs = refs[n_in + n_out :]
        in_bufs = dict(zip(far_in, bufs))
        in_bufs.update({i: refs_out[s.into] for i, s in enumerate(ins) if isinstance(s, Far) and s.into is not None})
        out_bufs = dict(zip(far_out, bufs[len(far_in) :]))
        rest = bufs[len(far_in) + len(far_out) : -1]
        sems = iter([bufs[-1].at[i] for i in range(n_sems)])
        sources = []
        for i, (start, stop) in enumerate(spans):
            if i in in_bufs:
                pairs = ins[i].pairs(refs_in[start:stop], in_bufs[i])
                sources.append(Source(in_bufs[i], [pltpu.make_async_copy(a, b, next(sems)) for a, b in pairs]))
            else:
                sources.append(Source(refs_in[start], []))
        targets = []
        for i, ref in enumerate(refs_out):
            targets.append(Target(ref, out_bufs[i], sems) if i in out_bufs else Target(None, ref, sems))
        body(sources, targets, *rest)
        for s in sources:
            s.get()
        for t in targets:
            for copy in t.waiting:
                copy.wait()

    return pl.pallas_call(
        kernel,
        out_shape=[o.what if isinstance(o, Near) else pltpu.HBM(o.shape, o.dtype) for o in outs],
        in_specs=specs,
        out_specs=[hbm if i in far_out else vmem for i in range(n_out)],
        scratch_shapes=[pltpu.VMEM(ins[i].shape, ins[i].dtype) for i in far_in]
        + [pltpu.VMEM(outs[i].shape, outs[i].dtype) for i in far_out]
        + list(scratch)
        + [pltpu.SemaphoreType.DMA((n_sems,))],
        compiler_params=pltpu.CompilerParams(vmem_limit_bytes=limit * MIB),
        name=name,
    )(*args)


def plain(shape, dtype):
    return jax.ShapeDtypeStruct(shape, dtype)


def row_blocks(slots, own):
    def pairs(refs, buf):
        w = lax.axis_index(WIDTH)
        got = []
        for n, s in enumerate(slots):
            start = pl.multiple_of(lax.bitwise_xor(w, 2 * s) * own, own)
            got.append((refs[0].at[pl.ds(start, own), :], buf.at[n * own : (n + 1) * own, :]))
        return got

    return pairs


def reorder(ke, epd):
    first = lax.axis_index(WIDTH) * epd
    down = lax.broadcasted_iota(jnp.int32, (ke, ke), 0)
    across = lax.broadcasted_iota(jnp.int32, (ke, ke), 1)
    return jnp.where(lax.bitwise_xor(down, first) == across, 1.0, 0.0).astype(BF16)


def prepare(slots, inputs, w1, w2, wgate_t, wtower, own):
    dim = inputs.shape[1]
    epd, _, hid_n = w1.shape
    out_n = w2.shape[2]
    ke = wgate_t.shape[0]
    doms, _, th = wtower.shape

    def body(ins, outs):
        w1s, wgs, w2s, wts, _ = ins
        _, w1t, w2t, wt = (o.buf for o in outs)
        w1_buf = w1s.get()
        for i in range(epd):
            w1t[i * hid_n : (i + 1) * hid_n, :] = w1_buf[i].T
        w1t[epd * hid_n :, :] = mm(reorder(ke, epd), wgs.get()[...]).astype(BF16)
        w2_buf = w2s.get()
        for i in range(epd):
            w2t[i] = w2_buf[i].T
        wt_buf = wts.get()
        for k in range(doms):
            wt[k] = wt_buf[k].T
    return staged(
        body,
        [Far(a) for a in (w1, wgate_t, w2, wtower)]
        + [Far(inputs, (len(slots) * own, dim), row_blocks(slots, own), into=0)],
        [
            Near(plain((len(slots) * own, dim), BF16)),
            Near(plain((epd * hid_n + ke, dim), BF16)),
            Near(plain((epd, out_n, hid_n), BF16)),
            Near(plain((doms, th, out_n), BF16)),
        ],
        [],
        "prepare",
        12,
    )


def forward(blocks, w1, w2, wt, own, doms, keep, tower_out, name):
    epd, dim, hid_n = w1[1].shape
    out_n = w2[1].shape[2]
    ce = 2 * epd
    half = epd * hid_n
    ke = w1[0].shape[0] - half
    th = wt.shape[1]
    exps = ke // doms
    sizes = [(b.what if isinstance(b, Near) else b).shape[0] // own for b in blocks]
    ns = sum(sizes)

    def body(ins, outs, w1t, w2t, pre, *bufs):
        xs = ins[: len(blocks)]
        w1o, w1s, w2o, w2s, wts = ins[len(blocks) :]
        if keep:
            hid, slope, vals, gate, mixed = (o.buf for o in outs[:5])
        else:
            hid, vals, gate, mixed = bufs
        wt = wts.get()
        for i in range(epd):
            w1t[i * hid_n : (i + 1) * hid_n, :] = w1s.get()[i].T
            w2t[i] = w2s.get()[i].T
        parts = [(src, n) for src, size in zip(xs, sizes) for n in range(size)]
        for n, (src, place) in enumerate(parts):
            x = src.get()[place * own : (place + 1) * own, :]
            got = mm_t(w1o.get()[...], x)
            pre[:half, :] = got[:half]
            pre[ce * hid_n :, :] = got[half:]
            pre[half : ce * hid_n, :] = mm_t(w1t[...], x)
            logits = pre[ce * hid_n : ce * hid_n + ke, :].reshape(doms, exps, own)
            top = jnp.exp(logits - jnp.max(logits, axis=1, keepdims=True))
            soft = top / jnp.sum(top, axis=1, keepdims=True)
            gate[n] = soft.reshape(ke, own)

            def act(i, carry):
                at = pl.ds(pl.multiple_of(i * 16, 16), 16)
                v = pre[at, :]
                s = sigmoid(v)
                h = v * s
                hid[n, at, :] = h.astype(BF16)
                if keep:
                    slope[n, at, :] = (s + h * (1.0 - s)).astype(BF16)
                return carry

            lax.fori_loop(0, ce * hid_n // 16, act, 0, unroll=4 if keep else ce * hid_n // 16)
            for e in range(ce):
                w = w2o.get()[e] if e < epd else w2t[e - epd]
                vals[n, e * out_n : (e + 1) * out_n, :] = mm(w, hid[n, e * hid_n : (e + 1) * hid_n, :]).astype(BF16)
            if keep:
                for o in outs[:4]:
                    o.flush(n)
            for u in range(own // LANE):
                part = slice(u * LANE, (u + 1) * LANE)
                rows = [[gate[n, k * exps + e : k * exps + e + 1, part] for e in range(ce)] for k in range(doms)]

                def mix(i, carry):
                    acc = [None] * doms
                    for e in range(ce):
                        at = pl.ds(pl.multiple_of(e * out_n + i * 32, 32), 32)
                        v = vals[n, at, part].astype(F32)
                        for k in range(doms):
                            term = rows[k][e] * v
                            acc[k] = term if e == 0 else acc[k] + term
                    for k in range(doms):
                        at = pl.ds(pl.multiple_of(k * out_n + i * 32, 32), 32)
                        mixed[n, at, part] = acc[k].astype(BF16)
                    return carry

                lax.fori_loop(0, out_n // 32, mix, 0, unroll=4 if keep else out_n // 32)
            if keep:
                outs[4].flush(n)
            if n == 0 or not keep:
                tower = outs[-1]
                for k in range(doms):
                    tower.buf[n, k * th : (k + 1) * th, :] = mm(
                        wt[k], mixed[n, k * out_n : (k + 1) * out_n, :]
                    ).astype(tower_out)
                tower.flush(n)

    kept = [
        plain((ns, ce * hid_n, own), BF16),
        plain((ns, ce * hid_n, own), BF16),
        plain((ns, ce * out_n, own), BF16),
        plain((ns, ke, own), F32),
        plain((ns, doms * out_n, own), BF16),
    ]
    outs = list(kept) if keep else []
    outs.append(Near(plain((1 if keep else ns, doms * th, own), tower_out)))
    scratch = [
        pltpu.VMEM((half, dim), BF16),
        pltpu.VMEM((epd, out_n, hid_n), BF16),
        pltpu.VMEM((ce * hid_n + ke, own), F32),
    ]
    if not keep:
        scratch += [pltpu.VMEM(kept[i].shape, kept[i].dtype) for i in (0, 2, 3, 4)]
    ins = blocks + [Near(a) for a in (w1[0], w1[1], w2[0], w2[1], wt)]
    return staged(body, ins, outs, scratch, name, 40)


def combine(own_part, received, marks, devices):
    _, rows, own = own_part.shape
    doms = rows // LANE

    def body(ins, outs, cols):
        part = ins[0].get()
        got = [s.get() for s in ins[2:]]
        tower, low, message = (o.buf for o in outs)
        cols[...] = jnp.zeros_like(cols)
        for k in range(doms):
            at = slice(k * LANE, (k + 1) * LANE)
            total = part[0, at, :]
            for ref in got:
                total = total + ref[0, at, :].astype(F32)
            tower[at, :] = total
            low[at, :] = total.astype(BF16)
            mean = jnp.sum(total, axis=1, keepdims=True) * (1.0 / own)
            dev = total - mean
            cols[:, k : k + 1] = mean
            cols[:, doms + k : doms + k + 1] = jnp.sum(dev * dev, axis=1, keepdims=True)
        outs[0].flush()
        pair = jnp.concatenate([ins[1].get()[...].astype(F32), jnp.zeros((14, own), F32)], axis=0)
        low[rows:, :] = pair.astype(BF16)
        outs[1].flush()
        tile = cols[...].T[:8, :]
        for d in range(devices):
            message[d * 8 : (d + 1) * 8, :] = tile
        outs[2].flush()

    return staged(
        body,
        [Near(own_part), Far(marks)] + [Near(v) for v in received],
        [Near(plain((rows, own), F32)), Near(plain((rows + 16, own), BF16)), Near(plain((devices * 8, LANE), F32))],
        [pltpu.VMEM((LANE, LANE), F32)],
        "combine",
        16,
    )


def pick(dom, values):
    got = values[-1]
    for k in range(len(values) - 2, -1, -1):
        got = jnp.where(dom == k, values[k], got)
    return got


def chosen_tower(tower, dom, wide, lanes, doms):
    values = [tower[k * LANE : (k + 1) * LANE, lanes].astype(F32) for k in range(doms)]
    mean, gain, shift, head = (pick(dom, [wide[j * doms + k] for k in range(doms)]) for j in range(4))
    centred = pick(dom, values) - mean
    return values, centred, centred * gain + shift, gain, head


def spread_columns(wide, rows_ref, n):
    cols = rows_ref[...].T
    for j in range(n):
        wide[j] = jnp.broadcast_to(cols[:, j : j + 1], (LANE, LANE))


def normalise(stats, tower, marks, scale, shift, head, devices, count):
    rows, own = tower.shape
    doms = rows // LANE

    def body(ins, outs, prm, wide, q):
        st, tws, mks, sc, sh, hd = ins
        params, message = (o.buf for o in outs)
        prm[...] = jnp.zeros_like(prm)
        got = st.get()[...].reshape(devices, 8, LANE)
        total = jnp.sum(got, axis=0)
        mean = total * (1.0 / devices)
        dev = got - mean[None]
        spread = jnp.sum(dev * dev, axis=0) * float(own)
        var = (total[doms : 2 * doms] + spread[:doms]) * (1.0 / count)
        inv = lax.rsqrt(var + EPS)
        prm[0:doms, :] = mean[:doms]
        prm[doms : 2 * doms, :] = inv * sc.get()[...]
        prm[2 * doms : 3 * doms, :] = sh.get()[...]
        prm[3 * doms : 4 * doms, :] = hd.get()[...]
        prm[4 * doms : 5 * doms, :] = inv
        params[:16, :] = prm[:16, :]
        spread_columns(wide, prm, 4 * doms)
        tw, mk = tws.get(), mks.get()
        loss = jnp.zeros((1, LANE), F32)
        for u in range(own // LANE):
            part = slice(u * LANE, (u + 1) * LANE)
            dom = mk[0:1, part]
            target = mk[1:2, part].astype(F32)
            _, centred, affine, _, head_w = chosen_tower(tw, dom, wide, part, doms)
            s = sigmoid(affine)
            act = affine * s
            chosen = jnp.sum(act * head_w, axis=0, keepdims=True)
            soft = jnp.maximum(chosen, 0.0) + jnp.log(1.0 + jnp.exp(-jnp.abs(chosen)))
            loss = loss + (soft - target * chosen)
            score_grad = (sigmoid(chosen) - target) * (1.0 / count)
            grad = score_grad * head_w * (s + act * (1.0 - s))
            q[0:LANE, part] = grad
            q[LANE : 2 * LANE, part] = grad * centred
            q[2 * LANE :, part] = score_grad * act
        kinds = lax.broadcasted_iota(jnp.int32, (8, own), 0)
        one_hot = (kinds == mk[0:1, :]).astype(F32).astype(BF16)
        high = q[...].astype(BF16)
        sums = (mm_t(one_hot, high) + mm_t(one_hot, (q[...] - high.astype(F32)).astype(BF16)))[:doms]
        tile = [sums[:, :LANE], sums[:, LANE : 2 * LANE] * inv]
        all_rows = tile + [loss, jnp.zeros((1, LANE), F32)]
        twice = jnp.concatenate(all_rows + all_rows, axis=0).astype(BF16)
        for d in range(devices // 2):
            message[d * 16 : (d + 1) * 16, :] = twice
        params[16:, :] = jnp.concatenate([sums[:, 2 * LANE :], jnp.zeros((8 - doms, LANE), F32)], axis=0)
        outs[0].flush()

    return staged(
        body,
        [Near(stats), Near(tower), Far(marks), Far(scale), Far(shift), Far(head)],
        [Near(plain((24, LANE), F32)), Near(plain((devices * 8, LANE), BF16))],
        [
            pltpu.VMEM((LANE, LANE), F32),
            pltpu.VMEM((4 * doms, LANE, LANE), F32),
            pltpu.VMEM((3 * LANE, own), F32),
        ],
        "normalise",
        16,
    )


def layout(epd, hid_n, out_n, dim, doms, rows_n):
    second = epd * hid_n * out_n // LANE
    first = epd * hid_n * dim // LANE
    towers = -(-(doms * out_n + (dim // LANE) * 32) // (2 * 16 * rows_n)) * 16
    return second // rows_n, first // rows_n, towers


def pieces(kind, epd, hid_n, out_n, dim):
    flat = 0
    for i in range(epd):
        for q in range((out_n, dim)[kind] // LANE):
            yield i, q, flat
            flat += hid_n


def spots(kind, row, rows_n):
    got = []
    for j in range(rows_n):
        p = lax.bitwise_xor(row, j)
        got.append(p if kind == 0 else (p & 1) * (rows_n // 2) + lax.shift_right_logical(p, 1))
    return got


def backward(sums, params, tower, low_towers, marks, acts, inputs, w2, wgate_t, wtower, devices, rows_n, count):
    ns = 1 + len(low_towers)
    t_rows, own = tower.shape
    total_n = ns * own
    dim = inputs.shape[1]
    epd, hid_n, out_n = w2[0].shape
    ce = 2 * epd
    ke = wgate_t.shape[0]
    doms, _, th = wtower.shape
    exps = ke // doms
    m_sec, m_first, m_tow = layout(epd, hid_n, out_n, dim, doms, rows_n)

    def body(ins, outs, wide, prm, tg, mg, eg, gg, srow, tgf, facc):
        sm, pr, tw0, mk0 = ins[:4]
        low = ins[4 : 3 + ns]
        wts, gate, vals, w2o, w2s, slope, xs, hid, mixed = ins[3 + ns :]
        shift_out, scale_out, loss_out, sec_sib, first_sib, sec_mine, first_mine, tow_sib, tow_mine, pgs, lgs = outs
        pg, lg = pgs.buf, lgs.buf
        c = lax.rem(lax.axis_index(WIDTH), 2)
        r = lax.axis_index(ROWS)
        at_row = [spots(kind, r, rows_n) for kind in range(2)]
        prm[...] = jnp.zeros_like(prm)
        total = jnp.sum(sm.get()[...].astype(F32).reshape(devices, 8, LANE), axis=0)
        shift_out.buf[...] = total[:doms]
        scale_out.buf[...] = total[doms : 2 * doms]
        loss_out.buf[...] = jnp.sum(total[2 * doms : 2 * doms + 1, :], axis=1, keepdims=True) * (1.0 / count)
        for target in (shift_out, scale_out, loss_out):
            target.flush()
        given = pr.get()[...]
        gain, inv = given[doms : 2 * doms], given[4 * doms : 5 * doms]
        prm[0:16, :] = given[:16]
        prm[4 * doms : 5 * doms, :] = gain * total[:doms] * (1.0 / count)
        prm[5 * doms : 6 * doms, :] = gain * inv * total[doms : 2 * doms] * (1.0 / count)
        spread_columns(wide, prm, 6 * doms)
        for u in range(total_n // LANE):
            n = u * LANE // own
            part = slice(u * LANE, (u + 1) * LANE)
            here = slice(u * LANE - n * own, (u + 1) * LANE - n * own)
            if n == 0:
                tw = tw0.get()
                dom = mk0.get()[0:1, here]
                target = mk0.get()[1:2, here].astype(F32)
            else:
                tw = low[n - 1].get()
                pair = tw[t_rows : t_rows + 16, here].astype(F32)
                dom = pair[0:1].astype(jnp.int32)
                target = pair[1:2]
            values, _, affine, gain_s, head_w = chosen_tower(tw, dom, wide, here, doms)
            s = sigmoid(affine)
            a = affine * s
            chosen = jnp.sum(a * head_w, axis=0, keepdims=True)
            score_grad = (sigmoid(chosen) - target) * (1.0 / count)
            grad = gain_s * (score_grad * head_w * (s + a * (1.0 - s)))
            for k in range(doms):
                v = jnp.where(dom == k, grad, 0.0) - wide[4 * doms + k]
                v = v - (values[k] - wide[k]) * wide[5 * doms + k]
                down = v.astype(BF16)
                tg[k * th : (k + 1) * th, part] = down
                srow[k : k + 1, part] = jnp.sum(down.astype(F32) * values[k], axis=0, keepdims=True)
        wt = wts.get()
        for k in range(doms):
            mg[k * out_n : (k + 1) * out_n, :] = mm(wt[k], tg[k * th : (k + 1) * th, :])
        vals, gate = vals.get(), gate.get()
        gg[...] = jnp.zeros_like(gg)

        def tower_part(k):
            tgf[k * out_n : (k + 1) * out_n, :] = mm_t(
                mixed.get()[k * out_n : (k + 1) * out_n, :], tg[k * th : (k + 1) * th, :]
            )

        def hidden_part(n, e):
            at = slice(e * hid_n, (e + 1) * hid_n)
            part = slice(n * own, (n + 1) * own)
            w = (w2o, w2s)[e // epd].get()[e % epd]
            grad = mm(w, eg[e * out_n : (e + 1) * out_n, part])
            pg[at, part] = (grad * slope.get()[at, part].astype(F32)).astype(BF16)

        ready = []
        for u in range(total_n // LANE):
            part = slice(u * LANE, (u + 1) * LANE)
            rows = [[gate[k * exps + e : k * exps + e + 1, part] for e in range(ce)] for k in range(doms)]

            def spread(i, acc):
                up = [mg[pl.ds(pl.multiple_of(k * out_n + i * 16, 16), 16), part] for k in range(doms)]
                acc = list(acc)
                for e in range(ce):
                    at = pl.ds(pl.multiple_of(e * out_n + i * 16, 16), 16)
                    v = vals[at, part].astype(F32)
                    back = None
                    for k in range(doms):
                        term = rows[k][e] * up[k]
                        back = term if k == 0 else back + term
                        prod = up[k] * v
                        acc[k * ce + e] = acc[k * ce + e] + (prod[:8] + prod[8:])
                    eg[at, part] = back.astype(BF16)
                return tuple(acc)

            zero = jnp.zeros((8, LANE), F32)
            acc = lax.fori_loop(0, out_n // 16, spread, (zero,) * (doms * ce), unroll=out_n // 16)
            for k in range(doms):
                for e in range(ce):
                    gg[k * exps + e : k * exps + e + 1, part] = jnp.sum(acc[k * ce + e], axis=0, keepdims=True)
            if (u + 1) * LANE % own == 0:
                ready += [(hidden_part, (u * LANE // own, e)) for e in range(ce)]
            if ready:
                task, args = ready.pop(0)
                task(*args)
        for task, args in ready:
            task(*args)
        pgs.flush()
        here = lax.broadcasted_iota(jnp.int32, (exps, total_n), 0) < ce
        for k in range(doms):
            at = slice(k * exps, (k + 1) * exps)
            gg[at, :] = jnp.where(here, gate[at, :] * (gg[at, :] - srow[k : k + 1, :]), 0.0)
        lg[...] = mm(reorder(ke, epd), gg[...].astype(BF16)).astype(BF16)
        lgs.flush()
        hid = hid.get()

        def put(kind, slot, values):
            target = ((sec_sib, first_sib), (sec_mine, first_mine))[slot < epd][kind]
            size = (m_sec, m_first)[kind]
            step = math.gcd(size, hid_n)
            for i, q, flat in pieces(kind, epd, hid_n, out_n, dim):
                if i == slot % epd:
                    for off in range(0, hid_n, step):
                        j, o = divmod(flat + off, size)
                        part = values[off : off + step, q * LANE : (q + 1) * LANE]
                        target.buf[at_row[kind][j], o : o + step, :] = part.astype(BF16)

        x = xs.get()
        facc[...] = mm(pg[...], x[...])
        for e in range(ce):
            put(1, e, facc[e * hid_n : (e + 1) * hid_n, :])
        for e in range(ce):
            at = slice(e * hid_n, (e + 1) * hid_n)
            at_o = slice(e * out_n, (e + 1) * out_n)
            put(0, e, mm_t(hid[at, :], eg[at_o, :]))
        for target in (sec_sib, first_sib, sec_mine, first_mine):
            target.flush()
        for k in range(doms):
            tower_part(k)
        tgf[doms * out_n :, :] = jnp.zeros((tgf.shape[0] - doms * out_n, LANE), F32)
        part_g = mm(lg[...], x[...])
        for q in range(dim // LANE):
            tgf[doms * out_n + q * 32 : doms * out_n + q * 32 + ke, :] = part_g[:, q * LANE : (q + 1) * LANE]
        tgf[doms * out_n + ke : doms * out_n + 32, :] = given[16 : 48 - ke]
        for target, core in ((tow_sib, 1 - c), (tow_mine, c)):
            for j in range(rows_n):
                start = pl.multiple_of((core * rows_n + j) * m_tow, 8)
                target.buf[at_row[1][j], :, :] = tgf[pl.ds(start, m_tow), :].astype(BF16)
            target.flush()

    outs = [
        plain((doms, LANE), F32),
        plain((doms, LANE), F32),
        plain((1, 1), F32),
        Near(plain((rows_n, m_sec, LANE), BF16)),
        Near(plain((rows_n, m_first, LANE), BF16)),
        Near(plain((rows_n, m_sec, LANE), BF16)),
        Near(plain((rows_n, m_first, LANE), BF16)),
        Near(plain((rows_n, m_tow, LANE), BF16)),
        Near(plain((rows_n, m_tow, LANE), BF16)),
        Near(plain((ce * hid_n, total_n), BF16)),
        Near(plain((ke, total_n), BF16)),
    ]
    scratch = [
        pltpu.VMEM((6 * doms, LANE, LANE), F32),
        pltpu.VMEM((LANE, LANE), F32),
        pltpu.VMEM((doms * th, total_n), BF16),
        pltpu.VMEM((doms * out_n, total_n), F32),
        pltpu.VMEM((ce * out_n, total_n), BF16),
        pltpu.VMEM((ke, total_n), F32),
        pltpu.VMEM((8, total_n), F32),
        pltpu.VMEM((2 * rows_n * m_tow, LANE), F32),
        pltpu.VMEM((ce * hid_n, dim), F32),
    ]

    def side_by_side(which):
        def pairs(refs, buf):
            return [(r.at[n], buf.at[:, i * own : (i + 1) * own]) for i, (r, (_, n)) in enumerate(zip(refs, acts))]

        arrays = [a[which] for a, _ in acts]
        return Far(arrays, (arrays[0].shape[1], total_n), pairs)

    ins = [Near(sums), Near(params), Near(tower), Far(marks)]
    ins += [Far(v, moved=True) for v in low_towers]
    ins += [Far(wtower), side_by_side(3), side_by_side(2), Far(w2[0]), Far(w2[1], moved=True), side_by_side(1)]
    ins += [Far(inputs, (total_n, dim), row_blocks(list(range(ns)), own)), side_by_side(0), side_by_side(4)]
    return staged(body, ins, outs, scratch, "backward", 44)


def backward_inputs(pg, lg, w1, wgate_t, own):
    total_n = pg.shape[1]
    ns = total_n // own
    epd, dim, hid_n = w1[0].shape
    ce = 2 * epd
    ke = wgate_t.shape[0]

    def body(ins, outs, w1c):
        w1o, w1s, wgs, pgs, lgs = ins
        wg = jnp.concatenate([wgs.get()[...], jnp.zeros((LANE - ke, dim), BF16)], axis=0).T[:, :ke]
        for g, src in enumerate((w1o, w1s)):
            ref = src.get()
            for i in range(epd):
                e = g * epd + i
                w1c[:, e * hid_n : (e + 1) * hid_n] = ref[i]
        pg, lg = pgs.get(), lgs.get()
        for n in range(ns - 1, -1, -1):
            part = slice(n * own, (n + 1) * own)
            gi = mm(w1c[...], pg[:, part]) + mm(wg, lg[:, part])
            if n:
                outs[1].buf[n - 1] = gi.astype(BF16)
                outs[1].flush(n - 1)
            else:
                outs[0].buf[...] = gi
                outs[0].flush()

    return staged(
        body,
        [Far(w1[0]), Far(w1[1], moved=True), Far(wgate_t), Near(pg), Near(lg)],
        [Near(plain((dim, own), F32)), Near(plain((max(ns - 1, 1), dim, own), BF16))],
        [pltpu.VMEM((dim, ce * hid_n), BF16)],
        "backward_inputs",
        16,
    )


def finish_inputs(own_part, received):
    dim, own = own_part.shape

    def body(ins, outs):
        for u in range(own // LANE):
            lanes = slice(u * LANE, (u + 1) * LANE)
            part = total(*(src.buf[:, lanes] for src in ins))
            outs[0].buf[lanes, :] = part.T
            outs[0].flush(pl.ds(u * LANE, LANE))

    return staged(
        body, [Near(own_part)] + [Near(v) for v in received], [plain((own, dim), F32)], [], "finish_inputs", 12
    )[0]


def finish_weights(second, first, other, epd, hid_n, out_n, dim, doms, exps, rows_n):
    m_sec, m_first, m_tow = layout(epd, hid_n, out_n, dim, doms, rows_n)
    ke = doms * exps

    def body(ins, outs, buf, tgf):
        out_f, out_s, out_t, out_g, out_h = (o.buf for o in outs)
        c = lax.rem(lax.axis_index(WIDTH), 2)
        r = lax.axis_index(ROWS)
        at_row = [spots(kind, r, rows_n) for kind in range(2)]
        for kind, size in ((0, m_sec), (1, m_first)):
            got = ins[kind].get()
            step = math.gcd(size, hid_n)
            for i, q, flat in pieces(kind, epd, hid_n, out_n, dim):
                for off in range(0, hid_n, step):
                    j, o = divmod(flat + off, size)
                    piece = got[at_row[kind][j], o : o + step, :].astype(F32)
                    if kind == 0:
                        out_s[i, off : off + step, q * LANE : (q + 1) * LANE] = piece
                    else:
                        buf[off : off + step, :] = piece
                if kind == 1:
                    out_f[i, q * LANE : (q + 1) * LANE, :] = buf[...].T
                if q == (out_n, dim)[kind] // LANE - 1:
                    outs[1 - kind].flush(i)
        near, sib = ins[1].get(), ins[2].get()
        for j in range(rows_n):
            at = at_row[1][j]
            for core, value in ((c, near[at, m_first:, :]), (1 - c, sib[at])):
                start = pl.multiple_of((core * rows_n + j) * m_tow, 8)
                tgf[pl.ds(start, m_tow), :] = value.astype(F32)
        for k in range(doms):
            out_t[k] = tgf[k * out_n : (k + 1) * out_n, :]
        outs[2].flush()
        for q in range(dim // LANE):
            at = doms * out_n + q * 32
            out_g[:, q * LANE : (q + 1) * LANE] = tgf[at : at + ke, :]
        outs[3].flush()
        out_h[...] = tgf[doms * out_n + ke : doms * out_n + ke + doms, :]
        outs[4].flush()

    return staged(
        body,
        [Near(second), Near(first), Near(other)],
        [
            plain((epd, dim, hid_n), F32),
            plain((epd, hid_n, out_n), F32),
            plain((doms, out_n, LANE), F32),
            plain((ke, dim), F32),
            plain((doms, LANE), F32),
        ],
        [pltpu.VMEM((hid_n, LANE), F32), pltpu.VMEM((2 * rows_n * m_tow, LANE), F32)],
        "finish_weights",
        16,
    )


def swap(value, axis, mask):
    size = lax.axis_size(axis)
    return lax.ppermute(value, axis, [(i, i ^ mask) for i in range(size)])


def total(*values):
    got = values[0].astype(F32)
    for value in values[1:]:
        got = got + value.astype(F32)
    return got


def send(value, axis, mask):
    return swap(value.astype(BF16), axis, mask)


together = lax.optimization_barrier


def reduce_rows(second, first, towers, beside):
    n_rows, n_width = lax.axis_size(ROWS), lax.axis_size(WIDTH)
    half = n_rows // 2
    far = [2 * q for q in range(1, half)]
    low = total(*(v[half:] for v in first)).astype(BF16)
    high = [total(*(v[m : m + 2] for v in second)).astype(BF16) for m in far]
    across = total(*towers).astype(BF16)
    first_got = swap(low, ROWS, 1)
    second_got = [swap(v, ROWS, m) for v, m in zip(high, far)]
    towers = total(*towers, *(swap(across, WIDTH, mask) for mask in range(2, n_width, 2)))
    tower_low, operand = together((towers[half:].astype(BF16), beside[1]))
    tower_got = swap(tower_low, ROWS, 1)
    inputs_part = tuple(beside[0](operand))
    first_got, second_got, tower_got, inputs_part = together((first_got, second_got, tower_got, inputs_part))

    def piece(q):
        return jnp.concatenate(
            [total(*(v[q] for v in first), first_got[q]), total(towers[q], tower_got[q])], axis=0
        )

    pair = total(*(v[:2] for v in second), *second_got)
    high = [piece(q).astype(BF16) for q in range(1, half)]
    high, low = together((high, pair.astype(BF16)))
    moved = [swap(v, ROWS, m) for v, m in zip(high, far)]
    moved, low = together((moved, swap(low, ROWS, 1)))
    pair = total(pair, low[::-1])
    return pair.astype(BF16), total(piece(0), *moved).astype(BF16), inputs_part


def gather_rows(pair, first, m_first, beside):
    half = lax.axis_size(ROWS) // 2
    far = [2 * q for q in range(1, half)]
    pair, first = together((pair, first))
    high, beside = together(([swap(first, ROWS, m) for m in far], beside))
    pair, evens = together((pair, jnp.stack([first] + high)))
    low, high = swap(evens, ROWS, 1), [swap(pair, ROWS, m) for m in far]
    low, high, beside = together((low, high, finish_inputs(*beside)))
    second, first = jnp.concatenate([pair] + high), jnp.concatenate([evens, low])
    return second, first, swap(first[:, m_first:], WIDTH, 1), beside


def local(inputs, w_first, w_second, w_gate, w_tower, norm_scale, norm_shift, w_head, domains, labels):
    n_width, n_rows = lax.axis_size(WIDTH), lax.axis_size(ROWS)
    devices = n_width * n_rows
    own = inputs.shape[0] // n_width
    count = float(own * devices)
    dim = inputs.shape[1]
    epd, _, hid_n = w_first.shape
    out_n = w_second.shape[2]
    doms, _, exps = w_gate.shape
    ke = doms * exps
    n_x = n_width // 2
    others = list(range(1, n_x))
    w1 = (w_first, swap(w_first, WIDTH, 1))
    w2 = (w_second, swap(w_second, WIDTH, 1))
    wgate_t = jnp.transpose(w_gate, (0, 2, 1)).reshape(ke, dim)
    marks = jnp.stack([domains, labels])

    x_far, w1_own, w2_own, wt = prepare(others, inputs, w_first, w_second, wgate_t, w_tower, own)
    w1t, w2t = (w1_own, w1[1]), (w2_own, w2[1])
    far = forward([Near(x_far)], w1t, w2t, wt, own, doms, False, BF16, "forward_send")[0]
    sent = [swap(far[s - 1 : s], WIDTH, 2 * s) for s in others]
    blocks = [Far(inputs, (own, dim), row_blocks([0], own)), Near(x_far)]
    kept = forward(blocks, w1t, w2t, wt, own, doms, True, F32, "forward_keep")
    tower, low, message = combine(kept[5], sent, marks, devices)
    stats = lax.all_to_all(message, BOTH, 0, 0, tiled=True)
    stats, low = together((stats, low))
    lows = [swap(low, WIDTH, 2 * s) for s in others]
    params, message = normalise(stats, tower, marks, norm_scale, norm_shift, w_head, devices, count)
    sums = lax.all_to_all(message, BOTH, 0, 0, tiled=True)

    acts = [(kept[:5], s) for s in range(n_x)]
    grad_shift, grad_scale, loss, sec_sib, first_sib, sec_own, first_own, tow_sib, tow_own, pg, lg = backward(
        sums, params, tower, lows, marks, acts, inputs, w2, wgate_t, w_tower, devices, n_rows, count
    )
    first_sib = swap(first_sib, WIDTH, 1)
    first_sib, sec_sib, tow_sib = together((first_sib, sec_sib, tow_sib))
    second, first, (gi_own, gi_out) = reduce_rows(
        (sec_own, swap(sec_sib, WIDTH, 1)),
        (first_own, first_sib),
        (tow_own, swap(tow_sib, WIDTH, 1)),
        (lambda grad: backward_inputs(grad, lg, w1, wgate_t, own), pg),
    )
    inputs_got = [swap(gi_out[s - 1], WIDTH, 2 * s) for s in others]
    m_first = layout(epd, hid_n, out_n, dim, doms, n_rows)[1]
    second, first, other, grad_inputs = gather_rows(second, first, m_first, (gi_own, inputs_got))
    grad_first, grad_second, grad_tower, grad_gate, grad_head = finish_weights(
        second, first, other, epd, hid_n, out_n, dim, doms, exps, n_rows
    )
    return (
        loss[0, 0],
        grad_inputs,
        grad_first,
        grad_second,
        grad_gate.reshape(doms, exps, dim).transpose(0, 2, 1),
        grad_tower,
        grad_scale,
        grad_shift,
        grad_head,
    )


def solution(mesh):
    placed = (
        P(ROWS, None),
        P(WIDTH, None, None),
        P(WIDTH, None, None),
        P(),
        P(),
        P(),
        P(),
        P(),
        P(BOTH),
        P(BOTH),
    )
    return jax.shard_map(
        local,
        mesh=mesh,
        in_specs=placed,
        out_specs=(
            P(),
            P(BOTH, None),
            P(WIDTH, None, None),
            P(WIDTH, None, None),
            P(),
            P(),
            P(),
            P(),
            P(),
        ),
        check_vma=False,
    )
```

profile of v0, /device:TPU:0, one launch (start us, length us, event | category | flops | bytes accessed | tf_op | source)
XLA Modules:
  0.0 100.1 jit_solution(18205864839894268899)
XLA Ops:
  0.6 0.5 collective-permute-start
  1.2 0.1 collective-permute-start.1
  1.2 2.2 %prepare.1 = (bf16[512,512]{1,0:T(8,128)(2,1)S(1)}, bf16[536,512]{1,0:T(8,128)(2,1)S(1)}, bf16[2,256,256]{2,1,0:T(8,128)(2,1)S(1)}, bf16[3,128,256]{2,1,0:T(8,128)(2,1)S(1)}) custom-call(bf16[2,512,256]{2,1,0:T(8,128)(2,1)} %refs_0_.5, bf16[24,512]{1,0:T(8,128)(2,1)} %bitcast.40, bf16[2,256,256]{2,1,0:T(8,128)(2,1)} %refs_10_.1, ...), custom_call_target="tpu_custom_call" | custom-call | tf_op jit(solution)/shard_map/prepare/pallas_call | solution.py:123
  3.5 2.5 %forward_send.1 = bf16[1,384,512]{2,1,0:T(8,128)(2,1)S(1)} custom-call(bf16[512,512]{1,0:T(8,128)(2,1)S(1)} %get-tuple-element.78.refs_1_.refs_0_, bf16[536,512]{1,0:T(8,128)(2,1)S(1)} %get-tuple-element.79.refs_2_.refs_1_, bf16[2,512,256]{2,1,0:T(8,128)(2,1)S(1)} %collective-permute-done.refs_3_.refs_2_.refs_1_, ...), custom_call_target="tpu_custom_call" | custom-call | tf_op jit(solution)/shard_map/forward_send/pallas_call | solution.py:123
  6.0 3.0 %collective-permute-start.2 = (bf16[1,384,512]{2,1,0:T(8,128)(2,1)S(1)}, bf16[1,384,512]{2,1,0:T(8,128)(2,1)S(1)}, u32[]{:S(2)}, u32[]{:S(2)}) collective-permute-start(bf16[1,384,512]{2,1,0:T(8,128)(2,1)S(1)} %forward_send.1), channel_id=1, source_target_pairs={{0,2},{1,3},{2,0},{3,1},{4,6},{5,7},{6,4},{7,5},{8,10},{9,11},{10,... | collective-permute-start | bytes 1179656 | tf_op jit(solution)/shard_map/ppermute | solution.py:742
  8.9 0.6 pad_add_fusion.refs_1_.refs_2_.refs_3_
  9.5 8.2 %forward_keep.1 = (bf16[2,1024,512]{2,1,0:T(8,128)(2,1)}, bf16[2,1024,512]{2,1,0:T(8,128)(2,1)}, bf16[2,1024,512]{2,1,0:T(8,128)(2,1)}, f32[2,24,512]{2,1,0:T(8,...) custom-call(bf16[2048,512]{1,0:T(8,128)(2,1)} %refs_14_.1, ...), custom_call_target="tpu_custom_call" | custom-call | tf_op jit(solution)/shard_map/forward_keep/pallas_call | solution.py:123
  17.7 0.5 collective-permute-done.2.refs_2_
  18.3 1.5 %combine.1 = (f32[384,512]{1,0:T(8,128)S(1)}, bf16[400,512]{1,0:T(8,128)(2,1)S(1)}, f32[256,128]{1,0:T(8,128)S(1)}) custom-call(f32[1,384,512]{2,1,0:T(8,128)S(1)} %get-tuple-element.82.refs_0_, s32[2,512]{1,0:T(2,128)} %pad_add_fusion.refs_1_.refs_2_.refs_3_, bf16[1,384,512]{2,1,0:T(8,128)(2,1)S(1)} %collective-permute-done.2.refs_2_), custom_call_target="tpu_custom_call" | custom-call | tf_op jit(solution)/shard_map/combine/pallas_call | solution.py:123
  19.8 14.1 %all_to_all.23 = f32[32,8,128]{2,1,0:T(8,128)S(1)} all-to-all(f32[32,8,128]{2,1,0:T(8,128)S(1)} %bitcast.36), channel_id=1, replica_groups=mesh['rows'=8,'width'=4] {'rows','width'}, dimensions={0} | all-to-all | bytes 262144 | tf_op jit(solution)/shard_map/all_to_all | solution.py:824
  33.9 0.4 collective-permute-start.3
  34.4 2.4 %normalise.1 = (f32[24,128]{1,0:T(8,128)S(1)}, bf16[256,128]{1,0:T(8,128)(2,1)S(1)}) custom-call(f32[256,128]{1,0:T(8,128)S(1)} %bitcast.34, f32[384,512]{1,0:T(8,128)S(1)} %get-tuple-element.86.refs_1_.refs_2_, s32[2,512]{1,0:T(2,128)} %pad_add_fusion.refs_1_.refs_2_.refs_3_, f32[3,128]{1,0:T(4,128)} %refs_3_.3, f32[3,128]{1,0:T(4,128)} %refs_4_.3, ...), custom_call_target="tpu_custom_call" | custom-call | tf_op jit(solution)/shard_map/normalise/pallas_call | solution.py:123
  36.8 10.0 %all_to_all.24 = bf16[32,8,128]{2,1,0:T(8,128)(2,1)S(1)} all-to-all(bf16[32,8,128]{2,1,0:T(8,128)(2,1)S(1)} %bitcast.37), channel_id=1, replica_groups=mesh['rows'=8,'width'=4] {'rows','width'}, dimensions={0} | all-to-all | bytes 131072 | tf_op jit(solution)/shard_map/all_to_all | solution.py:828
  46.8 9.1 %backward.1 = (f32[3,128]{1,0:T(4,128)}, f32[3,128]{1,0:T(4,128)}, f32[1,1]{1,0:T(1,128)}, bf16[8,128,128]{2,1,0:T(8,128)(2,1)S(1)}, bf16[8,256,128]{2,1,0:T(8,1...) custom-call(bf16[256,128]{1,0:T(8,128)(2,1)S(1)} %bitcast.35, ...), custom_call_target="tpu_custom_call" | custom-call | tf_op jit(solution)/shard_map/backward/pallas_call | solution.py:123
  55.9 0.2 collective-permute-start.4
  56.1 1.8 %collective-permute-done.4 = bf16[8,256,128]{2,1,0:T(8,128)(2,1)S(1)} collective-permute-done((bf16[8,256,128]{2,1,0:T(8,128)(2,1)S(1)}, bf16[8,256,128]{2,1,0:T(8,128)(2,1)S(1)}, u32[]{:S(2)}, u32[]{:S(2)}) %collective-permute-start.4) | collective-permute-done | bytes 524320 | tf_op jit(solution)/shard_map/ppermute | solution.py:742
  57.9 0.1 collective-permute-start.10
  58.0 0.4 collective-permute-start.5
  58.4 0.1 add_convert_fusion
  58.5 0.9 collective-permute-start.6
  59.4 0.5 collective-permute-start.11
  60.0 1.2 %collective-permute-start.9 = (bf16[2,128,128]{2,1,0:T(8,128)(2,1)S(1)}, bf16[2,128,128]{2,1,0:T(8,128)(2,1)S(1)}, u32[]{:S(2)}, u32[]{:S(2)}) collective-permute-start(bf16[2,128,128]{2,1,0:T(8,128)(2,1)S(1)} %get-tuple-element.151), channel_id=1, source_target_pairs={{0,24},{4,28},{8,16},{12,20},{16,8},{20,12},{24,0},{28,4},{1,25},{... | collective-permute-start | bytes 196616 | tf_op jit(solution)/shard_map/ppermute | solution.py:742
  61.2 0.9 collective-permute-start.8
  62.2 2.3 %collective-permute-start.7 = (bf16[2,128,128]{2,1,0:T(8,128)(2,1)S(1)}, bf16[2,128,128]{2,1,0:T(8,128)(2,1)S(1)}, u32[]{:S(2)}, u32[]{:S(2)}) collective-permute-start(bf16[2,128,128]{2,1,0:T(8,128)(2,1)S(1)} %get-tuple-element.153), channel_id=1, source_target_pairs={{0,8},{4,12},{8,0},{12,4},{16,24},{20,28},{24,16},{28,20},{1,9},{5... | collective-permute-start | bytes 196616 | tf_op jit(solution)/shard_map/ppermute | solution.py:742
  64.5 0.4 collective-permute-done.11
  65.0 1.1 %collective-permute-start.12 = (bf16[4,64,128]{2,1,0:T(8,128)(2,1)S(1)}, bf16[4,64,128]{2,1,0:T(8,128)(2,1)S(1)}, u32[]{:S(2)}, u32[]{:S(2)}) collective-permute-start(bf16[4,64,128]{2,1,0:T(8,128)(2,1)S(1)} %slice.192), channel_id=1, source_target_pairs={{0,4},{4,0},{8,12},{12,8},{16,20},{20,16},{24,28},{28,24},{1,5},{5... | collective-permute-start | bytes 196616 | tf_op jit(solution)/shard_map/ppermute | solution.py:742
  66.1 3.1 %backward_inputs.1 = (f32[512,512]{1,0:T(8,128)S(1)}, bf16[1,512,512]{2,1,0:T(8,128)(2,1)S(1)}) custom-call(bf16[2,512,256]{2,1,0:T(8,128)(2,1)} %refs_0_.5, bf16[2,512,256]{2,1,0:T(8,128)(2,1)S(1)} %collective-permute-done.refs_3_.refs_2_.refs_1_, bf16[24,512]{1,0:T(8,128)(2,1)} %bitcast.41, bf16[1024,1024]{1,0:T(8,128)(2,1)S(1)} %get-tuple-element.107.refs_3_, ...), custom_call_target="tpu_custom_call" | custom-call | tf_op jit(solution)/shard_map/backward_inputs/pallas_call | solution.py:123
  69.3 0.1 add_bitcast_fusion
  69.5 0.7 collective-permute-start.13
  70.2 0.9 collective-permute-start.14
  71.1 2.9 %collective-permute-start.15 = (bf16[320,128]{1,0:T(8,128)(2,1)S(1)}, bf16[320,128]{1,0:T(8,128)(2,1)S(1)}, u32[]{:S(2)}, u32[]{:S(2)}) collective-permute-start(bf16[320,128]{1,0:T(8,128)(2,1)S(1)} %pad_maximum_fusion.4), channel_id=1, source_target_pairs={{0,24},{4,28},{8,16},{12,20},{16,8},{20,12},{24,0},{28,4},{1,25},{... | collective-permute-start | bytes 245768 | tf_op jit(solution)/shard_map/ppermute | solution.py:742
  74.0 1.0 %collective-permute-start.16 = (bf16[2,128,128]{2,1,0:T(8,128)(2,1)S(1)}, bf16[2,128,128]{2,1,0:T(8,128)(2,1)S(1)}, u32[]{:S(2)}, u32[]{:S(2)}) collective-permute-start(bf16[2,128,128]{2,1,0:T(8,128)(2,1)S(1)} %fusion.14), channel_id=1, source_target_pairs={{0,4},{4,0},{8,12},{12,8},{16,20},{20,16},{24,28},{28,24},{1,5},{5... | collective-permute-start | bytes 196616 | tf_op jit(solution)/shard_map/ppermute | solution.py:742
  75.0 1.3 %collective-permute-start.20 = (bf16[512,512]{1,0:T(8,128)(2,1)S(1)}, bf16[512,512]{1,0:T(8,128)(2,1)S(1)}, u32[]{:S(2)}, u32[]{:S(2)}) collective-permute-start(bf16[512,512]{1,0:T(8,128)(2,1)S(1)} %bitcast.38), channel_id=1, source_target_pairs={{0,2},{1,3},{2,0},{3,1},{4,6},{5,7},{6,4},{7,5},{8,10},{9,11},{10,... | collective-permute-start | bytes 1572872 | tf_op jit(solution)/shard_map/ppermute | solution.py:742
  76.3 1.9 %collective-permute-done.16 = bf16[2,128,128]{2,1,0:T(8,128)(2,1)S(1)} collective-permute-done((bf16[2,128,128]{2,1,0:T(8,128)(2,1)S(1)}, bf16[2,128,128]{2,1,0:T(8,128)(2,1)S(1)}, u32[]{:S(2)}, u32[]{:S(2)}) %collective-permute-start.16) | collective-permute-done | bytes 65568 | tf_op jit(solution)/shard_map/ppermute | solution.py:742
  78.3 0.2 collective-permute-done.14
  78.6 1.9 %collective-permute-start.19 = (bf16[320,128]{1,0:T(8,128)(2,1)S(1)}, bf16[320,128]{1,0:T(8,128)(2,1)S(1)}, u32[]{:S(2)}, u32[]{:S(2)}) collective-permute-start(bf16[320,128]{1,0:T(8,128)(2,1)S(1)} %fusion.3), channel_id=1, source_target_pairs={{0,24},{4,28},{8,16},{12,20},{16,8},{20,12},{24,0},{28,4},{1,25},{... | collective-permute-start | bytes 245768 | tf_op jit(solution)/shard_map/ppermute | solution.py:742
  80.5 1.1 %collective-permute-start.18 = (bf16[320,128]{1,0:T(8,128)(2,1)S(1)}, bf16[320,128]{1,0:T(8,128)(2,1)S(1)}, u32[]{:S(2)}, u32[]{:S(2)}) collective-permute-start(bf16[320,128]{1,0:T(8,128)(2,1)S(1)} %fusion.3), channel_id=1, source_target_pairs={{0,16},{4,20},{8,24},{12,28},{16,0},{20,4},{24,8},{28,12},{1,17},{... | collective-permute-start | bytes 245768 | tf_op jit(solution)/shard_map/ppermute | solution.py:742
  81.6 1.4 %collective-permute-start.17 = (bf16[320,128]{1,0:T(8,128)(2,1)S(1)}, bf16[320,128]{1,0:T(8,128)(2,1)S(1)}, u32[]{:S(2)}, u32[]{:S(2)}) collective-permute-start(bf16[320,128]{1,0:T(8,128)(2,1)S(1)} %fusion.3), channel_id=1, source_target_pairs={{0,8},{4,12},{8,0},{12,4},{16,24},{20,28},{24,16},{28,20},{1,9},{5... | collective-permute-start | bytes 245768 | tf_op jit(solution)/shard_map/ppermute | solution.py:742
  83.0 2.0 %collective-permute-done.19 = bf16[320,128]{1,0:T(8,128)(2,1)S(1)} collective-permute-done((bf16[320,128]{1,0:T(8,128)(2,1)S(1)}, bf16[320,128]{1,0:T(8,128)(2,1)S(1)}, u32[]{:S(2)}, u32[]{:S(2)}) %collective-permute-start.19) | collective-permute-done | bytes 81952 | tf_op jit(solution)/shard_map/ppermute | solution.py:742
  85.0 2.0 %collective-permute-done.18 = bf16[320,128]{1,0:T(8,128)(2,1)S(1)} collective-permute-done((bf16[320,128]{1,0:T(8,128)(2,1)S(1)}, bf16[320,128]{1,0:T(8,128)(2,1)S(1)}, u32[]{:S(2)}, u32[]{:S(2)}) %collective-permute-start.18) | collective-permute-done | bytes 81952 | tf_op jit(solution)/shard_map/ppermute | solution.py:742
  87.0 2.0 %collective-permute-start.21 = (bf16[4,320,128]{2,1,0:T(8,128)(2,1)S(1)}, bf16[4,320,128]{2,1,0:T(8,128)(2,1)S(1)}, u32[]{:S(2)}, u32[]{:S(2)}) collective-permute-start(bf16[4,320,128]{2,1,0:T(8,128)(2,1)S(1)} %pad_maximum_fusion), channel_id=1, source_target_pairs={{0,4},{4,0},{8,12},{12,8},{16,20},{20,16},{24,28},{28,24},{1,5},{5... | collective-permute-start | bytes 983048 | tf_op jit(solution)/shard_map/ppermute | solution.py:742
  89.0 1.0 %collective-permute-start.24 = (bf16[2,128,128]{2,1,0:T(8,128)(2,1)S(1)}, bf16[2,128,128]{2,1,0:T(8,128)(2,1)S(1)}, u32[]{:S(2)}, u32[]{:S(2)}) collective-permute-start(bf16[2,128,128]{2,1,0:T(8,128)(2,1)S(1)} %add_convert_fusion.1), channel_id=1, source_target_pairs={{0,24},{4,28},{8,16},{12,20},{16,8},{20,12},{24,0},{28,4},{1,25},{... | collective-permute-start | bytes 196616 | tf_op jit(solution)/shard_map/ppermute | solution.py:742
  90.0 0.1 collective-permute-start.23
  90.2 3.2 %collective-permute-start.22 = (bf16[2,128,128]{2,1,0:T(8,128)(2,1)S(1)}, bf16[2,128,128]{2,1,0:T(8,128)(2,1)S(1)}, u32[]{:S(2)}, u32[]{:S(2)}) collective-permute-start(bf16[2,128,128]{2,1,0:T(8,128)(2,1)S(1)} %add_convert_fusion.1), channel_id=1, source_target_pairs={{0,8},{4,12},{8,0},{12,4},{16,24},{20,28},{24,16},{28,20},{1,9},{5... | collective-permute-start | bytes 196616 | tf_op jit(solution)/shard_map/ppermute | solution.py:742
  93.4 1.7 %finish_inputs.1 = f32[512,512]{1,0:T(8,128)} custom-call(f32[512,512]{1,0:T(8,128)S(1)} %get-tuple-element.133.refs_0_, bf16[512,512]{1,0:T(8,128)(2,1)S(1)} %collective-permute-done.20.refs_1_), custom_call_target="tpu_custom_call" | custom-call | tf_op jit(solution)/shard_map/finish_inputs/pallas_call | solution.py:123
  95.1 1.3 %collective-permute-done.23 = bf16[2,128,128]{2,1,0:T(8,128)(2,1)S(1)} collective-permute-done((bf16[2,128,128]{2,1,0:T(8,128)(2,1)S(1)}, bf16[2,128,128]{2,1,0:T(8,128)(2,1)S(1)}, u32[]{:S(2)}, u32[]{:S(2)}) %collective-permute-start.23) | collective-permute-done | bytes 65568 | tf_op jit(solution)/shard_map/ppermute | solution.py:742
  96.7 1.3 %collective-permute-done.25.refs_2_ = bf16[8,64,128]{2,1,0:T(8,128)(2,1)S(1)} collective-permute-done((bf16[8,64,128]{2,1,0:T(8,128)(2,1)S(1)}, bf16[8,64,128]{2,1,0:T(8,128)(2,1)S(1)}, u32[]{:S(2)}, u32[]{:S(2)}) %collective-permute-start.25) | collective-permute-done | bytes 131104 | tf_op jit(solution)/shard_map/ppermute | solution.py:742
  98.0 2.0 %finish_weights.1 = (f32[2,512,256]{2,1,0:T(8,128)}, f32[2,256,256]{2,1,0:T(8,128)}, f32[3,256,128]{2,1,0:T(8,128)}, f32[24,512]{1,0:T(8,128)}, f32[3,128]{1,0:T(4,128)}) custom-call(bf16[8,128,128]{2,1,0:T(8,128)(2,1)S(1)} %pad_maximum_fusion.1.refs_0_, bf16[8,320,128]{2,1,0:T(8,128)(2,1)S(1)} %constant_dynamic-update-slice_fusion.refs_1_, ...), custom_call_target="tpu_custom_call" | custom-call | tf_op jit(solution)/shard_map/finish_weights/pallas_call | solution.py:123
  (37 shorter events, 0.7 us)
Async XLA Ops:
  0.6 2.8 %collective-permute-start = (bf16[2,512,256]{2,1,0:T(8,128)(2,1)}, bf16[2,512,256]{2,1,0:T(8,128)(2,1)S(1)}, u32[]{:S(2)}, u32[]{:S(2)}) collective-permute-start(bf16[2,512,256]{2,1,0:T(8,128)(2,1)} %refs_0_.5), channel_id=1, source_target_pairs={{0,1},{1,0},{2,3},{3,2},{4,5},{5,4},{6,7},{7,6},{8,9},{9,8},{10,11... | collective-permute-start | bytes 1572872 | tf_op jit(solution)/shard_map/ppermute | solution.py:742
  1.2 2.3 %collective-permute-start.1 = (bf16[2,256,256]{2,1,0:T(8,128)(2,1)}, bf16[2,256,256]{2,1,0:T(8,128)(2,1)S(1)}, u32[]{:S(2)}, u32[]{:S(2)}) collective-permute-start(bf16[2,256,256]{2,1,0:T(8,128)(2,1)} %refs_10_.1), channel_id=1, source_target_pairs={{0,1},{1,0},{2,3},{3,2},{4,5},{5,4},{6,7},{7,6},{8,9},{9,8},{10,11... | collective-permute-start | bytes 786440 | tf_op jit(solution)/shard_map/ppermute | solution.py:742
  3.4 5.5 %copy-start = (s32[512]{0:T(512)S(1)}, s32[512]{0:T(512)}, u32[]{:S(2)}) copy-start(s32[512]{0:T(512)} %param.19) | copy-start | bytes 6148
  3.4 5.5 %copy-start.1 = (s32[512]{0:T(512)S(1)}, s32[512]{0:T(512)}, u32[]{:S(2)}) copy-start(s32[512]{0:T(512)} %param.18) | copy-start | bytes 6148
  6.0 12.3 %collective-permute-start.2 = (bf16[1,384,512]{2,1,0:T(8,128)(2,1)S(1)}, bf16[1,384,512]{2,1,0:T(8,128)(2,1)S(1)}, u32[]{:S(2)}, u32[]{:S(2)}) collective-permute-start(bf16[1,384,512]{2,1,0:T(8,128)(2,1)S(1)} %forward_send.1), channel_id=1, source_target_pairs={{0,2},{1,3},{2,0},{3,1},{4,6},{5,7},{6,4},{7,5},{8,10},{9,11},{10,... | collective-permute-start | bytes 1179656 | tf_op jit(solution)/shard_map/ppermute | solution.py:742
  33.9 12.9 %collective-permute-start.3 = (bf16[400,512]{1,0:T(8,128)(2,1)S(1)}, bf16[400,512]{1,0:T(8,128)(2,1)S(1)}, u32[]{:S(2)}, u32[]{:S(2)}) collective-permute-start(bf16[400,512]{1,0:T(8,128)(2,1)S(1)} %get-tuple-element.89), channel_id=1, source_target_pairs={{0,2},{1,3},{2,0},{3,1},{4,6},{5,7},{6,4},{7,5},{8,10},{9,11},{10,... | collective-permute-start | bytes 1228808 | tf_op jit(solution)/shard_map/ppermute | solution.py:742
  55.9 2.0 %collective-permute-start.4 = (bf16[8,256,128]{2,1,0:T(8,128)(2,1)S(1)}, bf16[8,256,128]{2,1,0:T(8,128)(2,1)S(1)}, u32[]{:S(2)}, u32[]{:S(2)}) collective-permute-start(bf16[8,256,128]{2,1,0:T(8,128)(2,1)S(1)} %get-tuple-element.97), channel_id=1, source_target_pairs={{0,1},{1,0},{2,3},{3,2},{4,5},{5,4},{6,7},{7,6},{8,9},{9,8},{10,11... | collective-permute-start | bytes 1572872 | tf_op jit(solution)/shard_map/ppermute | solution.py:742
  57.9 1.5 %collective-permute-start.10 = (bf16[8,64,128]{2,1,0:T(8,128)(2,1)S(1)}, bf16[8,64,128]{2,1,0:T(8,128)(2,1)S(1)}, u32[]{:S(2)}, u32[]{:S(2)}) collective-permute-start(bf16[8,64,128]{2,1,0:T(8,128)(2,1)S(1)} %get-tuple-element.104), channel_id=1, source_target_pairs={{0,1},{1,0},{2,3},{3,2},{4,5},{5,4},{6,7},{7,6},{8,9},{9,8},{10,11... | collective-permute-start | bytes 393224 | tf_op jit(solution)/shard_map/ppermute | solution.py:742
  58.0 1.9 %collective-permute-start.5 = (bf16[8,128,128]{2,1,0:T(8,128)(2,1)S(1)}, bf16[8,128,128]{2,1,0:T(8,128)(2,1)S(1)}, u32[]{:S(2)}, u32[]{:S(2)}) collective-permute-start(bf16[8,128,128]{2,1,0:T(8,128)(2,1)S(1)} %get-tuple-element.100), channel_id=1, source_target_pairs={{0,1},{1,0},{2,3},{3,2},{4,5},{5,4},{6,7},{7,6},{8,9},{9,8},{10,11... | collective-permute-start | bytes 786440 | tf_op jit(solution)/shard_map/ppermute | solution.py:742
  58.5 10.8 %collective-permute-start.6 = (bf16[4,256,128]{2,1,0:T(8,128)(2,1)S(1)}, bf16[4,256,128]{2,1,0:T(8,128)(2,1)S(1)}, u32[]{:S(2)}, u32[]{:S(2)}) collective-permute-start(bf16[4,256,128]{2,1,0:T(8,128)(2,1)S(1)} %add_convert_fusion), channel_id=1, source_target_pairs={{0,4},{4,0},{8,12},{12,8},{16,20},{20,16},{24,28},{28,24},{1,5},{5... | collective-permute-start | bytes 786440 | tf_op jit(solution)/shard_map/ppermute | solution.py:742
  59.4 5.5 %collective-permute-start.11 = (bf16[8,64,128]{2,1,0:T(8,128)(2,1)S(1)}, bf16[8,64,128]{2,1,0:T(8,128)(2,1)S(1)}, u32[]{:S(2)}, u32[]{:S(2)}) collective-permute-start(bf16[8,64,128]{2,1,0:T(8,128)(2,1)S(1)} %fusion), channel_id=1, source_target_pairs={{0,2},{1,3},{2,0},{3,1},{4,6},{5,7},{6,4},{7,5},{8,10},{9,11},{10,... | collective-permute-start | bytes 393224 | tf_op jit(solution)/shard_map/ppermute | solution.py:742
  60.0 9.2 %collective-permute-start.9 = (bf16[2,128,128]{2,1,0:T(8,128)(2,1)S(1)}, bf16[2,128,128]{2,1,0:T(8,128)(2,1)S(1)}, u32[]{:S(2)}, u32[]{:S(2)}) collective-permute-start(bf16[2,128,128]{2,1,0:T(8,128)(2,1)S(1)} %get-tuple-element.151), channel_id=1, source_target_pairs={{0,24},{4,28},{8,16},{12,20},{16,8},{20,12},{24,0},{28,4},{1,25},{... | collective-permute-start | bytes 196616 | tf_op jit(solution)/shard_map/ppermute | solution.py:742
  61.2 8.0 %collective-permute-start.8 = (bf16[2,128,128]{2,1,0:T(8,128)(2,1)S(1)}, bf16[2,128,128]{2,1,0:T(8,128)(2,1)S(1)}, u32[]{:S(2)}, u32[]{:S(2)}) collective-permute-start(bf16[2,128,128]{2,1,0:T(8,128)(2,1)S(1)} %get-tuple-element.152), channel_id=1, source_target_pairs={{0,16},{4,20},{8,24},{12,28},{16,0},{20,4},{24,8},{28,12},{1,17},{... | collective-permute-start | bytes 196616 | tf_op jit(solution)/shard_map/ppermute | solution.py:742
  62.2 7.1 %collective-permute-start.7 = (bf16[2,128,128]{2,1,0:T(8,128)(2,1)S(1)}, bf16[2,128,128]{2,1,0:T(8,128)(2,1)S(1)}, u32[]{:S(2)}, u32[]{:S(2)}) collective-permute-start(bf16[2,128,128]{2,1,0:T(8,128)(2,1)S(1)} %get-tuple-element.153), channel_id=1, source_target_pairs={{0,8},{4,12},{8,0},{12,4},{16,24},{20,28},{24,16},{28,20},{1,9},{5... | collective-permute-start | bytes 196616 | tf_op jit(solution)/shard_map/ppermute | solution.py:742
  65.0 4.3 %collective-permute-start.12 = (bf16[4,64,128]{2,1,0:T(8,128)(2,1)S(1)}, bf16[4,64,128]{2,1,0:T(8,128)(2,1)S(1)}, u32[]{:S(2)}, u32[]{:S(2)}) collective-permute-start(bf16[4,64,128]{2,1,0:T(8,128)(2,1)S(1)} %slice.192), channel_id=1, source_target_pairs={{0,4},{4,0},{8,12},{12,8},{16,20},{20,16},{24,28},{28,24},{1,5},{5... | collective-permute-start | bytes 196616 | tf_op jit(solution)/shard_map/ppermute | solution.py:742
  69.5 8.7 %collective-permute-start.13 = (bf16[320,128]{1,0:T(8,128)(2,1)S(1)}, bf16[320,128]{1,0:T(8,128)(2,1)S(1)}, u32[]{:S(2)}, u32[]{:S(2)}) collective-permute-start(bf16[320,128]{1,0:T(8,128)(2,1)S(1)} %get-tuple-element.116), channel_id=1, source_target_pairs={{0,8},{4,12},{8,0},{12,4},{16,24},{20,28},{24,16},{28,20},{1,9},{5... | collective-permute-start | bytes 245768 | tf_op jit(solution)/shard_map/ppermute | solution.py:742
  70.2 8.3 %collective-permute-start.14 = (bf16[320,128]{1,0:T(8,128)(2,1)S(1)}, bf16[320,128]{1,0:T(8,128)(2,1)S(1)}, u32[]{:S(2)}, u32[]{:S(2)}) collective-permute-start(bf16[320,128]{1,0:T(8,128)(2,1)S(1)} %get-tuple-element.117), channel_id=1, source_target_pairs={{0,16},{4,20},{8,24},{12,28},{16,0},{20,4},{24,8},{28,12},{1,17},{... | collective-permute-start | bytes 245768 | tf_op jit(solution)/shard_map/ppermute | solution.py:742
  71.1 7.4 %collective-permute-start.15 = (bf16[320,128]{1,0:T(8,128)(2,1)S(1)}, bf16[320,128]{1,0:T(8,128)(2,1)S(1)}, u32[]{:S(2)}, u32[]{:S(2)}) collective-permute-start(bf16[320,128]{1,0:T(8,128)(2,1)S(1)} %pad_maximum_fusion.4), channel_id=1, source_target_pairs={{0,24},{4,28},{8,16},{12,20},{16,8},{20,12},{24,0},{28,4},{1,25},{... | collective-permute-start | bytes 245768 | tf_op jit(solution)/shard_map/ppermute | solution.py:742
  74.0 4.3 %collective-permute-start.16 = (bf16[2,128,128]{2,1,0:T(8,128)(2,1)S(1)}, bf16[2,128,128]{2,1,0:T(8,128)(2,1)S(1)}, u32[]{:S(2)}, u32[]{:S(2)}) collective-permute-start(bf16[2,128,128]{2,1,0:T(8,128)(2,1)S(1)} %fusion.14), channel_id=1, source_target_pairs={{0,4},{4,0},{8,12},{12,8},{16,20},{20,16},{24,28},{28,24},{1,5},{5... | collective-permute-start | bytes 196616 | tf_op jit(solution)/shard_map/ppermute | solution.py:742
  75.0 11.9 %collective-permute-start.20 = (bf16[512,512]{1,0:T(8,128)(2,1)S(1)}, bf16[512,512]{1,0:T(8,128)(2,1)S(1)}, u32[]{:S(2)}, u32[]{:S(2)}) collective-permute-start(bf16[512,512]{1,0:T(8,128)(2,1)S(1)} %bitcast.38), channel_id=1, source_target_pairs={{0,2},{1,3},{2,0},{3,1},{4,6},{5,7},{6,4},{7,5},{8,10},{9,11},{10,... | collective-permute-start | bytes 1572872 | tf_op jit(solution)/shard_map/ppermute | solution.py:742
  78.6 6.4 %collective-permute-start.19 = (bf16[320,128]{1,0:T(8,128)(2,1)S(1)}, bf16[320,128]{1,0:T(8,128)(2,1)S(1)}, u32[]{:S(2)}, u32[]{:S(2)}) collective-permute-start(bf16[320,128]{1,0:T(8,128)(2,1)S(1)} %fusion.3), channel_id=1, source_target_pairs={{0,24},{4,28},{8,16},{12,20},{16,8},{20,12},{24,0},{28,4},{1,25},{... | collective-permute-start | bytes 245768 | tf_op jit(solution)/shard_map/ppermute | solution.py:742
  80.5 6.4 %collective-permute-start.18 = (bf16[320,128]{1,0:T(8,128)(2,1)S(1)}, bf16[320,128]{1,0:T(8,128)(2,1)S(1)}, u32[]{:S(2)}, u32[]{:S(2)}) collective-permute-start(bf16[320,128]{1,0:T(8,128)(2,1)S(1)} %fusion.3), channel_id=1, source_target_pairs={{0,16},{4,20},{8,24},{12,28},{16,0},{20,4},{24,8},{28,12},{1,17},{... | collective-permute-start | bytes 245768 | tf_op jit(solution)/shard_map/ppermute | solution.py:742
  81.6 5.3 %collective-permute-start.17 = (bf16[320,128]{1,0:T(8,128)(2,1)S(1)}, bf16[320,128]{1,0:T(8,128)(2,1)S(1)}, u32[]{:S(2)}, u32[]{:S(2)}) collective-permute-start(bf16[320,128]{1,0:T(8,128)(2,1)S(1)} %fusion.3), channel_id=1, source_target_pairs={{0,8},{4,12},{8,0},{12,4},{16,24},{20,28},{24,16},{28,20},{1,9},{5... | collective-permute-start | bytes 245768 | tf_op jit(solution)/shard_map/ppermute | solution.py:742
  87.0 9.5 %collective-permute-start.21 = (bf16[4,320,128]{2,1,0:T(8,128)(2,1)S(1)}, bf16[4,320,128]{2,1,0:T(8,128)(2,1)S(1)}, u32[]{:S(2)}, u32[]{:S(2)}) collective-permute-start(bf16[4,320,128]{2,1,0:T(8,128)(2,1)S(1)} %pad_maximum_fusion), channel_id=1, source_target_pairs={{0,4},{4,0},{8,12},{12,8},{16,20},{20,16},{24,28},{28,24},{1,5},{5... | collective-permute-start | bytes 983048 | tf_op jit(solution)/shard_map/ppermute | solution.py:742
  89.0 6.1 %collective-permute-start.24 = (bf16[2,128,128]{2,1,0:T(8,128)(2,1)S(1)}, bf16[2,128,128]{2,1,0:T(8,128)(2,1)S(1)}, u32[]{:S(2)}, u32[]{:S(2)}) collective-permute-start(bf16[2,128,128]{2,1,0:T(8,128)(2,1)S(1)} %add_convert_fusion.1), channel_id=1, source_target_pairs={{0,24},{4,28},{8,16},{12,20},{16,8},{20,12},{24,0},{28,4},{1,25},{... | collective-permute-start | bytes 196616 | tf_op jit(solution)/shard_map/ppermute | solution.py:742
  90.0 6.4 %collective-permute-start.23 = (bf16[2,128,128]{2,1,0:T(8,128)(2,1)S(1)}, bf16[2,128,128]{2,1,0:T(8,128)(2,1)S(1)}, u32[]{:S(2)}, u32[]{:S(2)}) collective-permute-start(bf16[2,128,128]{2,1,0:T(8,128)(2,1)S(1)} %add_convert_fusion.1), channel_id=1, source_target_pairs={{0,16},{4,20},{8,24},{12,28},{16,0},{20,4},{24,8},{28,12},{1,17},{... | collective-permute-start | bytes 196616 | tf_op jit(solution)/shard_map/ppermute | solution.py:742
  90.2 6.3 %collective-permute-start.22 = (bf16[2,128,128]{2,1,0:T(8,128)(2,1)S(1)}, bf16[2,128,128]{2,1,0:T(8,128)(2,1)S(1)}, u32[]{:S(2)}, u32[]{:S(2)}) collective-permute-start(bf16[2,128,128]{2,1,0:T(8,128)(2,1)S(1)} %add_convert_fusion.1), channel_id=1, source_target_pairs={{0,8},{4,12},{8,0},{12,4},{16,24},{20,28},{24,16},{28,20},{1,9},{5... | collective-permute-start | bytes 196616 | tf_op jit(solution)/shard_map/ppermute | solution.py:742
  96.5 1.4 %collective-permute-start.25 = (bf16[8,64,128]{2,1,0:T(8,128)(2,1)S(1)}, bf16[8,64,128]{2,1,0:T(8,128)(2,1)S(1)}, u32[]{:S(2)}, u32[]{:S(2)}) collective-permute-start(bf16[8,64,128]{2,1,0:T(8,128)(2,1)S(1)} %slice.138), channel_id=1, source_target_pairs={{0,1},{1,0},{2,3},{3,2},{4,5},{5,4},{6,7},{7,6},{8,9},{9,8},{10,11... | collective-permute-start | bytes 393224 | tf_op jit(solution)/shard_map/ppermute | solution.py:742
where the time goes:
time: 100 us
  Pallas kernels  32.6 us (33%)
  starting transfers between devices  29.4 us (29%)
  blocking collectives  24.2 us (24%)
  waiting for transfers between devices  11.6 us (12%)
  other arithmetic  1.19 us (1%)
  between operations  1.06 us (1%)
    pallas_call x9, Pallas kernels, staged(): pl.pallas_call(kernel, out_shape=[o.what if isinstance(o, Near) else pltp...  32.6 us
    ppermute x26, starting transfers between devices, swap(): return lax.ppermute(value, axis, [(i, i ^ mask) for i in range(size)])  29.4 us
    all_to_all x1, blocking collectives, local(): stats = lax.all_to_all(message, BOTH, 0, 0, tiled=True)  14.1 us
    ppermute x26, waiting for transfers between devices, swap(): return lax.ppermute(value, axis, [(i, i ^ mask) for i in range(size)])  11.6 us
    all_to_all x1, blocking collectives, local(): sums = lax.all_to_all(message, BOTH, 0, 0, tiled=True)  10 us
  transfers between devices with their start and end apart: 26, of which 9 were waited for; matrix products, arithmetic and copies ran while one was open for 1% of the time, Pallas kernels for 18%

commit v1 on v0

--- a/solution.py
+++ b/solution.py
@@ -65,9 +65,9 @@
 
 class Far:
     def __init__(self, arrays, shape=None, pairs=None, moved=False, into=None):
-        self.moved = moved
         self.into = into
         self.arrays = arrays if isinstance(arrays, (list, tuple)) else [arrays]
+        self.moved = moved if isinstance(moved, list) else [moved] * len(self.arrays)
         self.shape = shape or self.arrays[0].shape
         self.dtype = self.arrays[0].dtype
         self.pairs = pairs or (lambda refs, buf: [(refs[0], buf)])
@@ -83,12 +83,9 @@
     for s in ins:
         if isinstance(s, Far):
             spans.append((len(args), len(args) + len(s.arrays)))
-            if s.moved:
-                args += s.arrays
-                specs += [anywhere] * len(s.arrays)
-                continue
-            args += [pltpu.with_memory_space_constraint(a, pltpu.HBM) for a in s.arrays]
-            specs += [hbm] * len(s.arrays)
+            for a, moved in zip(s.arrays, s.moved):
+                args.append(a if moved else pltpu.with_memory_space_constraint(a, pltpu.HBM))
+                specs.append(anywhere if moved else hbm)
         else:
             spans.append((len(args), len(args) + 1))
             args.append(s.what)
@@ -323,7 +320,7 @@
 
     return staged(
         body,
-        [Near(own_part), Far(marks)] + [Near(v) for v in received],
+        [Near(own_part), Near(marks)] + [Near(v) for v in received],
         [Near(plain((rows, own), F32)), Near(plain((rows + 16, own), BF16)), Near(plain((devices * 8, LANE), F32))],
         [pltpu.VMEM((LANE, LANE), F32)],
         "combine",
@@ -404,7 +401,7 @@
 
     return staged(
         body,
-        [Near(stats), Near(tower), Far(marks), Far(scale), Far(shift), Far(head)],
+        [Near(v) for v in (stats, tower, marks, scale, shift, head)],
         [Near(plain((24, LANE), F32)), Near(plain((devices * 8, LANE), BF16))],
         [
             pltpu.VMEM((LANE, LANE), F32),
@@ -439,7 +436,9 @@
     return got
 
 
-def backward(sums, params, tower, low_towers, marks, acts, inputs, w2, wgate_t, wtower, devices, rows_n, count):
+def backward(
+    sums, params, tower, low_towers, marks, acts, inputs, w1, w2, wgate_t, wtower, devices, rows_n, count
+):
     ns = 1 + len(low_towers)
     t_rows, own = tower.shape
     total_n = ns * own
@@ -454,8 +453,8 @@
     def body(ins, outs, wide, prm, tg, mg, eg, gg, srow, tgf, facc):
         sm, pr, tw0, mk0 = ins[:4]
         low = ins[4 : 3 + ns]
-        wts, gate, vals, w2o, w2s, slope, xs, hid, mixed = ins[3 + ns :]
-        shift_out, scale_out, loss_out, sec_sib, first_sib, sec_mine, first_mine, tow_sib, tow_mine, pgs, lgs = outs
+        wts, gate, vals, w2o, w2s, slope, xs, hid, mixed, _ = ins[3 + ns :]
+        shift_out, scale_out, loss_out, sec_sib, first_sib, sec_mine, first_mine, tow_sib, tow_mine, pgs, lgs, _ = outs
         pg, lg = pgs.buf, lgs.buf
         c = lax.rem(lax.axis_index(WIDTH), 2)
         r = lax.axis_index(ROWS)
@@ -603,6 +602,7 @@
         Near(plain((rows_n, m_tow, LANE), BF16)),
         Near(plain((ce * hid_n, total_n), BF16)),
         Near(plain((ke, total_n), BF16)),
+        Near(plain((dim, ce * hid_n), BF16)),
     ]
     scratch = [
         pltpu.VMEM((6 * doms, LANE, LANE), F32),
@@ -623,29 +623,29 @@
         arrays = [a[which] for a, _ in acts]
         return Far(arrays, (arrays[0].shape[1], total_n), pairs)
 
-    ins = [Near(sums), Near(params), Near(tower), Far(marks)]
-    ins += [Far(v, moved=True) for v in low_towers]
+    ins = [Near(sums), Near(params), Near(tower), Near(marks)]
+    ins += [Near(v) for v in low_towers]
     ins += [Far(wtower), side_by_side(3), side_by_side(2), Far(w2[0]), Far(w2[1], moved=True), side_by_side(1)]
     ins += [Far(inputs, (total_n, dim), row_blocks(list(range(ns)), own)), side_by_side(0), side_by_side(4)]
+
+    def joined(refs, buf):
+        slots = [(refs[e // epd].at[e % epd], e) for e in range(ce)]
+        return [(ref, buf.at[:, e * hid_n : (e + 1) * hid_n]) for ref, e in slots]
+
+    ins.append(Far(w1, pairs=joined, moved=[False, True], into=len(outs) - 1))
     return staged(body, ins, outs, scratch, "backward", 44)
 
 
 def backward_inputs(pg, lg, w1, wgate_t, own):
     total_n = pg.shape[1]
     ns = total_n // own
-    epd, dim, hid_n = w1[0].shape
-    ce = 2 * epd
+    dim = w1.shape[0]
     ke = wgate_t.shape[0]
 
-    def body(ins, outs, w1c):
-        w1o, w1s, wgs, pgs, lgs = ins
+    def body(ins, outs):
+        w1c, wgs, pgs, lgs = ins
         wg = jnp.concatenate([wgs.get()[...], jnp.zeros((LANE - ke, dim), BF16)], axis=0).T[:, :ke]
-        for g, src in enumerate((w1o, w1s)):
-            ref = src.get()
-            for i in range(epd):
-                e = g * epd + i
-                w1c[:, e * hid_n : (e + 1) * hid_n] = ref[i]
-        pg, lg = pgs.get(), lgs.get()
+        pg, lg, w1c = pgs.get(), lgs.get(), w1c.get()
         for n in range(ns - 1, -1, -1):
             part = slice(n * own, (n + 1) * own)
             gi = mm(w1c[...], pg[:, part]) + mm(wg, lg[:, part])
@@ -658,9 +658,9 @@
 
     return staged(
         body,
-        [Far(w1[0]), Far(w1[1], moved=True), Far(wgate_t), Near(pg), Near(lg)],
+        [Near(w1), Near(wgate_t), Near(pg), Near(lg)],
         [Near(plain((dim, own), F32)), Near(plain((max(ns - 1, 1), dim, own), BF16))],
-        [pltpu.VMEM((dim, ce * hid_n), BF16)],
+        [],
         "backward_inputs",
         16,
     )
@@ -828,8 +828,8 @@
     sums = lax.all_to_all(message, BOTH, 0, 0, tiled=True)
 
     acts = [(kept[:5], s) for s in range(n_x)]
-    grad_shift, grad_scale, loss, sec_sib, first_sib, sec_own, first_own, tow_sib, tow_own, pg, lg = backward(
-        sums, params, tower, lows, marks, acts, inputs, w2, wgate_t, w_tower, devices, n_rows, count
+    grad_shift, grad_scale, loss, sec_sib, first_sib, sec_own, first_own, tow_sib, tow_own, pg, lg, w1_joined = backward(
+        sums, params, tower, lows, marks, acts, inputs, w1, w2, wgate_t, w_tower, devices, n_rows, count
     )
     first_sib = swap(first_sib, WIDTH, 1)
     first_sib, sec_sib, tow_sib = together((first_sib, sec_sib, tow_sib))
@@ -837,7 +837,7 @@
         (sec_own, swap(sec_sib, WIDTH, 1)),
         (first_own, first_sib),
         (tow_own, swap(tow_sib, WIDTH, 1)),
-        (lambda grad: backward_inputs(grad, lg, w1, wgate_t, own), pg),
+        (lambda grad: backward_inputs(grad, lg, w1_joined, wgate_t, own), pg),
     )
     inputs_got = [swap(gi_out[s - 1], WIDTH, 2 * s) for s in others]
     m_first = layout(epd, hid_n, out_n, dim, doms, n_rows)[1]

time: 100 us -> 97.8 us (0.978)
  Pallas kernels: 32.6 us -> 29.4 us
  waiting for transfers between devices: 11.6 us -> 13.6 us
  starting transfers between devices: 29.4 us -> 28.4 us
    pallas_call x9, Pallas kernels: 32.6 us -> 29.4 us  [staged(): pl.pallas_call(kernel, out_shape=[o.what if isinstance(o, Near) else pltp...]
    ppermute x26, waiting for transfers between devices: 11.6 us -> 13.6 us  [swap(): return lax.ppermute(value, axis, [(i, i ^ mask) for i in range(size)])]
  transfers between devices with their start and end apart: 26 -> 26, of which waited for: 9 -> 11; matrix products, arithmetic and copies ran while one was open for 1% -> 0% of each run, Pallas kernels for 18% -> 16%
where the time goes in v1:
time: 97.8 us; the launch traced here: 97.6 us
  Pallas kernels  29.4 us (30%)
  starting transfers between devices  28.4 us (29%)
  blocking collectives  24.4 us (25%)
  waiting for transfers between devices  13.6 us (14%)
  between operations  1.09 us (1%)
    pallas_call x9, Pallas kernels, staged(): pl.pallas_call(kernel, out_shape=[o.what if isinstance(o, Near) else pltp...  29.4 us
    ppermute x26, starting transfers between devices, swap(): return lax.ppermute(value, axis, [(i, i ^ mask) for i in range(size)])  28.4 us
    all_to_all x1, blocking collectives, local(): stats = lax.all_to_all(message, BOTH, 0, 0, tiled=True)  14.1 us
    ppermute x26, waiting for transfers between devices, swap(): return lax.ppermute(value, axis, [(i, i ^ mask) for i in range(size)])  13.6 us
    all_to_all x1, blocking collectives, local(): sums = lax.all_to_all(message, BOTH, 0, 0, tiled=True)  10.2 us
  transfers between devices with their start and end apart: 26, of which 11 were waited for; matrix products, arithmetic and copies ran while one was open for 0% of the time, Pallas kernels for 16%

profile of v1, /device:TPU:0, one launch (start us, length us, event | category | flops | bytes accessed | tf_op | source)
XLA Modules:
  0.0 97.6 jit_solution(2699009203999684659)
XLA Ops:
  0.6 0.5 collective-permute-start
  1.2 0.1 collective-permute-start.1
  1.2 2.2 %prepare.1 = (bf16[512,512]{1,0:T(8,128)(2,1)S(1)}, bf16[536,512]{1,0:T(8,128)(2,1)S(1)}, bf16[2,256,256]{2,1,0:T(8,128)(2,1)S(1)}, bf16[3,128,256]{2,1,0:T(8,128)(2,1)S(1)}) custom-call(bf16[2,512,256]{2,1,0:T(8,128)(2,1)} %refs_19_.1, bf16[24,512]{1,0:T(8,128)(2,1)} %bitcast.37, bf16[2,256,256]{2,1,0:T(8,128)(2,1)} %refs_10_.1, ...), custom_call_target="tpu_custom_call" | custom-call | tf_op jit(solution)/shard_map/prepare/pallas_call | solution.py:120
  3.5 2.5 %forward_send.1 = bf16[1,384,512]{2,1,0:T(8,128)(2,1)S(1)} custom-call(bf16[512,512]{1,0:T(8,128)(2,1)S(1)} %get-tuple-element.79.refs_1_.refs_0_, bf16[536,512]{1,0:T(8,128)(2,1)S(1)} %get-tuple-element.80.refs_2_.refs_1_, bf16[2,512,256]{2,1,0:T(8,128)(2,1)S(1)} %collective-permute-done.refs_3_.refs_2_.refs_20_, ...), custom_call_target="tpu_custom_call" | custom-call | tf_op jit(solution)/shard_map/forward_send/pallas_call | solution.py:120
  6.0 3.0 %collective-permute-start.2 = (bf16[1,384,512]{2,1,0:T(8,128)(2,1)S(1)}, bf16[1,384,512]{2,1,0:T(8,128)(2,1)S(1)}, u32[]{:S(2)}, u32[]{:S(2)}) collective-permute-start(bf16[1,384,512]{2,1,0:T(8,128)(2,1)S(1)} %forward_send.1), channel_id=1, source_target_pairs={{0,2},{1,3},{2,0},{3,1},{4,6},{5,7},{6,4},{7,5},{8,10},{9,11},{10,... | collective-permute-start | bytes 1179656 | tf_op jit(solution)/shard_map/ppermute | solution.py:742
  9.0 8.2 %forward_keep.1 = (bf16[2,1024,512]{2,1,0:T(8,128)(2,1)}, bf16[2,1024,512]{2,1,0:T(8,128)(2,1)}, bf16[2,1024,512]{2,1,0:T(8,128)(2,1)}, f32[2,24,512]{2,1,0:T(8,...) custom-call(bf16[2048,512]{1,0:T(8,128)(2,1)} %refs_14_.1, ...), custom_call_target="tpu_custom_call" | custom-call | tf_op jit(solution)/shard_map/forward_keep/pallas_call | solution.py:120
  17.2 1.1 %collective-permute-done.2.refs_2_ = bf16[1,384,512]{2,1,0:T(8,128)(2,1)S(1)} collective-permute-done((bf16[1,384,512]{2,1,0:T(8,128)(2,1)S(1)}, bf16[1,384,512]{2,1,0:T(8,128)(2,1)S(1)}, u32[]{:S(2)}, u32[]{:S(2)}) %collective-permute-start.2) | collective-permute-done | bytes 393248 | tf_op jit(solution)/shard_map/ppermute | solution.py:742
  18.3 0.9 combine.1
  19.2 14.1 %all_to_all.23 = f32[32,8,128]{2,1,0:T(8,128)S(1)} all-to-all(f32[32,8,128]{2,1,0:T(8,128)S(1)} %bitcast.36), channel_id=1, replica_groups=mesh['rows'=8,'width'=4] {'rows','width'}, dimensions={0} | all-to-all | bytes 262144 | tf_op jit(solution)/shard_map/all_to_all | solution.py:824
  33.3 0.4 collective-permute-start.3
  33.8 1.5 %normalise.1 = (f32[24,128]{1,0:T(8,128)S(1)}, bf16[256,128]{1,0:T(8,128)(2,1)S(1)}) custom-call(f32[256,128]{1,0:T(8,128)S(1)} %bitcast.34, f32[384,512]{1,0:T(8,128)S(1)} %get-tuple-element.87.refs_1_.refs_2_, s32[2,512]{1,0:T(2,128)S(1)} %pad_add_fusion.refs_1_.refs_2_.refs_3_, f32[3,128]{1,0:T(4,128)S(1)} %copy-done.1, f32[3,128]{1,0:T(4,128)S(1)} %copy-done.2, ...), custom_call_target="tpu_custom_call" | custom-call | tf_op jit(solution)/shard_map/normalise/pallas_call | solution.py:120
  35.3 10.2 %all_to_all.24 = bf16[32,8,128]{2,1,0:T(8,128)(2,1)S(1)} all-to-all(bf16[32,8,128]{2,1,0:T(8,128)(2,1)S(1)} %bitcast.39), channel_id=1, replica_groups=mesh['rows'=8,'width'=4] {'rows','width'}, dimensions={0} | all-to-all | bytes 131072 | tf_op jit(solution)/shard_map/all_to_all | solution.py:828
  45.6 8.3 %backward.1 = (f32[3,128]{1,0:T(4,128)}, f32[3,128]{1,0:T(4,128)}, f32[1,1]{1,0:T(1,128)}, bf16[8,128,128]{2,1,0:T(8,128)(2,1)S(1)}, bf16[8,256,128]{2,1,0:T(8,1...) custom-call(bf16[256,128]{1,0:T(8,128)(2,1)S(1)} %bitcast.35, ...), custom_call_target="tpu_custom_call" | custom-call | tf_op jit(solution)/shard_map/backward/pallas_call | solution.py:120
  53.9 0.2 collective-permute-start.4
  54.1 1.8 %collective-permute-done.4 = bf16[8,256,128]{2,1,0:T(8,128)(2,1)S(1)} collective-permute-done((bf16[8,256,128]{2,1,0:T(8,128)(2,1)S(1)}, bf16[8,256,128]{2,1,0:T(8,128)(2,1)S(1)}, u32[]{:S(2)}, u32[]{:S(2)}) %collective-permute-start.4) | collective-permute-done | bytes 524320 | tf_op jit(solution)/shard_map/ppermute | solution.py:742
  55.9 0.1 collective-permute-start.10
  56.0 0.4 collective-permute-start.5
  56.4 0.1 add_convert_fusion
  56.5 1.5 %collective-permute-start.6 = (bf16[4,256,128]{2,1,0:T(8,128)(2,1)S(1)}, bf16[4,256,128]{2,1,0:T(8,128)(2,1)S(1)}, u32[]{:S(2)}, u32[]{:S(2)}) collective-permute-start(bf16[4,256,128]{2,1,0:T(8,128)(2,1)S(1)} %add_convert_fusion), channel_id=1, source_target_pairs={{0,4},{4,0},{8,12},{12,8},{16,20},{20,16},{24,28},{28,24},{1,5},{5... | collective-permute-start | bytes 786440 | tf_op jit(solution)/shard_map/ppermute | solution.py:742
  58.1 0.4 collective-permute-start.11
  58.5 1.4 %collective-permute-start.9 = (bf16[2,128,128]{2,1,0:T(8,128)(2,1)S(1)}, bf16[2,128,128]{2,1,0:T(8,128)(2,1)S(1)}, u32[]{:S(2)}, u32[]{:S(2)}) collective-permute-start(bf16[2,128,128]{2,1,0:T(8,128)(2,1)S(1)} %get-tuple-element.153), channel_id=1, source_target_pairs={{0,24},{4,28},{8,16},{12,20},{16,8},{20,12},{24,0},{28,4},{1,25},{... | collective-permute-start | bytes 196616 | tf_op jit(solution)/shard_map/ppermute | solution.py:742
  59.9 0.8 collective-permute-start.8
  60.7 2.2 %collective-permute-start.7 = (bf16[2,128,128]{2,1,0:T(8,128)(2,1)S(1)}, bf16[2,128,128]{2,1,0:T(8,128)(2,1)S(1)}, u32[]{:S(2)}, u32[]{:S(2)}) collective-permute-start(bf16[2,128,128]{2,1,0:T(8,128)(2,1)S(1)} %get-tuple-element.155), channel_id=1, source_target_pairs={{0,8},{4,12},{8,0},{12,4},{16,24},{20,28},{24,16},{28,20},{1,9},{5... | collective-permute-start | bytes 196616 | tf_op jit(solution)/shard_map/ppermute | solution.py:742
  63.0 0.4 collective-permute-done.11
  63.5 1.1 %collective-permute-start.12 = (bf16[4,64,128]{2,1,0:T(8,128)(2,1)S(1)}, bf16[4,64,128]{2,1,0:T(8,128)(2,1)S(1)}, u32[]{:S(2)}, u32[]{:S(2)}) collective-permute-start(bf16[4,64,128]{2,1,0:T(8,128)(2,1)S(1)} %slice.192), channel_id=1, source_target_pairs={{0,4},{4,0},{8,12},{12,8},{16,20},{20,16},{24,28},{28,24},{1,5},{5... | collective-permute-start | bytes 196616 | tf_op jit(solution)/shard_map/ppermute | solution.py:742
  64.5 2.1 %backward_inputs.1 = (f32[512,512]{1,0:T(8,128)S(1)}, bf16[1,512,512]{2,1,0:T(8,128)(2,1)S(1)}) custom-call(bf16[512,1024]{1,0:T(8,128)(2,1)S(1)} %get-tuple-element.108.refs_0_, bf16[24,512]{1,0:T(8,128)(2,1)S(1)} %bitcast.38, bf16[1024,1024]{1,0:T(8,128)(2,1)S(1)} %get-tuple-element.109.refs_2_, bf16[24,1024]{1,0:T(8,128)(2,1)S(1)} %get-tuple-element.110.refs_3_), custom_call_target="tpu_custom_call" | custom-call | tf_op jit(solution)/shard_map/backward_inputs/pallas_call | solution.py:120
  66.7 0.5 collective-permute-done.8
  67.2 0.6 collective-permute-done.12
  67.8 0.1 add_bitcast_fusion
  68.0 0.1 collective-permute-start.13
  68.1 1.4 %collective-permute-start.14 = (bf16[320,128]{1,0:T(8,128)(2,1)S(1)}, bf16[320,128]{1,0:T(8,128)(2,1)S(1)}, u32[]{:S(2)}, u32[]{:S(2)}) collective-permute-start(bf16[320,128]{1,0:T(8,128)(2,1)S(1)} %get-tuple-element.119), channel_id=1, source_target_pairs={{0,16},{4,20},{8,24},{12,28},{16,0},{20,4},{24,8},{28,12},{1,17},{... | collective-permute-start | bytes 245768 | tf_op jit(solution)/shard_map/ppermute | solution.py:742
  69.6 2.9 %collective-permute-start.15 = (bf16[320,128]{1,0:T(8,128)(2,1)S(1)}, bf16[320,128]{1,0:T(8,128)(2,1)S(1)}, u32[]{:S(2)}, u32[]{:S(2)}) collective-permute-start(bf16[320,128]{1,0:T(8,128)(2,1)S(1)} %pad_maximum_fusion.4), channel_id=1, source_target_pairs={{0,24},{4,28},{8,16},{12,20},{16,8},{20,12},{24,0},{28,4},{1,25},{... | collective-permute-start | bytes 245768 | tf_op jit(solution)/shard_map/ppermute | solution.py:742
  72.5 1.0 %collective-permute-start.16 = (bf16[2,128,128]{2,1,0:T(8,128)(2,1)S(1)}, bf16[2,128,128]{2,1,0:T(8,128)(2,1)S(1)}, u32[]{:S(2)}, u32[]{:S(2)}) collective-permute-start(bf16[2,128,128]{2,1,0:T(8,128)(2,1)S(1)} %fusion.14), channel_id=1, source_target_pairs={{0,4},{4,0},{8,12},{12,8},{16,20},{20,16},{24,28},{28,24},{1,5},{5... | collective-permute-start | bytes 196616 | tf_op jit(solution)/shard_map/ppermute | solution.py:742
  73.5 1.0 %collective-permute-start.20 = (bf16[512,512]{1,0:T(8,128)(2,1)S(1)}, bf16[512,512]{1,0:T(8,128)(2,1)S(1)}, u32[]{:S(2)}, u32[]{:S(2)}) collective-permute-start(bf16[512,512]{1,0:T(8,128)(2,1)S(1)} %bitcast.40), channel_id=1, source_target_pairs={{0,2},{1,3},{2,0},{3,1},{4,6},{5,7},{6,4},{7,5},{8,10},{9,11},{10,... | collective-permute-start | bytes 1572872 | tf_op jit(solution)/shard_map/ppermute | solution.py:742
  74.5 2.3 %collective-permute-done.16 = bf16[2,128,128]{2,1,0:T(8,128)(2,1)S(1)} collective-permute-done((bf16[2,128,128]{2,1,0:T(8,128)(2,1)S(1)}, bf16[2,128,128]{2,1,0:T(8,128)(2,1)S(1)}, u32[]{:S(2)}, u32[]{:S(2)}) %collective-permute-start.16) | collective-permute-done | bytes 65568 | tf_op jit(solution)/shard_map/ppermute | solution.py:742
  76.7 0.2 collective-permute-done.14
  77.0 2.0 %collective-permute-start.19 = (bf16[320,128]{1,0:T(8,128)(2,1)S(1)}, bf16[320,128]{1,0:T(8,128)(2,1)S(1)}, u32[]{:S(2)}, u32[]{:S(2)}) collective-permute-start(bf16[320,128]{1,0:T(8,128)(2,1)S(1)} %fusion.3), channel_id=1, source_target_pairs={{0,24},{4,28},{8,16},{12,20},{16,8},{20,12},{24,0},{28,4},{1,25},{... | collective-permute-start | bytes 245768 | tf_op jit(solution)/shard_map/ppermute | solution.py:742
  79.0 1.0 %collective-permute-start.18 = (bf16[320,128]{1,0:T(8,128)(2,1)S(1)}, bf16[320,128]{1,0:T(8,128)(2,1)S(1)}, u32[]{:S(2)}, u32[]{:S(2)}) collective-permute-start(bf16[320,128]{1,0:T(8,128)(2,1)S(1)} %fusion.3), channel_id=1, source_target_pairs={{0,16},{4,20},{8,24},{12,28},{16,0},{20,4},{24,8},{28,12},{1,17},{... | collective-permute-start | bytes 245768 | tf_op jit(solution)/shard_map/ppermute | solution.py:742
  80.0 1.5 %collective-permute-start.17 = (bf16[320,128]{1,0:T(8,128)(2,1)S(1)}, bf16[320,128]{1,0:T(8,128)(2,1)S(1)}, u32[]{:S(2)}, u32[]{:S(2)}) collective-permute-start(bf16[320,128]{1,0:T(8,128)(2,1)S(1)} %fusion.3), channel_id=1, source_target_pairs={{0,8},{4,12},{8,0},{12,4},{16,24},{20,28},{24,16},{28,20},{1,9},{5... | collective-permute-start | bytes 245768 | tf_op jit(solution)/shard_map/ppermute | solution.py:742
  81.5 2.0 %collective-permute-done.19 = bf16[320,128]{1,0:T(8,128)(2,1)S(1)} collective-permute-done((bf16[320,128]{1,0:T(8,128)(2,1)S(1)}, bf16[320,128]{1,0:T(8,128)(2,1)S(1)}, u32[]{:S(2)}, u32[]{:S(2)}) %collective-permute-start.19) | collective-permute-done | bytes 81952 | tf_op jit(solution)/shard_map/ppermute | solution.py:742
  83.4 2.0 %collective-permute-done.18 = bf16[320,128]{1,0:T(8,128)(2,1)S(1)} collective-permute-done((bf16[320,128]{1,0:T(8,128)(2,1)S(1)}, bf16[320,128]{1,0:T(8,128)(2,1)S(1)}, u32[]{:S(2)}, u32[]{:S(2)}) %collective-permute-start.18) | collective-permute-done | bytes 81952 | tf_op jit(solution)/shard_map/ppermute | solution.py:742
  85.5 1.0 %collective-permute-start.21 = (bf16[4,320,128]{2,1,0:T(8,128)(2,1)S(1)}, bf16[4,320,128]{2,1,0:T(8,128)(2,1)S(1)}, u32[]{:S(2)}, u32[]{:S(2)}) collective-permute-start(bf16[4,320,128]{2,1,0:T(8,128)(2,1)S(1)} %pad_maximum_fusion), channel_id=1, source_target_pairs={{0,4},{4,0},{8,12},{12,8},{16,20},{20,16},{24,28},{28,24},{1,5},{5... | collective-permute-start | bytes 983048 | tf_op jit(solution)/shard_map/ppermute | solution.py:742
  86.5 1.8 %collective-permute-start.24 = (bf16[2,128,128]{2,1,0:T(8,128)(2,1)S(1)}, bf16[2,128,128]{2,1,0:T(8,128)(2,1)S(1)}, u32[]{:S(2)}, u32[]{:S(2)}) collective-permute-start(bf16[2,128,128]{2,1,0:T(8,128)(2,1)S(1)} %add_convert_fusion.1), channel_id=1, source_target_pairs={{0,24},{4,28},{8,16},{12,20},{16,8},{20,12},{24,0},{28,4},{1,25},{... | collective-permute-start | bytes 196616 | tf_op jit(solution)/shard_map/ppermute | solution.py:742
  88.4 2.5 %collective-permute-start.22 = (bf16[2,128,128]{2,1,0:T(8,128)(2,1)S(1)}, bf16[2,128,128]{2,1,0:T(8,128)(2,1)S(1)}, u32[]{:S(2)}, u32[]{:S(2)}) collective-permute-start(bf16[2,128,128]{2,1,0:T(8,128)(2,1)S(1)} %add_convert_fusion.1), channel_id=1, source_target_pairs={{0,8},{4,12},{8,0},{12,4},{16,24},{20,28},{24,16},{28,20},{1,9},{5... | collective-permute-start | bytes 196616 | tf_op jit(solution)/shard_map/ppermute | solution.py:742
  90.9 1.7 %finish_inputs.1 = f32[512,512]{1,0:T(8,128)} custom-call(f32[512,512]{1,0:T(8,128)S(1)} %get-tuple-element.135.refs_0_, bf16[512,512]{1,0:T(8,128)(2,1)S(1)} %collective-permute-done.20.refs_1_), custom_call_target="tpu_custom_call" | custom-call | tf_op jit(solution)/shard_map/finish_inputs/pallas_call | solution.py:120
  92.6 1.3 %collective-permute-done.23 = bf16[2,128,128]{2,1,0:T(8,128)(2,1)S(1)} collective-permute-done((bf16[2,128,128]{2,1,0:T(8,128)(2,1)S(1)}, bf16[2,128,128]{2,1,0:T(8,128)(2,1)S(1)}, u32[]{:S(2)}, u32[]{:S(2)}) %collective-permute-start.23) | collective-permute-done | bytes 65568 | tf_op jit(solution)/shard_map/ppermute | solution.py:742
  94.2 1.3 %collective-permute-done.25.refs_2_ = bf16[8,64,128]{2,1,0:T(8,128)(2,1)S(1)} collective-permute-done((bf16[8,64,128]{2,1,0:T(8,128)(2,1)S(1)}, bf16[8,64,128]{2,1,0:T(8,128)(2,1)S(1)}, u32[]{:S(2)}, u32[]{:S(2)}) %collective-permute-start.25) | collective-permute-done | bytes 131104 | tf_op jit(solution)/shard_map/ppermute | solution.py:742
  95.5 2.0 %finish_weights.1 = (f32[2,512,256]{2,1,0:T(8,128)}, f32[2,256,256]{2,1,0:T(8,128)}, f32[3,256,128]{2,1,0:T(8,128)}, f32[24,512]{1,0:T(8,128)}, f32[3,128]{1,0:T(4,128)}) custom-call(bf16[8,128,128]{2,1,0:T(8,128)(2,1)S(1)} %pad_maximum_fusion.1.refs_0_, bf16[8,320,128]{2,1,0:T(8,128)(2,1)S(1)} %constant_dynamic-update-slice_fusion.refs_1_, ...), custom_call_target="tpu_custom_call" | custom-call | tf_op jit(solution)/shard_map/finish_weights/pallas_call | solution.py:120
  (45 shorter events, 0.7 us)
Async XLA Ops:
  0.6 2.8 %collective-permute-start = (bf16[2,512,256]{2,1,0:T(8,128)(2,1)}, bf16[2,512,256]{2,1,0:T(8,128)(2,1)S(1)}, u32[]{:S(2)}, u32[]{:S(2)}) collective-permute-start(bf16[2,512,256]{2,1,0:T(8,128)(2,1)} %refs_19_.1), channel_id=1, source_target_pairs={{0,1},{1,0},{2,3},{3,2},{4,5},{5,4},{6,7},{7,6},{8,9},{9,8},{10,11... | collective-permute-start | bytes 1572872 | tf_op jit(solution)/shard_map/ppermute | solution.py:742
  1.2 2.3 %collective-permute-start.1 = (bf16[2,256,256]{2,1,0:T(8,128)(2,1)}, bf16[2,256,256]{2,1,0:T(8,128)(2,1)S(1)}, u32[]{:S(2)}, u32[]{:S(2)}) collective-permute-start(bf16[2,256,256]{2,1,0:T(8,128)(2,1)} %refs_10_.1), channel_id=1, source_target_pairs={{0,1},{1,0},{2,3},{3,2},{4,5},{5,4},{6,7},{7,6},{8,9},{9,8},{10,11... | collective-permute-start | bytes 786440 | tf_op jit(solution)/shard_map/ppermute | solution.py:742
  3.4 5.5 %copy-start.4 = (s32[512]{0:T(512)S(1)}, s32[512]{0:T(512)}, u32[]{:S(2)}) copy-start(s32[512]{0:T(512)} %param.19) | copy-start | bytes 6148
  3.4 5.5 %copy-start.5 = (s32[512]{0:T(512)S(1)}, s32[512]{0:T(512)}, u32[]{:S(2)}) copy-start(s32[512]{0:T(512)} %param.18) | copy-start | bytes 6148
  6.0 12.3 %collective-permute-start.2 = (bf16[1,384,512]{2,1,0:T(8,128)(2,1)S(1)}, bf16[1,384,512]{2,1,0:T(8,128)(2,1)S(1)}, u32[]{:S(2)}, u32[]{:S(2)}) collective-permute-start(bf16[1,384,512]{2,1,0:T(8,128)(2,1)S(1)} %forward_send.1), channel_id=1, source_target_pairs={{0,2},{1,3},{2,0},{3,1},{4,6},{5,7},{6,4},{7,5},{8,10},{9,11},{10,... | collective-permute-start | bytes 1179656 | tf_op jit(solution)/shard_map/ppermute | solution.py:742
  9.0 24.8 %copy-start.1 = (f32[3,128]{1,0:T(4,128)S(1)}, f32[3,128]{1,0:T(4,128)}, u32[]{:S(2)}) copy-start(f32[3,128]{1,0:T(4,128)} %refs_3_.3) | copy-start | bytes 4612
  9.0 24.8 %copy-start.2 = (f32[3,128]{1,0:T(4,128)S(1)}, f32[3,128]{1,0:T(4,128)}, u32[]{:S(2)}) copy-start(f32[3,128]{1,0:T(4,128)} %refs_4_.3) | copy-start | bytes 4612
  9.0 24.8 %copy-start.3 = (f32[3,128]{1,0:T(4,128)S(1)}, f32[3,128]{1,0:T(4,128)}, u32[]{:S(2)}) copy-start(f32[3,128]{1,0:T(4,128)} %refs_5_.2) | copy-start | bytes 4612
  33.3 12.2 %collective-permute-start.3 = (bf16[400,512]{1,0:T(8,128)(2,1)S(1)}, bf16[400,512]{1,0:T(8,128)(2,1)S(1)}, u32[]{:S(2)}, u32[]{:S(2)}) collective-permute-start(bf16[400,512]{1,0:T(8,128)(2,1)S(1)} %get-tuple-element.90), channel_id=1, source_target_pairs={{0,2},{1,3},{2,0},{3,1},{4,6},{5,7},{6,4},{7,5},{8,10},{9,11},{10,... | collective-permute-start | bytes 1228808 | tf_op jit(solution)/shard_map/ppermute | solution.py:742
  53.9 10.6 %copy-start = (bf16[3,512,8]{1,2,0:T(8,128)(2,1)S(1)}, bf16[3,512,8]{1,2,0:T(8,128)(2,1)}, u32[]{:S(2)}) copy-start(bf16[3,512,8]{1,2,0:T(8,128)(2,1)} %param.13) | copy-start | bytes 73732
  53.9 2.0 %collective-permute-start.4 = (bf16[8,256,128]{2,1,0:T(8,128)(2,1)S(1)}, bf16[8,256,128]{2,1,0:T(8,128)(2,1)S(1)}, u32[]{:S(2)}, u32[]{:S(2)}) collective-permute-start(bf16[8,256,128]{2,1,0:T(8,128)(2,1)S(1)} %get-tuple-element.98), channel_id=1, source_target_pairs={{0,1},{1,0},{2,3},{3,2},{4,5},{5,4},{6,7},{7,6},{8,9},{9,8},{10,11... | collective-permute-start | bytes 1572872 | tf_op jit(solution)/shard_map/ppermute | solution.py:742
  55.9 2.1 %collective-permute-start.10 = (bf16[8,64,128]{2,1,0:T(8,128)(2,1)S(1)}, bf16[8,64,128]{2,1,0:T(8,128)(2,1)S(1)}, u32[]{:S(2)}, u32[]{:S(2)}) collective-permute-start(bf16[8,64,128]{2,1,0:T(8,128)(2,1)S(1)} %get-tuple-element.105), channel_id=1, source_target_pairs={{0,1},{1,0},{2,3},{3,2},{4,5},{5,4},{6,7},{7,6},{8,9},{9,8},{10,11... | collective-permute-start | bytes 393224 | tf_op jit(solution)/shard_map/ppermute | solution.py:742
  56.0 2.4 %collective-permute-start.5 = (bf16[8,128,128]{2,1,0:T(8,128)(2,1)S(1)}, bf16[8,128,128]{2,1,0:T(8,128)(2,1)S(1)}, u32[]{:S(2)}, u32[]{:S(2)}) collective-permute-start(bf16[8,128,128]{2,1,0:T(8,128)(2,1)S(1)} %get-tuple-element.101), channel_id=1, source_target_pairs={{0,1},{1,0},{2,3},{3,2},{4,5},{5,4},{6,7},{7,6},{8,9},{9,8},{10,11... | collective-permute-start | bytes 786440 | tf_op jit(solution)/shard_map/ppermute | solution.py:742
  56.5 10.2 %collective-permute-start.6 = (bf16[4,256,128]{2,1,0:T(8,128)(2,1)S(1)}, bf16[4,256,128]{2,1,0:T(8,128)(2,1)S(1)}, u32[]{:S(2)}, u32[]{:S(2)}) collective-permute-start(bf16[4,256,128]{2,1,0:T(8,128)(2,1)S(1)} %add_convert_fusion), channel_id=1, source_target_pairs={{0,4},{4,0},{8,12},{12,8},{16,20},{20,16},{24,28},{28,24},{1,5},{5... | collective-permute-start | bytes 786440 | tf_op jit(solution)/shard_map/ppermute | solution.py:742
  58.1 5.3 %collective-permute-start.11 = (bf16[8,64,128]{2,1,0:T(8,128)(2,1)S(1)}, bf16[8,64,128]{2,1,0:T(8,128)(2,1)S(1)}, u32[]{:S(2)}, u32[]{:S(2)}) collective-permute-start(bf16[8,64,128]{2,1,0:T(8,128)(2,1)S(1)} %fusion), channel_id=1, source_target_pairs={{0,2},{1,3},{2,0},{3,1},{4,6},{5,7},{6,4},{7,5},{8,10},{9,11},{10,... | collective-permute-start | bytes 393224 | tf_op jit(solution)/shard_map/ppermute | solution.py:742
  58.5 8.1 %collective-permute-start.9 = (bf16[2,128,128]{2,1,0:T(8,128)(2,1)S(1)}, bf16[2,128,128]{2,1,0:T(8,128)(2,1)S(1)}, u32[]{:S(2)}, u32[]{:S(2)}) collective-permute-start(bf16[2,128,128]{2,1,0:T(8,128)(2,1)S(1)} %get-tuple-element.153), channel_id=1, source_target_pairs={{0,24},{4,28},{8,16},{12,20},{16,8},{20,12},{24,0},{28,4},{1,25},{... | collective-permute-start | bytes 196616 | tf_op jit(solution)/shard_map/ppermute | solution.py:742
  59.9 7.3 %collective-permute-start.8 = (bf16[2,128,128]{2,1,0:T(8,128)(2,1)S(1)}, bf16[2,128,128]{2,1,0:T(8,128)(2,1)S(1)}, u32[]{:S(2)}, u32[]{:S(2)}) collective-permute-start(bf16[2,128,128]{2,1,0:T(8,128)(2,1)S(1)} %get-tuple-element.154), channel_id=1, source_target_pairs={{0,16},{4,20},{8,24},{12,28},{16,0},{20,4},{24,8},{28,12},{1,17},{... | collective-permute-start | bytes 196616 | tf_op jit(solution)/shard_map/ppermute | solution.py:742
  60.7 6.5 %collective-permute-start.7 = (bf16[2,128,128]{2,1,0:T(8,128)(2,1)S(1)}, bf16[2,128,128]{2,1,0:T(8,128)(2,1)S(1)}, u32[]{:S(2)}, u32[]{:S(2)}) collective-permute-start(bf16[2,128,128]{2,1,0:T(8,128)(2,1)S(1)} %get-tuple-element.155), channel_id=1, source_target_pairs={{0,8},{4,12},{8,0},{12,4},{16,24},{20,28},{24,16},{28,20},{1,9},{5... | collective-permute-start | bytes 196616 | tf_op jit(solution)/shard_map/ppermute | solution.py:742
  63.5 4.3 %collective-permute-start.12 = (bf16[4,64,128]{2,1,0:T(8,128)(2,1)S(1)}, bf16[4,64,128]{2,1,0:T(8,128)(2,1)S(1)}, u32[]{:S(2)}, u32[]{:S(2)}) collective-permute-start(bf16[4,64,128]{2,1,0:T(8,128)(2,1)S(1)} %slice.192), channel_id=1, source_target_pairs={{0,4},{4,0},{8,12},{12,8},{16,20},{20,16},{24,28},{28,24},{1,5},{5... | collective-permute-start | bytes 196616 | tf_op jit(solution)/shard_map/ppermute | solution.py:742
  68.0 8.7 %collective-permute-start.13 = (bf16[320,128]{1,0:T(8,128)(2,1)S(1)}, bf16[320,128]{1,0:T(8,128)(2,1)S(1)}, u32[]{:S(2)}, u32[]{:S(2)}) collective-permute-start(bf16[320,128]{1,0:T(8,128)(2,1)S(1)} %get-tuple-element.118), channel_id=1, source_target_pairs={{0,8},{4,12},{8,0},{12,4},{16,24},{20,28},{24,16},{28,20},{1,9},{5... | collective-permute-start | bytes 245768 | tf_op jit(solution)/shard_map/ppermute | solution.py:742
  68.1 8.8 %collective-permute-start.14 = (bf16[320,128]{1,0:T(8,128)(2,1)S(1)}, bf16[320,128]{1,0:T(8,128)(2,1)S(1)}, u32[]{:S(2)}, u32[]{:S(2)}) collective-permute-start(bf16[320,128]{1,0:T(8,128)(2,1)S(1)} %get-tuple-element.119), channel_id=1, source_target_pairs={{0,16},{4,20},{8,24},{12,28},{16,0},{20,4},{24,8},{28,12},{1,17},{... | collective-permute-start | bytes 245768 | tf_op jit(solution)/shard_map/ppermute | solution.py:742
  69.6 7.3 %collective-permute-start.15 = (bf16[320,128]{1,0:T(8,128)(2,1)S(1)}, bf16[320,128]{1,0:T(8,128)(2,1)S(1)}, u32[]{:S(2)}, u32[]{:S(2)}) collective-permute-start(bf16[320,128]{1,0:T(8,128)(2,1)S(1)} %pad_maximum_fusion.4), channel_id=1, source_target_pairs={{0,24},{4,28},{8,16},{12,20},{16,8},{20,12},{24,0},{28,4},{1,25},{... | collective-permute-start | bytes 245768 | tf_op jit(solution)/shard_map/ppermute | solution.py:742
  72.5 4.3 %collective-permute-start.16 = (bf16[2,128,128]{2,1,0:T(8,128)(2,1)S(1)}, bf16[2,128,128]{2,1,0:T(8,128)(2,1)S(1)}, u32[]{:S(2)}, u32[]{:S(2)}) collective-permute-start(bf16[2,128,128]{2,1,0:T(8,128)(2,1)S(1)} %fusion.14), channel_id=1, source_target_pairs={{0,4},{4,0},{8,12},{12,8},{16,20},{20,16},{24,28},{28,24},{1,5},{5... | collective-permute-start | bytes 196616 | tf_op jit(solution)/shard_map/ppermute | solution.py:742
  73.5 12.0 %collective-permute-start.20 = (bf16[512,512]{1,0:T(8,128)(2,1)S(1)}, bf16[512,512]{1,0:T(8,128)(2,1)S(1)}, u32[]{:S(2)}, u32[]{:S(2)}) collective-permute-start(bf16[512,512]{1,0:T(8,128)(2,1)S(1)} %bitcast.40), channel_id=1, source_target_pairs={{0,2},{1,3},{2,0},{3,1},{4,6},{5,7},{6,4},{7,5},{8,10},{9,11},{10,... | collective-permute-start | bytes 1572872 | tf_op jit(solution)/shard_map/ppermute | solution.py:742
  77.0 6.4 %collective-permute-start.19 = (bf16[320,128]{1,0:T(8,128)(2,1)S(1)}, bf16[320,128]{1,0:T(8,128)(2,1)S(1)}, u32[]{:S(2)}, u32[]{:S(2)}) collective-permute-start(bf16[320,128]{1,0:T(8,128)(2,1)S(1)} %fusion.3), channel_id=1, source_target_pairs={{0,24},{4,28},{8,16},{12,20},{16,8},{20,12},{24,0},{28,4},{1,25},{... | collective-permute-start | bytes 245768 | tf_op jit(solution)/shard_map/ppermute | solution.py:742
  79.0 6.5 %collective-permute-start.18 = (bf16[320,128]{1,0:T(8,128)(2,1)S(1)}, bf16[320,128]{1,0:T(8,128)(2,1)S(1)}, u32[]{:S(2)}, u32[]{:S(2)}) collective-permute-start(bf16[320,128]{1,0:T(8,128)(2,1)S(1)} %fusion.3), channel_id=1, source_target_pairs={{0,16},{4,20},{8,24},{12,28},{16,0},{20,4},{24,8},{28,12},{1,17},{... | collective-permute-start | bytes 245768 | tf_op jit(solution)/shard_map/ppermute | solution.py:742
  80.0 5.5 %collective-permute-start.17 = (bf16[320,128]{1,0:T(8,128)(2,1)S(1)}, bf16[320,128]{1,0:T(8,128)(2,1)S(1)}, u32[]{:S(2)}, u32[]{:S(2)}) collective-permute-start(bf16[320,128]{1,0:T(8,128)(2,1)S(1)} %fusion.3), channel_id=1, source_target_pairs={{0,8},{4,12},{8,0},{12,4},{16,24},{20,28},{24,16},{28,20},{1,9},{5... | collective-permute-start | bytes 245768 | tf_op jit(solution)/shard_map/ppermute | solution.py:742
  85.5 8.5 %collective-permute-start.21 = (bf16[4,320,128]{2,1,0:T(8,128)(2,1)S(1)}, bf16[4,320,128]{2,1,0:T(8,128)(2,1)S(1)}, u32[]{:S(2)}, u32[]{:S(2)}) collective-permute-start(bf16[4,320,128]{2,1,0:T(8,128)(2,1)S(1)} %pad_maximum_fusion), channel_id=1, source_target_pairs={{0,4},{4,0},{8,12},{12,8},{16,20},{20,16},{24,28},{28,24},{1,5},{5... | collective-permute-start | bytes 983048 | tf_op jit(solution)/shard_map/ppermute | solution.py:742
  86.5 6.1 %collective-permute-start.24 = (bf16[2,128,128]{2,1,0:T(8,128)(2,1)S(1)}, bf16[2,128,128]{2,1,0:T(8,128)(2,1)S(1)}, u32[]{:S(2)}, u32[]{:S(2)}) collective-permute-start(bf16[2,128,128]{2,1,0:T(8,128)(2,1)S(1)} %add_convert_fusion.1), channel_id=1, source_target_pairs={{0,24},{4,28},{8,16},{12,20},{16,8},{20,12},{24,0},{28,4},{1,25},{... | collective-permute-start | bytes 196616 | tf_op jit(solution)/shard_map/ppermute | solution.py:742
  88.3 5.7 %collective-permute-start.23 = (bf16[2,128,128]{2,1,0:T(8,128)(2,1)S(1)}, bf16[2,128,128]{2,1,0:T(8,128)(2,1)S(1)}, u32[]{:S(2)}, u32[]{:S(2)}) collective-permute-start(bf16[2,128,128]{2,1,0:T(8,128)(2,1)S(1)} %add_convert_fusion.1), channel_id=1, source_target_pairs={{0,16},{4,20},{8,24},{12,28},{16,0},{20,4},{24,8},{28,12},{1,17},{... | collective-permute-start | bytes 196616 | tf_op jit(solution)/shard_map/ppermute | solution.py:742
  88.4 5.6 %collective-permute-start.22 = (bf16[2,128,128]{2,1,0:T(8,128)(2,1)S(1)}, bf16[2,128,128]{2,1,0:T(8,128)(2,1)S(1)}, u32[]{:S(2)}, u32[]{:S(2)}) collective-permute-start(bf16[2,128,128]{2,1,0:T(8,128)(2,1)S(1)} %add_convert_fusion.1), channel_id=1, source_target_pairs={{0,8},{4,12},{8,0},{12,4},{16,24},{20,28},{24,16},{28,20},{1,9},{5... | collective-permute-start | bytes 196616 | tf_op jit(solution)/shard_map/ppermute | solution.py:742
  94.0 1.4 %collective-permute-start.25 = (bf16[8,64,128]{2,1,0:T(8,128)(2,1)S(1)}, bf16[8,64,128]{2,1,0:T(8,128)(2,1)S(1)}, u32[]{:S(2)}, u32[]{:S(2)}) collective-permute-start(bf16[8,64,128]{2,1,0:T(8,128)(2,1)S(1)} %slice.138), channel_id=1, source_target_pairs={{0,1},{1,0},{2,3},{3,2},{4,5},{5,4},{6,7},{7,6},{8,9},{9,8},{10,11... | collective-permute-start | bytes 393224 | tf_op jit(solution)/shard_map/ppermute | solution.py:742

commit v2 on v1

--- a/solution.py
+++ b/solution.py
@@ -27,6 +27,25 @@
 
 def sigmoid(v):
     return 0.5 * jnp.tanh(0.5 * v) + 0.5
+
+
+PLAIN = 8
+
+
+def base(values):
+    first = values[:, :PLAIN].astype(BF16).astype(F32)
+    return jnp.sum(first, axis=1, keepdims=True) * (1.0 / PLAIN)
+
+
+def encode(values):
+    lane = lax.broadcasted_iota(jnp.int32, values.shape, 1)
+    return jnp.where(lane < PLAIN, values, values - base(values)).astype(BF16)
+
+
+def decode(values, added, start=0):
+    lane = lax.broadcasted_iota(jnp.int32, values.shape, 1)
+    values = values.astype(F32)
+    return jnp.where(lane < PLAIN - start, values, values + added)
 
 
 class Source:
@@ -264,9 +283,8 @@
             if n == 0 or not keep:
                 tower = outs[-1]
                 for k in range(doms):
-                    tower.buf[n, k * th : (k + 1) * th, :] = mm(
-                        wt[k], mixed[n, k * out_n : (k + 1) * out_n, :]
-                    ).astype(tower_out)
+                    sums = mm(wt[k], mixed[n, k * out_n : (k + 1) * out_n, :])
+                    tower.buf[n, k * th : (k + 1) * th, :] = sums if keep else encode(sums)
                 tower.flush(n)
 
     kept = [
@@ -302,9 +320,9 @@
             at = slice(k * LANE, (k + 1) * LANE)
             total = part[0, at, :]
             for ref in got:
-                total = total + ref[0, at, :].astype(F32)
+                total = total + decode(ref[0, at, :], base(ref[0, at, :LANE]))
             tower[at, :] = total
-            low[at, :] = total.astype(BF16)
+            low[at, :] = encode(total)
             mean = jnp.sum(total, axis=1, keepdims=True) * (1.0 / own)
             dev = total - mean
             cols[:, k : k + 1] = mean
@@ -335,11 +353,10 @@
     return got
 
 
-def chosen_tower(tower, dom, wide, lanes, doms):
-    values = [tower[k * LANE : (k + 1) * LANE, lanes].astype(F32) for k in range(doms)]
+def chosen_tower(values, dom, wide, doms):
     mean, gain, shift, head = (pick(dom, [wide[j * doms + k] for k in range(doms)]) for j in range(4))
     centred = pick(dom, values) - mean
-    return values, centred, centred * gain + shift, gain, head
+    return centred, centred * gain + shift, gain, head
 
 
 def spread_columns(wide, rows_ref, n):
@@ -376,7 +393,8 @@
             part = slice(u * LANE, (u + 1) * LANE)
             dom = mk[0:1, part]
             target = mk[1:2, part].astype(F32)
-            _, centred, affine, _, head_w = chosen_tower(tw, dom, wide, part, doms)
+            values = [tw[k * LANE : (k + 1) * LANE, part] for k in range(doms)]
+            centred, affine, _, head_w = chosen_tower(values, dom, wide, doms)
             s = sigmoid(affine)
             act = affine * s
             chosen = jnp.sum(act * head_w, axis=0, keepdims=True)
@@ -393,16 +411,16 @@
         sums = (mm_t(one_hot, high) + mm_t(one_hot, (q[...] - high.astype(F32)).astype(BF16)))[:doms]
         tile = [sums[:, :LANE], sums[:, LANE : 2 * LANE] * inv]
         all_rows = tile + [loss, jnp.zeros((1, LANE), F32)]
-        twice = jnp.concatenate(all_rows + all_rows, axis=0).astype(BF16)
-        for d in range(devices // 2):
-            message[d * 16 : (d + 1) * 16, :] = twice
+        all_rows = jnp.concatenate(all_rows, axis=0)
+        for d in range(devices):
+            message[d * 8 : (d + 1) * 8, :] = all_rows
         params[16:, :] = jnp.concatenate([sums[:, 2 * LANE :], jnp.zeros((8 - doms, LANE), F32)], axis=0)
         outs[0].flush()
 
     return staged(
         body,
         [Near(v) for v in (stats, tower, marks, scale, shift, head)],
-        [Near(plain((24, LANE), F32)), Near(plain((devices * 8, LANE), BF16))],
+        [Near(plain((24, LANE), F32)), Near(plain((devices * 8, LANE), F32))],
         [
             pltpu.VMEM((LANE, LANE), F32),
             pltpu.VMEM((4 * doms, LANE, LANE), F32),
@@ -460,7 +478,7 @@
         r = lax.axis_index(ROWS)
         at_row = [spots(kind, r, rows_n) for kind in range(2)]
         prm[...] = jnp.zeros_like(prm)
-        total = jnp.sum(sm.get()[...].astype(F32).reshape(devices, 8, LANE), axis=0)
+        total = jnp.sum(sm.get()[...].reshape(devices, 8, LANE), axis=0)
         shift_out.buf[...] = total[:doms]
         scale_out.buf[...] = total[doms : 2 * doms]
         loss_out.buf[...] = jnp.sum(total[2 * doms : 2 * doms + 1, :], axis=1, keepdims=True) * (1.0 / count)
@@ -485,12 +503,17 @@
                 pair = tw[t_rows : t_rows + 16, here].astype(F32)
                 dom = pair[0:1].astype(jnp.int32)
                 target = pair[1:2]
-            values, _, affine, gain_s, head_w = chosen_tower(tw, dom, wide, here, doms)
+            values = [tw[k * LANE : (k + 1) * LANE, here] for k in range(doms)]
+            if n:
+                if here.start == 0:
+                    added = [jnp.broadcast_to(base(v), (LANE, LANE)) for v in values]
+                values = [decode(v, a, here.start) for v, a in zip(values, added)]
+            _, affine, gain_s, head_w = chosen_tower(values, dom, wide, doms)
             s = sigmoid(affine)
-            a = affine * s
-            chosen = jnp.sum(a * head_w, axis=0, keepdims=True)
+            act = affine * s
+            chosen = jnp.sum(act * head_w, axis=0, keepdims=True)
             score_grad = (sigmoid(chosen) - target) * (1.0 / count)
-            grad = gain_s * (score_grad * head_w * (s + a * (1.0 - s)))
+            grad = gain_s * (score_grad * head_w * (s + act * (1.0 - s)))
             for k in range(doms):
                 v = jnp.where(dom == k, grad, 0.0) - wide[4 * doms + k]
                 v = v - (values[k] - wide[k]) * wide[5 * doms + k]
@@ -565,7 +588,7 @@
                     for off in range(0, hid_n, step):
                         j, o = divmod(flat + off, size)
                         part = values[off : off + step, q * LANE : (q + 1) * LANE]
-                        target.buf[at_row[kind][j], o : o + step, :] = part.astype(BF16)
+                        target.buf[at_row[kind][j], o : o + step, :] = part.astype(target.buf.dtype)
 
         x = xs.get()
         facc[...] = mm(pg[...], x[...])
@@ -587,7 +610,7 @@
         for target, core in ((tow_sib, 1 - c), (tow_mine, c)):
             for j in range(rows_n):
                 start = pl.multiple_of((core * rows_n + j) * m_tow, 8)
-                target.buf[at_row[1][j], :, :] = tgf[pl.ds(start, m_tow), :].astype(BF16)
+                target.buf[at_row[1][j], :, :] = tgf[pl.ds(start, m_tow), :].astype(target.buf.dtype)
             target.flush()
 
     outs = [
@@ -596,10 +619,10 @@
         plain((1, 1), F32),
         Near(plain((rows_n, m_sec, LANE), BF16)),
         Near(plain((rows_n, m_first, LANE), BF16)),
-        Near(plain((rows_n, m_sec, LANE), BF16)),
-        Near(plain((rows_n, m_first, LANE), BF16)),
+        Near(plain((rows_n, m_sec, LANE), F32)),
+        Near(plain((rows_n, m_first, LANE), F32)),
         Near(plain((rows_n, m_tow, LANE), BF16)),
-        Near(plain((rows_n, m_tow, LANE), BF16)),
+        Near(plain((rows_n, m_tow, LANE), F32)),
         Near(plain((ce * hid_n, total_n), BF16)),
         Near(plain((ke, total_n), BF16)),
         Near(plain((dim, ce * hid_n), BF16)),

time: 97.8 us -> 98.9 us (1.011)
  transfers between devices with their start and end apart: 26 -> 26, of which waited for: 11 -> 12; matrix products, arithmetic and copies ran while one was open for 0% -> 0% of each run, Pallas kernels for 16% -> 16%
where the time goes in v2:
time: 98.9 us; the launch traced here: 98.7 us
  Pallas kernels  29.8 us (30%)
  starting transfers between devices  28.2 us (29%)
  blocking collectives  25 us (25%)
  waiting for transfers between devices  14 us (14%)
  between operations  1.09 us (1%)
    pallas_call x9, Pallas kernels, staged(): pl.pallas_call(kernel, out_shape=[o.what if isinstance(o, Near) else pltp...  29.8 us
    ppermute x26, starting transfers between devices, swap(): return lax.ppermute(value, axis, [(i, i ^ mask) for i in range(size)])  28.2 us
    all_to_all x1, blocking collectives, local(): stats = lax.all_to_all(message, BOTH, 0, 0, tiled=True)  14.1 us
    ppermute x26, waiting for transfers between devices, swap(): return lax.ppermute(value, axis, [(i, i ^ mask) for i in range(size)])  14 us
    all_to_all x1, blocking collectives, local(): sums = lax.all_to_all(message, BOTH, 0, 0, tiled=True)  10.9 us
  transfers between devices with their start and end apart: 26, of which 12 were waited for; matrix products, arithmetic and copies ran while one was open for 0% of the time, Pallas kernels for 16%

profile of v2, /device:TPU:0, one launch (start us, length us, event | category | flops | bytes accessed | tf_op | source)
XLA Modules:
  0.0 98.7 jit_solution(13078857170141459811)
XLA Ops:
  0.6 0.5 collective-permute-start
  1.2 0.1 collective-permute-start.1
  1.2 2.2 %prepare.1 = (bf16[512,512]{1,0:T(8,128)(2,1)S(1)}, bf16[536,512]{1,0:T(8,128)(2,1)S(1)}, bf16[2,256,256]{2,1,0:T(8,128)(2,1)S(1)}, bf16[3,128,256]{2,1,0:T(8,128)(2,1)S(1)}) custom-call(bf16[2,512,256]{2,1,0:T(8,128)(2,1)} %refs_19_.1, bf16[24,512]{1,0:T(8,128)(2,1)} %bitcast.38, bf16[2,256,256]{2,1,0:T(8,128)(2,1)} %refs_10_.1, ...), custom_call_target="tpu_custom_call" | custom-call | tf_op jit(solution)/shard_map/prepare/pallas_call | solution.py:139
  3.5 2.6 %forward_send.1 = bf16[1,384,512]{2,1,0:T(8,128)(2,1)S(1)} custom-call(bf16[512,512]{1,0:T(8,128)(2,1)S(1)} %get-tuple-element.79.refs_1_.refs_0_, bf16[536,512]{1,0:T(8,128)(2,1)S(1)} %get-tuple-element.80.refs_2_.refs_1_, bf16[2,512,256]{2,1,0:T(8,128)(2,1)S(1)} %collective-permute-done.refs_3_.refs_2_.refs_20_, ...), custom_call_target="tpu_custom_call" | custom-call | tf_op jit(solution)/shard_map/forward_send/pallas_call | solution.py:139
  6.0 3.0 %collective-permute-start.2 = (bf16[1,384,512]{2,1,0:T(8,128)(2,1)S(1)}, bf16[1,384,512]{2,1,0:T(8,128)(2,1)S(1)}, u32[]{:S(2)}, u32[]{:S(2)}) collective-permute-start(bf16[1,384,512]{2,1,0:T(8,128)(2,1)S(1)} %forward_send.1), channel_id=1, source_target_pairs={{0,2},{1,3},{2,0},{3,1},{4,6},{5,7},{6,4},{7,5},{8,10},{9,11},{10,... | collective-permute-start | bytes 1179656 | tf_op jit(solution)/shard_map/ppermute | solution.py:765
  9.1 8.2 %forward_keep.1 = (bf16[2,1024,512]{2,1,0:T(8,128)(2,1)}, bf16[2,1024,512]{2,1,0:T(8,128)(2,1)}, bf16[2,1024,512]{2,1,0:T(8,128)(2,1)}, f32[2,24,512]{2,1,0:T(8,...) custom-call(bf16[2048,512]{1,0:T(8,128)(2,1)} %refs_14_.1, ...), custom_call_target="tpu_custom_call" | custom-call | tf_op jit(solution)/shard_map/forward_keep/pallas_call | solution.py:139
  17.3 1.1 %collective-permute-done.2.refs_2_ = bf16[1,384,512]{2,1,0:T(8,128)(2,1)S(1)} collective-permute-done((bf16[1,384,512]{2,1,0:T(8,128)(2,1)S(1)}, bf16[1,384,512]{2,1,0:T(8,128)(2,1)S(1)}, u32[]{:S(2)}, u32[]{:S(2)}) %collective-permute-start.2) | collective-permute-done | bytes 393248 | tf_op jit(solution)/shard_map/ppermute | solution.py:765
  18.4 1.1 %combine.1 = (f32[384,512]{1,0:T(8,128)S(1)}, bf16[400,512]{1,0:T(8,128)(2,1)S(1)}, f32[256,128]{1,0:T(8,128)S(1)}) custom-call(f32[1,384,512]{2,1,0:T(8,128)S(1)} %get-tuple-element.83.refs_0_, s32[2,512]{1,0:T(2,128)S(1)} %pad_add_fusion.refs_1_.refs_2_.refs_3_, bf16[1,384,512]{2,1,0:T(8,128)(2,1)S(1)} %collective-permute-done.2.refs_2_), custom_call_target="tpu_custom_call" | custom-call | tf_op jit(solution)/shard_map/combine/pallas_call | solution.py:139
  19.4 14.1 %all_to_all.23 = f32[32,8,128]{2,1,0:T(8,128)S(1)} all-to-all(f32[32,8,128]{2,1,0:T(8,128)S(1)} %bitcast.36), channel_id=1, replica_groups=mesh['rows'=8,'width'=4] {'rows','width'}, dimensions={0} | all-to-all | bytes 262144 | tf_op jit(solution)/shard_map/all_to_all | solution.py:847
  33.6 0.4 collective-permute-start.3
  34.0 1.5 %normalise.1 = (f32[24,128]{1,0:T(8,128)S(1)}, f32[256,128]{1,0:T(8,128)S(1)}) custom-call(f32[256,128]{1,0:T(8,128)S(1)} %bitcast.35, f32[384,512]{1,0:T(8,128)S(1)} %get-tuple-element.87.refs_1_.refs_2_, s32[2,512]{1,0:T(2,128)S(1)} %pad_add_fusion.refs_1_.refs_2_.refs_3_, f32[3,128]{1,0:T(4,128)S(1)} %copy-done.1, f32[3,128]{1,0:T(4,128)S(1)} %copy-done.2, ...), custom_call_target="tpu_custom_call" | custom-call | tf_op jit(solution)/shard_map/normalise/pallas_call | solution.py:139
  35.6 10.9 %all_to_all.24 = f32[32,8,128]{2,1,0:T(8,128)S(1)} all-to-all(f32[32,8,128]{2,1,0:T(8,128)S(1)} %bitcast.37), channel_id=1, replica_groups=mesh['rows'=8,'width'=4] {'rows','width'}, dimensions={0} | all-to-all | bytes 262144 | tf_op jit(solution)/shard_map/all_to_all | solution.py:851
  46.4 8.5 %backward.1 = (f32[3,128]{1,0:T(4,128)}, f32[3,128]{1,0:T(4,128)}, f32[1,1]{1,0:T(1,128)}, bf16[8,128,128]{2,1,0:T(8,128)(2,1)S(1)}, bf16[8,256,128]{2,1,0:T(8,1...) custom-call(f32[256,128]{1,0:T(8,128)S(1)} %bitcast.34, ...), custom_call_target="tpu_custom_call" | custom-call | tf_op jit(solution)/shard_map/backward/pallas_call | solution.py:139
  55.0 0.3 collective-permute-start.4
  55.2 1.7 %collective-permute-done.4 = bf16[8,256,128]{2,1,0:T(8,128)(2,1)S(1)} collective-permute-done((bf16[8,256,128]{2,1,0:T(8,128)(2,1)S(1)}, bf16[8,256,128]{2,1,0:T(8,128)(2,1)S(1)}, u32[]{:S(2)}, u32[]{:S(2)}) %collective-permute-start.4) | collective-permute-done | bytes 524320 | tf_op jit(solution)/shard_map/ppermute | solution.py:765
  56.9 0.2 collective-permute-start.10
  57.1 0.3 collective-permute-start.5
  57.5 1.6 %collective-permute-start.6 = (bf16[4,256,128]{2,1,0:T(8,128)(2,1)S(1)}, bf16[4,256,128]{2,1,0:T(8,128)(2,1)S(1)}, u32[]{:S(2)}, u32[]{:S(2)}) collective-permute-start(bf16[4,256,128]{2,1,0:T(8,128)(2,1)S(1)} %add_convert_fusion), channel_id=1, source_target_pairs={{0,4},{4,0},{8,12},{12,8},{16,20},{20,16},{24,28},{28,24},{1,5},{5... | collective-permute-start | bytes 786440 | tf_op jit(solution)/shard_map/ppermute | solution.py:765
  59.1 0.4 collective-permute-start.11
  59.5 1.4 %collective-permute-start.9 = (bf16[2,128,128]{2,1,0:T(8,128)(2,1)S(1)}, bf16[2,128,128]{2,1,0:T(8,128)(2,1)S(1)}, u32[]{:S(2)}, u32[]{:S(2)}) collective-permute-start(bf16[2,128,128]{2,1,0:T(8,128)(2,1)S(1)} %get-tuple-element.153), channel_id=1, source_target_pairs={{0,24},{4,28},{8,16},{12,20},{16,8},{20,12},{24,0},{28,4},{1,25},{... | collective-permute-start | bytes 196616 | tf_op jit(solution)/shard_map/ppermute | solution.py:765
  60.9 0.9 collective-permute-start.8
  61.8 2.2 %collective-permute-start.7 = (bf16[2,128,128]{2,1,0:T(8,128)(2,1)S(1)}, bf16[2,128,128]{2,1,0:T(8,128)(2,1)S(1)}, u32[]{:S(2)}, u32[]{:S(2)}) collective-permute-start(bf16[2,128,128]{2,1,0:T(8,128)(2,1)S(1)} %get-tuple-element.155), channel_id=1, source_target_pairs={{0,8},{4,12},{8,0},{12,4},{16,24},{20,28},{24,16},{28,20},{1,9},{5... | collective-permute-start | bytes 196616 | tf_op jit(solution)/shard_map/ppermute | solution.py:765
  64.0 0.5 collective-permute-done.11
  64.5 1.1 %collective-permute-start.12 = (bf16[4,64,128]{2,1,0:T(8,128)(2,1)S(1)}, bf16[4,64,128]{2,1,0:T(8,128)(2,1)S(1)}, u32[]{:S(2)}, u32[]{:S(2)}) collective-permute-start(bf16[4,64,128]{2,1,0:T(8,128)(2,1)S(1)} %slice.198), channel_id=1, source_target_pairs={{0,4},{4,0},{8,12},{12,8},{16,20},{20,16},{24,28},{28,24},{1,5},{5... | collective-permute-start | bytes 196616 | tf_op jit(solution)/shard_map/ppermute | solution.py:765
  65.6 2.1 %backward_inputs.1 = (f32[512,512]{1,0:T(8,128)S(1)}, bf16[1,512,512]{2,1,0:T(8,128)(2,1)S(1)}) custom-call(bf16[512,1024]{1,0:T(8,128)(2,1)S(1)} %get-tuple-element.108.refs_0_, bf16[24,512]{1,0:T(8,128)(2,1)S(1)} %bitcast.39, bf16[1024,1024]{1,0:T(8,128)(2,1)S(1)} %get-tuple-element.109.refs_2_, bf16[24,1024]{1,0:T(8,128)(2,1)S(1)} %get-tuple-element.110.refs_3_), custom_call_target="tpu_custom_call" | custom-call | tf_op jit(solution)/shard_map/backward_inputs/pallas_call | solution.py:139
  67.7 0.5 collective-permute-done.8
  68.2 0.6 collective-permute-done.12
  68.9 0.1 add_bitcast_fusion
  69.1 0.2 collective-permute-start.13
  69.3 1.3 %collective-permute-start.14 = (bf16[320,128]{1,0:T(8,128)(2,1)S(1)}, bf16[320,128]{1,0:T(8,128)(2,1)S(1)}, u32[]{:S(2)}, u32[]{:S(2)}) collective-permute-start(bf16[320,128]{1,0:T(8,128)(2,1)S(1)} %get-tuple-element.119), channel_id=1, source_target_pairs={{0,16},{4,20},{8,24},{12,28},{16,0},{20,4},{24,8},{28,12},{1,17},{... | collective-permute-start | bytes 245768 | tf_op jit(solution)/shard_map/ppermute | solution.py:765
  70.6 2.9 %collective-permute-start.15 = (bf16[320,128]{1,0:T(8,128)(2,1)S(1)}, bf16[320,128]{1,0:T(8,128)(2,1)S(1)}, u32[]{:S(2)}, u32[]{:S(2)}) collective-permute-start(bf16[320,128]{1,0:T(8,128)(2,1)S(1)} %pad_maximum_fusion.4), channel_id=1, source_target_pairs={{0,24},{4,28},{8,16},{12,20},{16,8},{20,12},{24,0},{28,4},{1,25},{... | collective-permute-start | bytes 245768 | tf_op jit(solution)/shard_map/ppermute | solution.py:765
  73.5 1.0 %collective-permute-start.16 = (bf16[2,128,128]{2,1,0:T(8,128)(2,1)S(1)}, bf16[2,128,128]{2,1,0:T(8,128)(2,1)S(1)}, u32[]{:S(2)}, u32[]{:S(2)}) collective-permute-start(bf16[2,128,128]{2,1,0:T(8,128)(2,1)S(1)} %fusion.14), channel_id=1, source_target_pairs={{0,4},{4,0},{8,12},{12,8},{16,20},{20,16},{24,28},{28,24},{1,5},{5... | collective-permute-start | bytes 196616 | tf_op jit(solution)/shard_map/ppermute | solution.py:765
  74.5 1.0 collective-permute-start.20
  75.5 2.3 %collective-permute-done.16 = bf16[2,128,128]{2,1,0:T(8,128)(2,1)S(1)} collective-permute-done((bf16[2,128,128]{2,1,0:T(8,128)(2,1)S(1)}, bf16[2,128,128]{2,1,0:T(8,128)(2,1)S(1)}, u32[]{:S(2)}, u32[]{:S(2)}) %collective-permute-start.16) | collective-permute-done | bytes 65568 | tf_op jit(solution)/shard_map/ppermute | solution.py:765
  77.8 0.1 collective-permute-done.14
  78.0 2.0 %collective-permute-start.19 = (bf16[320,128]{1,0:T(8,128)(2,1)S(1)}, bf16[320,128]{1,0:T(8,128)(2,1)S(1)}, u32[]{:S(2)}, u32[]{:S(2)}) collective-permute-start(bf16[320,128]{1,0:T(8,128)(2,1)S(1)} %fusion.3), channel_id=1, source_target_pairs={{0,24},{4,28},{8,16},{12,20},{16,8},{20,12},{24,0},{28,4},{1,25},{... | collective-permute-start | bytes 245768 | tf_op jit(solution)/shard_map/ppermute | solution.py:765
  80.0 1.0 collective-permute-start.18
  81.0 1.5 %collective-permute-start.17 = (bf16[320,128]{1,0:T(8,128)(2,1)S(1)}, bf16[320,128]{1,0:T(8,128)(2,1)S(1)}, u32[]{:S(2)}, u32[]{:S(2)}) collective-permute-start(bf16[320,128]{1,0:T(8,128)(2,1)S(1)} %fusion.3), channel_id=1, source_target_pairs={{0,8},{4,12},{8,0},{12,4},{16,24},{20,28},{24,16},{28,20},{1,9},{5... | collective-permute-start | bytes 245768 | tf_op jit(solution)/shard_map/ppermute | solution.py:765
  82.5 2.0 %collective-permute-done.19 = bf16[320,128]{1,0:T(8,128)(2,1)S(1)} collective-permute-done((bf16[320,128]{1,0:T(8,128)(2,1)S(1)}, bf16[320,128]{1,0:T(8,128)(2,1)S(1)}, u32[]{:S(2)}, u32[]{:S(2)}) %collective-permute-start.19) | collective-permute-done | bytes 81952 | tf_op jit(solution)/shard_map/ppermute | solution.py:765
  84.4 2.4 %collective-permute-done.18 = bf16[320,128]{1,0:T(8,128)(2,1)S(1)} collective-permute-done((bf16[320,128]{1,0:T(8,128)(2,1)S(1)}, bf16[320,128]{1,0:T(8,128)(2,1)S(1)}, u32[]{:S(2)}, u32[]{:S(2)}) %collective-permute-start.18) | collective-permute-done | bytes 81952 | tf_op jit(solution)/shard_map/ppermute | solution.py:765
  86.8 0.6 collective-permute-start.21
  87.4 2.2 %collective-permute-start.24 = (bf16[2,128,128]{2,1,0:T(8,128)(2,1)S(1)}, bf16[2,128,128]{2,1,0:T(8,128)(2,1)S(1)}, u32[]{:S(2)}, u32[]{:S(2)}) collective-permute-start(bf16[2,128,128]{2,1,0:T(8,128)(2,1)S(1)} %add_convert_fusion.1), channel_id=1, source_target_pairs={{0,24},{4,28},{8,16},{12,20},{16,8},{20,12},{24,0},{28,4},{1,25},{... | collective-permute-start | bytes 196616 | tf_op jit(solution)/shard_map/ppermute | solution.py:765
  89.6 2.2 %collective-permute-start.22 = (bf16[2,128,128]{2,1,0:T(8,128)(2,1)S(1)}, bf16[2,128,128]{2,1,0:T(8,128)(2,1)S(1)}, u32[]{:S(2)}, u32[]{:S(2)}) collective-permute-start(bf16[2,128,128]{2,1,0:T(8,128)(2,1)S(1)} %add_convert_fusion.1), channel_id=1, source_target_pairs={{0,8},{4,12},{8,0},{12,4},{16,24},{20,28},{24,16},{28,20},{1,9},{5... | collective-permute-start | bytes 196616 | tf_op jit(solution)/shard_map/ppermute | solution.py:765
  91.8 1.7 %finish_inputs.1 = f32[512,512]{1,0:T(8,128)} custom-call(f32[512,512]{1,0:T(8,128)S(1)} %get-tuple-element.135.refs_0_, bf16[512,512]{1,0:T(8,128)(2,1)S(1)} %collective-permute-done.20.refs_1_), custom_call_target="tpu_custom_call" | custom-call | tf_op jit(solution)/shard_map/finish_inputs/pallas_call | solution.py:139
  93.5 0.2 collective-permute-done.24
  93.8 1.4 %collective-permute-done.23 = bf16[2,128,128]{2,1,0:T(8,128)(2,1)S(1)} collective-permute-done((bf16[2,128,128]{2,1,0:T(8,128)(2,1)S(1)}, bf16[2,128,128]{2,1,0:T(8,128)(2,1)S(1)}, u32[]{:S(2)}, u32[]{:S(2)}) %collective-permute-start.23) | collective-permute-done | bytes 65568 | tf_op jit(solution)/shard_map/ppermute | solution.py:765
  95.3 1.3 %collective-permute-done.25.refs_2_ = bf16[8,64,128]{2,1,0:T(8,128)(2,1)S(1)} collective-permute-done((bf16[8,64,128]{2,1,0:T(8,128)(2,1)S(1)}, bf16[8,64,128]{2,1,0:T(8,128)(2,1)S(1)}, u32[]{:S(2)}, u32[]{:S(2)}) %collective-permute-start.25) | collective-permute-done | bytes 131104 | tf_op jit(solution)/shard_map/ppermute | solution.py:765
  96.6 2.0 %finish_weights.1 = (f32[2,512,256]{2,1,0:T(8,128)}, f32[2,256,256]{2,1,0:T(8,128)}, f32[3,256,128]{2,1,0:T(8,128)}, f32[24,512]{1,0:T(8,128)}, f32[3,128]{1,0:T(4,128)}) custom-call(bf16[8,128,128]{2,1,0:T(8,128)(2,1)S(1)} %pad_maximum_fusion.1.refs_0_, bf16[8,320,128]{2,1,0:T(8,128)(2,1)S(1)} %constant_dynamic-update-slice_fusion.refs_1_, ...), custom_call_target="tpu_custom_call" | custom-call | tf_op jit(solution)/shard_map/finish_weights/pallas_call | solution.py:139
  (45 shorter events, 0.7 us)
Async XLA Ops:
  0.6 2.8 %collective-permute-start = (bf16[2,512,256]{2,1,0:T(8,128)(2,1)}, bf16[2,512,256]{2,1,0:T(8,128)(2,1)S(1)}, u32[]{:S(2)}, u32[]{:S(2)}) collective-permute-start(bf16[2,512,256]{2,1,0:T(8,128)(2,1)} %refs_19_.1), channel_id=1, source_target_pairs={{0,1},{1,0},{2,3},{3,2},{4,5},{5,4},{6,7},{7,6},{8,9},{9,8},{10,11... | collective-permute-start | bytes 1572872 | tf_op jit(solution)/shard_map/ppermute | solution.py:765
  1.2 2.3 %collective-permute-start.1 = (bf16[2,256,256]{2,1,0:T(8,128)(2,1)}, bf16[2,256,256]{2,1,0:T(8,128)(2,1)S(1)}, u32[]{:S(2)}, u32[]{:S(2)}) collective-permute-start(bf16[2,256,256]{2,1,0:T(8,128)(2,1)} %refs_10_.1), channel_id=1, source_target_pairs={{0,1},{1,0},{2,3},{3,2},{4,5},{5,4},{6,7},{7,6},{8,9},{9,8},{10,11... | collective-permute-start | bytes 786440 | tf_op jit(solution)/shard_map/ppermute | solution.py:765
  3.4 5.6 %copy-start.4 = (s32[512]{0:T(512)S(1)}, s32[512]{0:T(512)}, u32[]{:S(2)}) copy-start(s32[512]{0:T(512)} %param.19) | copy-start | bytes 6148
  3.4 5.6 %copy-start.5 = (s32[512]{0:T(512)S(1)}, s32[512]{0:T(512)}, u32[]{:S(2)}) copy-start(s32[512]{0:T(512)} %param.18) | copy-start | bytes 6148
  6.0 12.3 %collective-permute-start.2 = (bf16[1,384,512]{2,1,0:T(8,128)(2,1)S(1)}, bf16[1,384,512]{2,1,0:T(8,128)(2,1)S(1)}, u32[]{:S(2)}, u32[]{:S(2)}) collective-permute-start(bf16[1,384,512]{2,1,0:T(8,128)(2,1)S(1)} %forward_send.1), channel_id=1, source_target_pairs={{0,2},{1,3},{2,0},{3,1},{4,6},{5,7},{6,4},{7,5},{8,10},{9,11},{10,... | collective-permute-start | bytes 1179656 | tf_op jit(solution)/shard_map/ppermute | solution.py:765
  9.0 25.0 %copy-start.1 = (f32[3,128]{1,0:T(4,128)S(1)}, f32[3,128]{1,0:T(4,128)}, u32[]{:S(2)}) copy-start(f32[3,128]{1,0:T(4,128)} %refs_3_.3) | copy-start | bytes 4612
  9.0 25.0 %copy-start.2 = (f32[3,128]{1,0:T(4,128)S(1)}, f32[3,128]{1,0:T(4,128)}, u32[]{:S(2)}) copy-start(f32[3,128]{1,0:T(4,128)} %refs_4_.3) | copy-start | bytes 4612
  9.1 25.0 %copy-start.3 = (f32[3,128]{1,0:T(4,128)S(1)}, f32[3,128]{1,0:T(4,128)}, u32[]{:S(2)}) copy-start(f32[3,128]{1,0:T(4,128)} %refs_5_.2) | copy-start | bytes 4612
  33.6 12.9 %collective-permute-start.3 = (bf16[400,512]{1,0:T(8,128)(2,1)S(1)}, bf16[400,512]{1,0:T(8,128)(2,1)S(1)}, u32[]{:S(2)}, u32[]{:S(2)}) collective-permute-start(bf16[400,512]{1,0:T(8,128)(2,1)S(1)} %get-tuple-element.90), channel_id=1, source_target_pairs={{0,2},{1,3},{2,0},{3,1},{4,6},{5,7},{6,4},{7,5},{8,10},{9,11},{10,... | collective-permute-start | bytes 1228808 | tf_op jit(solution)/shard_map/ppermute | solution.py:765
  55.0 10.6 %copy-start = (bf16[3,512,8]{1,2,0:T(8,128)(2,1)S(1)}, bf16[3,512,8]{1,2,0:T(8,128)(2,1)}, u32[]{:S(2)}) copy-start(bf16[3,512,8]{1,2,0:T(8,128)(2,1)} %param.13) | copy-start | bytes 73732
  55.0 2.0 %collective-permute-start.4 = (bf16[8,256,128]{2,1,0:T(8,128)(2,1)S(1)}, bf16[8,256,128]{2,1,0:T(8,128)(2,1)S(1)}, u32[]{:S(2)}, u32[]{:S(2)}) collective-permute-start(bf16[8,256,128]{2,1,0:T(8,128)(2,1)S(1)} %get-tuple-element.98), channel_id=1, source_target_pairs={{0,1},{1,0},{2,3},{3,2},{4,5},{5,4},{6,7},{7,6},{8,9},{9,8},{10,11... | collective-permute-start | bytes 1572872 | tf_op jit(solution)/shard_map/ppermute | solution.py:765
  56.9 2.2 %collective-permute-start.10 = (bf16[8,64,128]{2,1,0:T(8,128)(2,1)S(1)}, bf16[8,64,128]{2,1,0:T(8,128)(2,1)S(1)}, u32[]{:S(2)}, u32[]{:S(2)}) collective-permute-start(bf16[8,64,128]{2,1,0:T(8,128)(2,1)S(1)} %get-tuple-element.105), channel_id=1, source_target_pairs={{0,1},{1,0},{2,3},{3,2},{4,5},{5,4},{6,7},{7,6},{8,9},{9,8},{10,11... | collective-permute-start | bytes 393224 | tf_op jit(solution)/shard_map/ppermute | solution.py:765
  57.1 2.4 %collective-permute-start.5 = (bf16[8,128,128]{2,1,0:T(8,128)(2,1)S(1)}, bf16[8,128,128]{2,1,0:T(8,128)(2,1)S(1)}, u32[]{:S(2)}, u32[]{:S(2)}) collective-permute-start(bf16[8,128,128]{2,1,0:T(8,128)(2,1)S(1)} %get-tuple-element.101), channel_id=1, source_target_pairs={{0,1},{1,0},{2,3},{3,2},{4,5},{5,4},{6,7},{7,6},{8,9},{9,8},{10,11... | collective-permute-start | bytes 786440 | tf_op jit(solution)/shard_map/ppermute | solution.py:765
  57.5 10.2 %collective-permute-start.6 = (bf16[4,256,128]{2,1,0:T(8,128)(2,1)S(1)}, bf16[4,256,128]{2,1,0:T(8,128)(2,1)S(1)}, u32[]{:S(2)}, u32[]{:S(2)}) collective-permute-start(bf16[4,256,128]{2,1,0:T(8,128)(2,1)S(1)} %add_convert_fusion), channel_id=1, source_target_pairs={{0,4},{4,0},{8,12},{12,8},{16,20},{20,16},{24,28},{28,24},{1,5},{5... | collective-permute-start | bytes 786440 | tf_op jit(solution)/shard_map/ppermute | solution.py:765
  59.1 5.3 %collective-permute-start.11 = (bf16[8,64,128]{2,1,0:T(8,128)(2,1)S(1)}, bf16[8,64,128]{2,1,0:T(8,128)(2,1)S(1)}, u32[]{:S(2)}, u32[]{:S(2)}) collective-permute-start(bf16[8,64,128]{2,1,0:T(8,128)(2,1)S(1)} %fusion), channel_id=1, source_target_pairs={{0,2},{1,3},{2,0},{3,1},{4,6},{5,7},{6,4},{7,5},{8,10},{9,11},{10,... | collective-permute-start | bytes 393224 | tf_op jit(solution)/shard_map/ppermute | solution.py:765
  59.5 8.2 %collective-permute-start.9 = (bf16[2,128,128]{2,1,0:T(8,128)(2,1)S(1)}, bf16[2,128,128]{2,1,0:T(8,128)(2,1)S(1)}, u32[]{:S(2)}, u32[]{:S(2)}) collective-permute-start(bf16[2,128,128]{2,1,0:T(8,128)(2,1)S(1)} %get-tuple-element.153), channel_id=1, source_target_pairs={{0,24},{4,28},{8,16},{12,20},{16,8},{20,12},{24,0},{28,4},{1,25},{... | collective-permute-start | bytes 196616 | tf_op jit(solution)/shard_map/ppermute | solution.py:765
  60.9 7.3 %collective-permute-start.8 = (bf16[2,128,128]{2,1,0:T(8,128)(2,1)S(1)}, bf16[2,128,128]{2,1,0:T(8,128)(2,1)S(1)}, u32[]{:S(2)}, u32[]{:S(2)}) collective-permute-start(bf16[2,128,128]{2,1,0:T(8,128)(2,1)S(1)} %get-tuple-element.154), channel_id=1, source_target_pairs={{0,16},{4,20},{8,24},{12,28},{16,0},{20,4},{24,8},{28,12},{1,17},{... | collective-permute-start | bytes 196616 | tf_op jit(solution)/shard_map/ppermute | solution.py:765
  61.8 6.5 %collective-permute-start.7 = (bf16[2,128,128]{2,1,0:T(8,128)(2,1)S(1)}, bf16[2,128,128]{2,1,0:T(8,128)(2,1)S(1)}, u32[]{:S(2)}, u32[]{:S(2)}) collective-permute-start(bf16[2,128,128]{2,1,0:T(8,128)(2,1)S(1)} %get-tuple-element.155), channel_id=1, source_target_pairs={{0,8},{4,12},{8,0},{12,4},{16,24},{20,28},{24,16},{28,20},{1,9},{5... | collective-permute-start | bytes 196616 | tf_op jit(solution)/shard_map/ppermute | solution.py:765
  64.5 4.3 %collective-permute-start.12 = (bf16[4,64,128]{2,1,0:T(8,128)(2,1)S(1)}, bf16[4,64,128]{2,1,0:T(8,128)(2,1)S(1)}, u32[]{:S(2)}, u32[]{:S(2)}) collective-permute-start(bf16[4,64,128]{2,1,0:T(8,128)(2,1)S(1)} %slice.198), channel_id=1, source_target_pairs={{0,4},{4,0},{8,12},{12,8},{16,20},{20,16},{24,28},{28,24},{1,5},{5... | collective-permute-start | bytes 196616 | tf_op jit(solution)/shard_map/ppermute | solution.py:765
  69.1 8.7 %collective-permute-start.13 = (bf16[320,128]{1,0:T(8,128)(2,1)S(1)}, bf16[320,128]{1,0:T(8,128)(2,1)S(1)}, u32[]{:S(2)}, u32[]{:S(2)}) collective-permute-start(bf16[320,128]{1,0:T(8,128)(2,1)S(1)} %get-tuple-element.118), channel_id=1, source_target_pairs={{0,8},{4,12},{8,0},{12,4},{16,24},{20,28},{24,16},{28,20},{1,9},{5... | collective-permute-start | bytes 245768 | tf_op jit(solution)/shard_map/ppermute | solution.py:765
  69.3 8.6 %collective-permute-start.14 = (bf16[320,128]{1,0:T(8,128)(2,1)S(1)}, bf16[320,128]{1,0:T(8,128)(2,1)S(1)}, u32[]{:S(2)}, u32[]{:S(2)}) collective-permute-start(bf16[320,128]{1,0:T(8,128)(2,1)S(1)} %get-tuple-element.119), channel_id=1, source_target_pairs={{0,16},{4,20},{8,24},{12,28},{16,0},{20,4},{24,8},{28,12},{1,17},{... | collective-permute-start | bytes 245768 | tf_op jit(solution)/shard_map/ppermute | solution.py:765
  70.6 7.3 %collective-permute-start.15 = (bf16[320,128]{1,0:T(8,128)(2,1)S(1)}, bf16[320,128]{1,0:T(8,128)(2,1)S(1)}, u32[]{:S(2)}, u32[]{:S(2)}) collective-permute-start(bf16[320,128]{1,0:T(8,128)(2,1)S(1)} %pad_maximum_fusion.4), channel_id=1, source_target_pairs={{0,24},{4,28},{8,16},{12,20},{16,8},{20,12},{24,0},{28,4},{1,25},{... | collective-permute-start | bytes 245768 | tf_op jit(solution)/shard_map/ppermute | solution.py:765
  73.5 4.3 %collective-permute-start.16 = (bf16[2,128,128]{2,1,0:T(8,128)(2,1)S(1)}, bf16[2,128,128]{2,1,0:T(8,128)(2,1)S(1)}, u32[]{:S(2)}, u32[]{:S(2)}) collective-permute-start(bf16[2,128,128]{2,1,0:T(8,128)(2,1)S(1)} %fusion.14), channel_id=1, source_target_pairs={{0,4},{4,0},{8,12},{12,8},{16,20},{20,16},{24,28},{28,24},{1,5},{5... | collective-permute-start | bytes 196616 | tf_op jit(solution)/shard_map/ppermute | solution.py:765
  74.5 12.3 %collective-permute-start.20 = (bf16[512,512]{1,0:T(8,128)(2,1)S(1)}, bf16[512,512]{1,0:T(8,128)(2,1)S(1)}, u32[]{:S(2)}, u32[]{:S(2)}) collective-permute-start(bf16[512,512]{1,0:T(8,128)(2,1)S(1)} %bitcast.40), channel_id=1, source_target_pairs={{0,2},{1,3},{2,0},{3,1},{4,6},{5,7},{6,4},{7,5},{8,10},{9,11},{10,... | collective-permute-start | bytes 1572872 | tf_op jit(solution)/shard_map/ppermute | solution.py:765
  78.0 6.4 %collective-permute-start.19 = (bf16[320,128]{1,0:T(8,128)(2,1)S(1)}, bf16[320,128]{1,0:T(8,128)(2,1)S(1)}, u32[]{:S(2)}, u32[]{:S(2)}) collective-permute-start(bf16[320,128]{1,0:T(8,128)(2,1)S(1)} %fusion.3), channel_id=1, source_target_pairs={{0,24},{4,28},{8,16},{12,20},{16,8},{20,12},{24,0},{28,4},{1,25},{... | collective-permute-start | bytes 245768 | tf_op jit(solution)/shard_map/ppermute | solution.py:765
  80.0 6.8 %collective-permute-start.18 = (bf16[320,128]{1,0:T(8,128)(2,1)S(1)}, bf16[320,128]{1,0:T(8,128)(2,1)S(1)}, u32[]{:S(2)}, u32[]{:S(2)}) collective-permute-start(bf16[320,128]{1,0:T(8,128)(2,1)S(1)} %fusion.3), channel_id=1, source_target_pairs={{0,16},{4,20},{8,24},{12,28},{16,0},{20,4},{24,8},{28,12},{1,17},{... | collective-permute-start | bytes 245768 | tf_op jit(solution)/shard_map/ppermute | solution.py:765
  81.0 5.8 %collective-permute-start.17 = (bf16[320,128]{1,0:T(8,128)(2,1)S(1)}, bf16[320,128]{1,0:T(8,128)(2,1)S(1)}, u32[]{:S(2)}, u32[]{:S(2)}) collective-permute-start(bf16[320,128]{1,0:T(8,128)(2,1)S(1)} %fusion.3), channel_id=1, source_target_pairs={{0,8},{4,12},{8,0},{12,4},{16,24},{20,28},{24,16},{28,20},{1,9},{5... | collective-permute-start | bytes 245768 | tf_op jit(solution)/shard_map/ppermute | solution.py:765
  86.8 8.3 %collective-permute-start.21 = (bf16[4,320,128]{2,1,0:T(8,128)(2,1)S(1)}, bf16[4,320,128]{2,1,0:T(8,128)(2,1)S(1)}, u32[]{:S(2)}, u32[]{:S(2)}) collective-permute-start(bf16[4,320,128]{2,1,0:T(8,128)(2,1)S(1)} %pad_maximum_fusion), channel_id=1, source_target_pairs={{0,4},{4,0},{8,12},{12,8},{16,20},{20,16},{24,28},{28,24},{1,5},{5... | collective-permute-start | bytes 983048 | tf_op jit(solution)/shard_map/ppermute | solution.py:765
  87.4 6.3 %collective-permute-start.24 = (bf16[2,128,128]{2,1,0:T(8,128)(2,1)S(1)}, bf16[2,128,128]{2,1,0:T(8,128)(2,1)S(1)}, u32[]{:S(2)}, u32[]{:S(2)}) collective-permute-start(bf16[2,128,128]{2,1,0:T(8,128)(2,1)S(1)} %add_convert_fusion.1), channel_id=1, source_target_pairs={{0,24},{4,28},{8,16},{12,20},{16,8},{20,12},{24,0},{28,4},{1,25},{... | collective-permute-start | bytes 196616 | tf_op jit(solution)/shard_map/ppermute | solution.py:765
  89.6 5.5 %collective-permute-start.23 = (bf16[2,128,128]{2,1,0:T(8,128)(2,1)S(1)}, bf16[2,128,128]{2,1,0:T(8,128)(2,1)S(1)}, u32[]{:S(2)}, u32[]{:S(2)}) collective-permute-start(bf16[2,128,128]{2,1,0:T(8,128)(2,1)S(1)} %add_convert_fusion.1), channel_id=1, source_target_pairs={{0,16},{4,20},{8,24},{12,28},{16,0},{20,4},{24,8},{28,12},{1,17},{... | collective-permute-start | bytes 196616 | tf_op jit(solution)/shard_map/ppermute | solution.py:765
  89.6 5.5 %collective-permute-start.22 = (bf16[2,128,128]{2,1,0:T(8,128)(2,1)S(1)}, bf16[2,128,128]{2,1,0:T(8,128)(2,1)S(1)}, u32[]{:S(2)}, u32[]{:S(2)}) collective-permute-start(bf16[2,128,128]{2,1,0:T(8,128)(2,1)S(1)} %add_convert_fusion.1), channel_id=1, source_target_pairs={{0,8},{4,12},{8,0},{12,4},{16,24},{20,28},{24,16},{28,20},{1,9},{5... | collective-permute-start | bytes 196616 | tf_op jit(solution)/shard_map/ppermute | solution.py:765
  95.2 1.4 %collective-permute-start.25 = (bf16[8,64,128]{2,1,0:T(8,128)(2,1)S(1)}, bf16[8,64,128]{2,1,0:T(8,128)(2,1)S(1)}, u32[]{:S(2)}, u32[]{:S(2)}) collective-permute-start(bf16[8,64,128]{2,1,0:T(8,128)(2,1)S(1)} %slice.138), channel_id=1, source_target_pairs={{0,1},{1,0},{2,3},{3,2},{4,5},{5,4},{6,7},{7,6},{8,9},{9,8},{10,11... | collective-permute-start | bytes 393224 | tf_op jit(solution)/shard_map/ppermute | solution.py:765

commit v3 on v2

--- a/solution.py
+++ b/solution.py
@@ -226,7 +226,7 @@
         if keep:
             hid, slope, vals, gate, mixed = (o.buf for o in outs[:5])
         else:
-            hid, vals, gate, mixed = bufs
+            hid, vals, gate = bufs
         wt = wts.get()
         for i in range(epd):
             w1t[i * hid_n : (i + 1) * hid_n, :] = w1s.get()[i].T
@@ -257,9 +257,19 @@
             for e in range(ce):
                 w = w2o.get()[e] if e < epd else w2t[e - epd]
                 vals[n, e * out_n : (e + 1) * out_n, :] = mm(w, hid[n, e * hid_n : (e + 1) * hid_n, :]).astype(BF16)
-            if keep:
-                for o in outs[:4]:
-                    o.flush(n)
+            if not keep:
+                tower = outs[-1]
+                for k in range(doms):
+                    sums = None
+                    for e in range(ce):
+                        term = mm(wt[k], vals[n, e * out_n : (e + 1) * out_n, :])
+                        term = gate[n, k * exps + e : k * exps + e + 1, :] * term
+                        sums = term if e == 0 else sums + term
+                    tower.buf[n, k * th : (k + 1) * th, :] = encode(sums)
+                tower.flush(n)
+                continue
+            for o in outs[:4]:
+                o.flush(n)
             for u in range(own // LANE):
                 part = slice(u * LANE, (u + 1) * LANE)
                 rows = [[gate[n, k * exps + e : k * exps + e + 1, part] for e in range(ce)] for k in range(doms)]
@@ -277,14 +287,12 @@
                         mixed[n, at, part] = acc[k].astype(BF16)
                     return carry
 
-                lax.fori_loop(0, out_n // 32, mix, 0, unroll=4 if keep else out_n // 32)
-            if keep:
-                outs[4].flush(n)
-            if n == 0 or not keep:
+                lax.fori_loop(0, out_n // 32, mix, 0, unroll=4)
+            outs[4].flush(n)
+            if n == 0:
                 tower = outs[-1]
                 for k in range(doms):
-                    sums = mm(wt[k], mixed[n, k * out_n : (k + 1) * out_n, :])
-                    tower.buf[n, k * th : (k + 1) * th, :] = sums if keep else encode(sums)
+                    tower.buf[n, k * th : (k + 1) * th, :] = mm(wt[k], mixed[n, k * out_n : (k + 1) * out_n, :])
                 tower.flush(n)
 
     kept = [
@@ -302,7 +310,7 @@
         pltpu.VMEM((ce * hid_n + ke, own), F32),
     ]
     if not keep:
-        scratch += [pltpu.VMEM(kept[i].shape, kept[i].dtype) for i in (0, 2, 3, 4)]
+        scratch += [pltpu.VMEM(kept[i].shape, kept[i].dtype) for i in (0, 2, 3)]
     ins = blocks + [Near(a) for a in (w1[0], w1[1], w2[0], w2[1], wt)]
     return staged(body, ins, outs, scratch, name, 40)
 

time: 98.9 us -> 98.6 us (level)
  no operation moved by 1% of the time
where the time goes in v3:
time: 98.6 us; the launch traced here: 98.4 us
  Pallas kernels  29.4 us (30%)
  starting transfers between devices  28.2 us (29%)
  blocking collectives  25 us (25%)
  waiting for transfers between devices  14.1 us (14%)
  between operations  1.09 us (1%)
    pallas_call x9, Pallas kernels, staged(): pl.pallas_call(kernel, out_shape=[o.what if isinstance(o, Near) else pltp...  29.4 us
    ppermute x26, starting transfers between devices, swap(): return lax.ppermute(value, axis, [(i, i ^ mask) for i in range(size)])  28.2 us
    all_to_all x1, blocking collectives, local(): stats = lax.all_to_all(message, BOTH, 0, 0, tiled=True)  14.1 us
    ppermute x26, waiting for transfers between devices, swap(): return lax.ppermute(value, axis, [(i, i ^ mask) for i in range(size)])  14.1 us
    all_to_all x1, blocking collectives, local(): sums = lax.all_to_all(message, BOTH, 0, 0, tiled=True)  10.9 us
  transfers between devices with their start and end apart: 26, of which 12 were waited for; matrix products, arithmetic and copies ran while one was open for 0% of the time, Pallas kernels for 16%

profile of v3, /device:TPU:0, one launch (start us, length us, event | category | flops | bytes accessed | tf_op | source)
XLA Modules:
  0.0 98.4 jit_solution(4053181867907853428)
XLA Ops:
  0.6 0.5 collective-permute-start
  1.2 0.1 collective-permute-start.1
  1.2 2.2 %prepare.1 = (bf16[512,512]{1,0:T(8,128)(2,1)S(1)}, bf16[536,512]{1,0:T(8,128)(2,1)S(1)}, bf16[2,256,256]{2,1,0:T(8,128)(2,1)S(1)}, bf16[3,128,256]{2,1,0:T(8,128)(2,1)S(1)}) custom-call(bf16[2,512,256]{2,1,0:T(8,128)(2,1)} %refs_19_.1, bf16[24,512]{1,0:T(8,128)(2,1)} %bitcast.38, bf16[2,256,256]{2,1,0:T(8,128)(2,1)} %refs_10_.1, ...), custom_call_target="tpu_custom_call" | custom-call | tf_op jit(solution)/shard_map/prepare/pallas_call | solution.py:139
  3.5 2.2 %forward_send.1 = bf16[1,384,512]{2,1,0:T(8,128)(2,1)S(1)} custom-call(bf16[512,512]{1,0:T(8,128)(2,1)S(1)} %get-tuple-element.79.refs_1_.refs_0_, bf16[536,512]{1,0:T(8,128)(2,1)S(1)} %get-tuple-element.80.refs_2_.refs_1_, bf16[2,512,256]{2,1,0:T(8,128)(2,1)S(1)} %collective-permute-done.refs_3_.refs_2_.refs_20_, ...), custom_call_target="tpu_custom_call" | custom-call | tf_op jit(solution)/shard_map/forward_send/pallas_call | solution.py:139
  5.7 3.0 %collective-permute-start.2 = (bf16[1,384,512]{2,1,0:T(8,128)(2,1)S(1)}, bf16[1,384,512]{2,1,0:T(8,128)(2,1)S(1)}, u32[]{:S(2)}, u32[]{:S(2)}) collective-permute-start(bf16[1,384,512]{2,1,0:T(8,128)(2,1)S(1)} %forward_send.1), channel_id=1, source_target_pairs={{0,2},{1,3},{2,0},{3,1},{4,6},{5,7},{6,4},{7,5},{8,10},{9,11},{10,... | collective-permute-start | bytes 1179656 | tf_op jit(solution)/shard_map/ppermute | solution.py:773
  8.7 8.2 %forward_keep.1 = (bf16[2,1024,512]{2,1,0:T(8,128)(2,1)}, bf16[2,1024,512]{2,1,0:T(8,128)(2,1)}, bf16[2,1024,512]{2,1,0:T(8,128)(2,1)}, f32[2,24,512]{2,1,0:T(8,...) custom-call(bf16[2048,512]{1,0:T(8,128)(2,1)} %refs_14_.1, ...), custom_call_target="tpu_custom_call" | custom-call | tf_op jit(solution)/shard_map/forward_keep/pallas_call | solution.py:139
  16.9 1.1 %collective-permute-done.2.refs_2_ = bf16[1,384,512]{2,1,0:T(8,128)(2,1)S(1)} collective-permute-done((bf16[1,384,512]{2,1,0:T(8,128)(2,1)S(1)}, bf16[1,384,512]{2,1,0:T(8,128)(2,1)S(1)}, u32[]{:S(2)}, u32[]{:S(2)}) %collective-permute-start.2) | collective-permute-done | bytes 393248 | tf_op jit(solution)/shard_map/ppermute | solution.py:773
  18.0 1.1 %combine.1 = (f32[384,512]{1,0:T(8,128)S(1)}, bf16[400,512]{1,0:T(8,128)(2,1)S(1)}, f32[256,128]{1,0:T(8,128)S(1)}) custom-call(f32[1,384,512]{2,1,0:T(8,128)S(1)} %get-tuple-element.83.refs_0_, s32[2,512]{1,0:T(2,128)S(1)} %pad_add_fusion.refs_1_.refs_2_.refs_3_, bf16[1,384,512]{2,1,0:T(8,128)(2,1)S(1)} %collective-permute-done.2.refs_2_), custom_call_target="tpu_custom_call" | custom-call | tf_op jit(solution)/shard_map/combine/pallas_call | solution.py:139
  19.1 14.1 %all_to_all.23 = f32[32,8,128]{2,1,0:T(8,128)S(1)} all-to-all(f32[32,8,128]{2,1,0:T(8,128)S(1)} %bitcast.36), channel_id=1, replica_groups=mesh['rows'=8,'width'=4] {'rows','width'}, dimensions={0} | all-to-all | bytes 262144 | tf_op jit(solution)/shard_map/all_to_all | solution.py:855
  33.2 0.4 collective-permute-start.3
  33.7 1.5 %normalise.1 = (f32[24,128]{1,0:T(8,128)S(1)}, f32[256,128]{1,0:T(8,128)S(1)}) custom-call(f32[256,128]{1,0:T(8,128)S(1)} %bitcast.35, f32[384,512]{1,0:T(8,128)S(1)} %get-tuple-element.87.refs_1_.refs_2_, s32[2,512]{1,0:T(2,128)S(1)} %pad_add_fusion.refs_1_.refs_2_.refs_3_, f32[3,128]{1,0:T(4,128)S(1)} %copy-done.1, f32[3,128]{1,0:T(4,128)S(1)} %copy-done.2, ...), custom_call_target="tpu_custom_call" | custom-call | tf_op jit(solution)/shard_map/normalise/pallas_call | solution.py:139
  35.2 10.9 %all_to_all.24 = f32[32,8,128]{2,1,0:T(8,128)S(1)} all-to-all(f32[32,8,128]{2,1,0:T(8,128)S(1)} %bitcast.37), channel_id=1, replica_groups=mesh['rows'=8,'width'=4] {'rows','width'}, dimensions={0} | all-to-all | bytes 262144 | tf_op jit(solution)/shard_map/all_to_all | solution.py:859
  46.1 8.5 %backward.1 = (f32[3,128]{1,0:T(4,128)}, f32[3,128]{1,0:T(4,128)}, f32[1,1]{1,0:T(1,128)}, bf16[8,128,128]{2,1,0:T(8,128)(2,1)S(1)}, bf16[8,256,128]{2,1,0:T(8,1...) custom-call(f32[256,128]{1,0:T(8,128)S(1)} %bitcast.34, ...), custom_call_target="tpu_custom_call" | custom-call | tf_op jit(solution)/shard_map/backward/pallas_call | solution.py:139
  54.6 0.3 collective-permute-start.4
  54.9 1.7 %collective-permute-done.4 = bf16[8,256,128]{2,1,0:T(8,128)(2,1)S(1)} collective-permute-done((bf16[8,256,128]{2,1,0:T(8,128)(2,1)S(1)}, bf16[8,256,128]{2,1,0:T(8,128)(2,1)S(1)}, u32[]{:S(2)}, u32[]{:S(2)}) %collective-permute-start.4) | collective-permute-done | bytes 524320 | tf_op jit(solution)/shard_map/ppermute | solution.py:773
  56.6 0.2 collective-permute-start.10
  56.8 0.3 collective-permute-start.5
  57.2 1.6 %collective-permute-start.6 = (bf16[4,256,128]{2,1,0:T(8,128)(2,1)S(1)}, bf16[4,256,128]{2,1,0:T(8,128)(2,1)S(1)}, u32[]{:S(2)}, u32[]{:S(2)}) collective-permute-start(bf16[4,256,128]{2,1,0:T(8,128)(2,1)S(1)} %add_convert_fusion), channel_id=1, source_target_pairs={{0,4},{4,0},{8,12},{12,8},{16,20},{20,16},{24,28},{28,24},{1,5},{5... | collective-permute-start | bytes 786440 | tf_op jit(solution)/shard_map/ppermute | solution.py:773
  58.8 0.4 collective-permute-start.11
  59.2 1.4 %collective-permute-start.9 = (bf16[2,128,128]{2,1,0:T(8,128)(2,1)S(1)}, bf16[2,128,128]{2,1,0:T(8,128)(2,1)S(1)}, u32[]{:S(2)}, u32[]{:S(2)}) collective-permute-start(bf16[2,128,128]{2,1,0:T(8,128)(2,1)S(1)} %get-tuple-element.153), channel_id=1, source_target_pairs={{0,24},{4,28},{8,16},{12,20},{16,8},{20,12},{24,0},{28,4},{1,25},{... | collective-permute-start | bytes 196616 | tf_op jit(solution)/shard_map/ppermute | solution.py:773
  60.6 0.8 collective-permute-start.8
  61.4 2.3 %collective-permute-start.7 = (bf16[2,128,128]{2,1,0:T(8,128)(2,1)S(1)}, bf16[2,128,128]{2,1,0:T(8,128)(2,1)S(1)}, u32[]{:S(2)}, u32[]{:S(2)}) collective-permute-start(bf16[2,128,128]{2,1,0:T(8,128)(2,1)S(1)} %get-tuple-element.155), channel_id=1, source_target_pairs={{0,8},{4,12},{8,0},{12,4},{16,24},{20,28},{24,16},{28,20},{1,9},{5... | collective-permute-start | bytes 196616 | tf_op jit(solution)/shard_map/ppermute | solution.py:773
  63.7 0.4 collective-permute-done.11
  64.2 1.1 %collective-permute-start.12 = (bf16[4,64,128]{2,1,0:T(8,128)(2,1)S(1)}, bf16[4,64,128]{2,1,0:T(8,128)(2,1)S(1)}, u32[]{:S(2)}, u32[]{:S(2)}) collective-permute-start(bf16[4,64,128]{2,1,0:T(8,128)(2,1)S(1)} %slice.198), channel_id=1, source_target_pairs={{0,4},{4,0},{8,12},{12,8},{16,20},{20,16},{24,28},{28,24},{1,5},{5... | collective-permute-start | bytes 196616 | tf_op jit(solution)/shard_map/ppermute | solution.py:773
  65.2 2.1 %backward_inputs.1 = (f32[512,512]{1,0:T(8,128)S(1)}, bf16[1,512,512]{2,1,0:T(8,128)(2,1)S(1)}) custom-call(bf16[512,1024]{1,0:T(8,128)(2,1)S(1)} %get-tuple-element.108.refs_0_, bf16[24,512]{1,0:T(8,128)(2,1)S(1)} %bitcast.39, bf16[1024,1024]{1,0:T(8,128)(2,1)S(1)} %get-tuple-element.109.refs_2_, bf16[24,1024]{1,0:T(8,128)(2,1)S(1)} %get-tuple-element.110.refs_3_), custom_call_target="tpu_custom_call" | custom-call | tf_op jit(solution)/shard_map/backward_inputs/pallas_call | solution.py:139
  67.4 0.5 collective-permute-done.8
  67.8 0.6 collective-permute-done.12
  68.5 0.1 add_bitcast_fusion
  68.7 0.2 collective-permute-start.13
  68.9 1.3 %collective-permute-start.14 = (bf16[320,128]{1,0:T(8,128)(2,1)S(1)}, bf16[320,128]{1,0:T(8,128)(2,1)S(1)}, u32[]{:S(2)}, u32[]{:S(2)}) collective-permute-start(bf16[320,128]{1,0:T(8,128)(2,1)S(1)} %get-tuple-element.119), channel_id=1, source_target_pairs={{0,16},{4,20},{8,24},{12,28},{16,0},{20,4},{24,8},{28,12},{1,17},{... | collective-permute-start | bytes 245768 | tf_op jit(solution)/shard_map/ppermute | solution.py:773
  70.2 2.9 %collective-permute-start.15 = (bf16[320,128]{1,0:T(8,128)(2,1)S(1)}, bf16[320,128]{1,0:T(8,128)(2,1)S(1)}, u32[]{:S(2)}, u32[]{:S(2)}) collective-permute-start(bf16[320,128]{1,0:T(8,128)(2,1)S(1)} %pad_maximum_fusion.4), channel_id=1, source_target_pairs={{0,24},{4,28},{8,16},{12,20},{16,8},{20,12},{24,0},{28,4},{1,25},{... | collective-permute-start | bytes 245768 | tf_op jit(solution)/shard_map/ppermute | solution.py:773
  73.1 1.0 %collective-permute-start.16 = (bf16[2,128,128]{2,1,0:T(8,128)(2,1)S(1)}, bf16[2,128,128]{2,1,0:T(8,128)(2,1)S(1)}, u32[]{:S(2)}, u32[]{:S(2)}) collective-permute-start(bf16[2,128,128]{2,1,0:T(8,128)(2,1)S(1)} %fusion.14), channel_id=1, source_target_pairs={{0,4},{4,0},{8,12},{12,8},{16,20},{20,16},{24,28},{28,24},{1,5},{5... | collective-permute-start | bytes 196616 | tf_op jit(solution)/shard_map/ppermute | solution.py:773
  74.2 1.0 %collective-permute-start.20 = (bf16[512,512]{1,0:T(8,128)(2,1)S(1)}, bf16[512,512]{1,0:T(8,128)(2,1)S(1)}, u32[]{:S(2)}, u32[]{:S(2)}) collective-permute-start(bf16[512,512]{1,0:T(8,128)(2,1)S(1)} %bitcast.40), channel_id=1, source_target_pairs={{0,2},{1,3},{2,0},{3,1},{4,6},{5,7},{6,4},{7,5},{8,10},{9,11},{10,... | collective-permute-start | bytes 1572872 | tf_op jit(solution)/shard_map/ppermute | solution.py:773
  75.1 2.3 %collective-permute-done.16 = bf16[2,128,128]{2,1,0:T(8,128)(2,1)S(1)} collective-permute-done((bf16[2,128,128]{2,1,0:T(8,128)(2,1)S(1)}, bf16[2,128,128]{2,1,0:T(8,128)(2,1)S(1)}, u32[]{:S(2)}, u32[]{:S(2)}) %collective-permute-start.16) | collective-permute-done | bytes 65568 | tf_op jit(solution)/shard_map/ppermute | solution.py:773
  77.4 0.1 collective-permute-done.14
  77.7 2.0 %collective-permute-start.19 = (bf16[320,128]{1,0:T(8,128)(2,1)S(1)}, bf16[320,128]{1,0:T(8,128)(2,1)S(1)}, u32[]{:S(2)}, u32[]{:S(2)}) collective-permute-start(bf16[320,128]{1,0:T(8,128)(2,1)S(1)} %fusion.3), channel_id=1, source_target_pairs={{0,24},{4,28},{8,16},{12,20},{16,8},{20,12},{24,0},{28,4},{1,25},{... | collective-permute-start | bytes 245768 | tf_op jit(solution)/shard_map/ppermute | solution.py:773
  79.7 1.0 collective-permute-start.18
  80.6 1.5 %collective-permute-start.17 = (bf16[320,128]{1,0:T(8,128)(2,1)S(1)}, bf16[320,128]{1,0:T(8,128)(2,1)S(1)}, u32[]{:S(2)}, u32[]{:S(2)}) collective-permute-start(bf16[320,128]{1,0:T(8,128)(2,1)S(1)} %fusion.3), channel_id=1, source_target_pairs={{0,8},{4,12},{8,0},{12,4},{16,24},{20,28},{24,16},{28,20},{1,9},{5... | collective-permute-start | bytes 245768 | tf_op jit(solution)/shard_map/ppermute | solution.py:773
  82.1 2.0 %collective-permute-done.19 = bf16[320,128]{1,0:T(8,128)(2,1)S(1)} collective-permute-done((bf16[320,128]{1,0:T(8,128)(2,1)S(1)}, bf16[320,128]{1,0:T(8,128)(2,1)S(1)}, u32[]{:S(2)}, u32[]{:S(2)}) %collective-permute-start.19) | collective-permute-done | bytes 81952 | tf_op jit(solution)/shard_map/ppermute | solution.py:773
  84.1 2.4 %collective-permute-done.18 = bf16[320,128]{1,0:T(8,128)(2,1)S(1)} collective-permute-done((bf16[320,128]{1,0:T(8,128)(2,1)S(1)}, bf16[320,128]{1,0:T(8,128)(2,1)S(1)}, u32[]{:S(2)}, u32[]{:S(2)}) %collective-permute-start.18) | collective-permute-done | bytes 81952 | tf_op jit(solution)/shard_map/ppermute | solution.py:773
  86.5 0.5 collective-permute-start.21
  87.1 2.2 %collective-permute-start.24 = (bf16[2,128,128]{2,1,0:T(8,128)(2,1)S(1)}, bf16[2,128,128]{2,1,0:T(8,128)(2,1)S(1)}, u32[]{:S(2)}, u32[]{:S(2)}) collective-permute-start(bf16[2,128,128]{2,1,0:T(8,128)(2,1)S(1)} %add_convert_fusion.1), channel_id=1, source_target_pairs={{0,24},{4,28},{8,16},{12,20},{16,8},{20,12},{24,0},{28,4},{1,25},{... | collective-permute-start | bytes 196616 | tf_op jit(solution)/shard_map/ppermute | solution.py:773
  89.2 2.2 %collective-permute-start.22 = (bf16[2,128,128]{2,1,0:T(8,128)(2,1)S(1)}, bf16[2,128,128]{2,1,0:T(8,128)(2,1)S(1)}, u32[]{:S(2)}, u32[]{:S(2)}) collective-permute-start(bf16[2,128,128]{2,1,0:T(8,128)(2,1)S(1)} %add_convert_fusion.1), channel_id=1, source_target_pairs={{0,8},{4,12},{8,0},{12,4},{16,24},{20,28},{24,16},{28,20},{1,9},{5... | collective-permute-start | bytes 196616 | tf_op jit(solution)/shard_map/ppermute | solution.py:773
  91.5 1.7 %finish_inputs.1 = f32[512,512]{1,0:T(8,128)} custom-call(f32[512,512]{1,0:T(8,128)S(1)} %get-tuple-element.135.refs_0_, bf16[512,512]{1,0:T(8,128)(2,1)S(1)} %collective-permute-done.20.refs_1_), custom_call_target="tpu_custom_call" | custom-call | tf_op jit(solution)/shard_map/finish_inputs/pallas_call | solution.py:139
  93.2 0.3 collective-permute-done.24
  93.5 1.3 %collective-permute-done.23 = bf16[2,128,128]{2,1,0:T(8,128)(2,1)S(1)} collective-permute-done((bf16[2,128,128]{2,1,0:T(8,128)(2,1)S(1)}, bf16[2,128,128]{2,1,0:T(8,128)(2,1)S(1)}, u32[]{:S(2)}, u32[]{:S(2)}) %collective-permute-start.23) | collective-permute-done | bytes 65568 | tf_op jit(solution)/shard_map/ppermute | solution.py:773
  95.0 1.3 %collective-permute-done.25.refs_2_ = bf16[8,64,128]{2,1,0:T(8,128)(2,1)S(1)} collective-permute-done((bf16[8,64,128]{2,1,0:T(8,128)(2,1)S(1)}, bf16[8,64,128]{2,1,0:T(8,128)(2,1)S(1)}, u32[]{:S(2)}, u32[]{:S(2)}) %collective-permute-start.25) | collective-permute-done | bytes 131104 | tf_op jit(solution)/shard_map/ppermute | solution.py:773
  96.3 2.0 %finish_weights.1 = (f32[2,512,256]{2,1,0:T(8,128)}, f32[2,256,256]{2,1,0:T(8,128)}, f32[3,256,128]{2,1,0:T(8,128)}, f32[24,512]{1,0:T(8,128)}, f32[3,128]{1,0:T(4,128)}) custom-call(bf16[8,128,128]{2,1,0:T(8,128)(2,1)S(1)} %pad_maximum_fusion.1.refs_0_, bf16[8,320,128]{2,1,0:T(8,128)(2,1)S(1)} %constant_dynamic-update-slice_fusion.refs_1_, ...), custom_call_target="tpu_custom_call" | custom-call | tf_op jit(solution)/shard_map/finish_weights/pallas_call | solution.py:139
  (45 shorter events, 0.7 us)
Async XLA Ops:
  0.6 2.8 %collective-permute-start = (bf16[2,512,256]{2,1,0:T(8,128)(2,1)}, bf16[2,512,256]{2,1,0:T(8,128)(2,1)S(1)}, u32[]{:S(2)}, u32[]{:S(2)}) collective-permute-start(bf16[2,512,256]{2,1,0:T(8,128)(2,1)} %refs_19_.1), channel_id=1, source_target_pairs={{0,1},{1,0},{2,3},{3,2},{4,5},{5,4},{6,7},{7,6},{8,9},{9,8},{10,11... | collective-permute-start | bytes 1572872 | tf_op jit(solution)/shard_map/ppermute | solution.py:773
  1.2 2.3 %collective-permute-start.1 = (bf16[2,256,256]{2,1,0:T(8,128)(2,1)}, bf16[2,256,256]{2,1,0:T(8,128)(2,1)S(1)}, u32[]{:S(2)}, u32[]{:S(2)}) collective-permute-start(bf16[2,256,256]{2,1,0:T(8,128)(2,1)} %refs_10_.1), channel_id=1, source_target_pairs={{0,1},{1,0},{2,3},{3,2},{4,5},{5,4},{6,7},{7,6},{8,9},{9,8},{10,11... | collective-permute-start | bytes 786440 | tf_op jit(solution)/shard_map/ppermute | solution.py:773
  3.4 5.3 %copy-start.4 = (s32[512]{0:T(512)S(1)}, s32[512]{0:T(512)}, u32[]{:S(2)}) copy-start(s32[512]{0:T(512)} %param.19) | copy-start | bytes 6148
  3.4 5.3 %copy-start.5 = (s32[512]{0:T(512)S(1)}, s32[512]{0:T(512)}, u32[]{:S(2)}) copy-start(s32[512]{0:T(512)} %param.18) | copy-start | bytes 6148
  5.7 12.3 %collective-permute-start.2 = (bf16[1,384,512]{2,1,0:T(8,128)(2,1)S(1)}, bf16[1,384,512]{2,1,0:T(8,128)(2,1)S(1)}, u32[]{:S(2)}, u32[]{:S(2)}) collective-permute-start(bf16[1,384,512]{2,1,0:T(8,128)(2,1)S(1)} %forward_send.1), channel_id=1, source_target_pairs={{0,2},{1,3},{2,0},{3,1},{4,6},{5,7},{6,4},{7,5},{8,10},{9,11},{10,... | collective-permute-start | bytes 1179656 | tf_op jit(solution)/shard_map/ppermute | solution.py:773
  8.7 25.0 %copy-start.1 = (f32[3,128]{1,0:T(4,128)S(1)}, f32[3,128]{1,0:T(4,128)}, u32[]{:S(2)}) copy-start(f32[3,128]{1,0:T(4,128)} %refs_3_.3) | copy-start | bytes 4612
  8.7 25.0 %copy-start.2 = (f32[3,128]{1,0:T(4,128)S(1)}, f32[3,128]{1,0:T(4,128)}, u32[]{:S(2)}) copy-start(f32[3,128]{1,0:T(4,128)} %refs_4_.3) | copy-start | bytes 4612
  8.7 25.0 %copy-start.3 = (f32[3,128]{1,0:T(4,128)S(1)}, f32[3,128]{1,0:T(4,128)}, u32[]{:S(2)}) copy-start(f32[3,128]{1,0:T(4,128)} %refs_5_.2) | copy-start | bytes 4612
  33.2 12.9 %collective-permute-start.3 = (bf16[400,512]{1,0:T(8,128)(2,1)S(1)}, bf16[400,512]{1,0:T(8,128)(2,1)S(1)}, u32[]{:S(2)}, u32[]{:S(2)}) collective-permute-start(bf16[400,512]{1,0:T(8,128)(2,1)S(1)} %get-tuple-element.90), channel_id=1, source_target_pairs={{0,2},{1,3},{2,0},{3,1},{4,6},{5,7},{6,4},{7,5},{8,10},{9,11},{10,... | collective-permute-start | bytes 1228808 | tf_op jit(solution)/shard_map/ppermute | solution.py:773
  54.6 10.6 %copy-start = (bf16[3,512,8]{1,2,0:T(8,128)(2,1)S(1)}, bf16[3,512,8]{1,2,0:T(8,128)(2,1)}, u32[]{:S(2)}) copy-start(bf16[3,512,8]{1,2,0:T(8,128)(2,1)} %param.13) | copy-start | bytes 73732
  54.6 2.0 %collective-permute-start.4 = (bf16[8,256,128]{2,1,0:T(8,128)(2,1)S(1)}, bf16[8,256,128]{2,1,0:T(8,128)(2,1)S(1)}, u32[]{:S(2)}, u32[]{:S(2)}) collective-permute-start(bf16[8,256,128]{2,1,0:T(8,128)(2,1)S(1)} %get-tuple-element.98), channel_id=1, source_target_pairs={{0,1},{1,0},{2,3},{3,2},{4,5},{5,4},{6,7},{7,6},{8,9},{9,8},{10,11... | collective-permute-start | bytes 1572872 | tf_op jit(solution)/shard_map/ppermute | solution.py:773
  56.6 2.1 %collective-permute-start.10 = (bf16[8,64,128]{2,1,0:T(8,128)(2,1)S(1)}, bf16[8,64,128]{2,1,0:T(8,128)(2,1)S(1)}, u32[]{:S(2)}, u32[]{:S(2)}) collective-permute-start(bf16[8,64,128]{2,1,0:T(8,128)(2,1)S(1)} %get-tuple-element.105), channel_id=1, source_target_pairs={{0,1},{1,0},{2,3},{3,2},{4,5},{5,4},{6,7},{7,6},{8,9},{9,8},{10,11... | collective-permute-start | bytes 393224 | tf_op jit(solution)/shard_map/ppermute | solution.py:773
  56.8 2.4 %collective-permute-start.5 = (bf16[8,128,128]{2,1,0:T(8,128)(2,1)S(1)}, bf16[8,128,128]{2,1,0:T(8,128)(2,1)S(1)}, u32[]{:S(2)}, u32[]{:S(2)}) collective-permute-start(bf16[8,128,128]{2,1,0:T(8,128)(2,1)S(1)} %get-tuple-element.101), channel_id=1, source_target_pairs={{0,1},{1,0},{2,3},{3,2},{4,5},{5,4},{6,7},{7,6},{8,9},{9,8},{10,11... | collective-permute-start | bytes 786440 | tf_op jit(solution)/shard_map/ppermute | solution.py:773
  57.2 10.2 %collective-permute-start.6 = (bf16[4,256,128]{2,1,0:T(8,128)(2,1)S(1)}, bf16[4,256,128]{2,1,0:T(8,128)(2,1)S(1)}, u32[]{:S(2)}, u32[]{:S(2)}) collective-permute-start(bf16[4,256,128]{2,1,0:T(8,128)(2,1)S(1)} %add_convert_fusion), channel_id=1, source_target_pairs={{0,4},{4,0},{8,12},{12,8},{16,20},{20,16},{24,28},{28,24},{1,5},{5... | collective-permute-start | bytes 786440 | tf_op jit(solution)/shard_map/ppermute | solution.py:773
  58.8 5.3 %collective-permute-start.11 = (bf16[8,64,128]{2,1,0:T(8,128)(2,1)S(1)}, bf16[8,64,128]{2,1,0:T(8,128)(2,1)S(1)}, u32[]{:S(2)}, u32[]{:S(2)}) collective-permute-start(bf16[8,64,128]{2,1,0:T(8,128)(2,1)S(1)} %fusion), channel_id=1, source_target_pairs={{0,2},{1,3},{2,0},{3,1},{4,6},{5,7},{6,4},{7,5},{8,10},{9,11},{10,... | collective-permute-start | bytes 393224 | tf_op jit(solution)/shard_map/ppermute | solution.py:773
  59.2 8.2 %collective-permute-start.9 = (bf16[2,128,128]{2,1,0:T(8,128)(2,1)S(1)}, bf16[2,128,128]{2,1,0:T(8,128)(2,1)S(1)}, u32[]{:S(2)}, u32[]{:S(2)}) collective-permute-start(bf16[2,128,128]{2,1,0:T(8,128)(2,1)S(1)} %get-tuple-element.153), channel_id=1, source_target_pairs={{0,24},{4,28},{8,16},{12,20},{16,8},{20,12},{24,0},{28,4},{1,25},{... | collective-permute-start | bytes 196616 | tf_op jit(solution)/shard_map/ppermute | solution.py:773
  60.6 7.3 %collective-permute-start.8 = (bf16[2,128,128]{2,1,0:T(8,128)(2,1)S(1)}, bf16[2,128,128]{2,1,0:T(8,128)(2,1)S(1)}, u32[]{:S(2)}, u32[]{:S(2)}) collective-permute-start(bf16[2,128,128]{2,1,0:T(8,128)(2,1)S(1)} %get-tuple-element.154), channel_id=1, source_target_pairs={{0,16},{4,20},{8,24},{12,28},{16,0},{20,4},{24,8},{28,12},{1,17},{... | collective-permute-start | bytes 196616 | tf_op jit(solution)/shard_map/ppermute | solution.py:773
  61.4 6.5 %collective-permute-start.7 = (bf16[2,128,128]{2,1,0:T(8,128)(2,1)S(1)}, bf16[2,128,128]{2,1,0:T(8,128)(2,1)S(1)}, u32[]{:S(2)}, u32[]{:S(2)}) collective-permute-start(bf16[2,128,128]{2,1,0:T(8,128)(2,1)S(1)} %get-tuple-element.155), channel_id=1, source_target_pairs={{0,8},{4,12},{8,0},{12,4},{16,24},{20,28},{24,16},{28,20},{1,9},{5... | collective-permute-start | bytes 196616 | tf_op jit(solution)/shard_map/ppermute | solution.py:773
  64.2 4.3 %collective-permute-start.12 = (bf16[4,64,128]{2,1,0:T(8,128)(2,1)S(1)}, bf16[4,64,128]{2,1,0:T(8,128)(2,1)S(1)}, u32[]{:S(2)}, u32[]{:S(2)}) collective-permute-start(bf16[4,64,128]{2,1,0:T(8,128)(2,1)S(1)} %slice.198), channel_id=1, source_target_pairs={{0,4},{4,0},{8,12},{12,8},{16,20},{20,16},{24,28},{28,24},{1,5},{5... | collective-permute-start | bytes 196616 | tf_op jit(solution)/shard_map/ppermute | solution.py:773
  68.7 8.7 %collective-permute-start.13 = (bf16[320,128]{1,0:T(8,128)(2,1)S(1)}, bf16[320,128]{1,0:T(8,128)(2,1)S(1)}, u32[]{:S(2)}, u32[]{:S(2)}) collective-permute-start(bf16[320,128]{1,0:T(8,128)(2,1)S(1)} %get-tuple-element.118), channel_id=1, source_target_pairs={{0,8},{4,12},{8,0},{12,4},{16,24},{20,28},{24,16},{28,20},{1,9},{5... | collective-permute-start | bytes 245768 | tf_op jit(solution)/shard_map/ppermute | solution.py:773
  68.9 8.7 %collective-permute-start.14 = (bf16[320,128]{1,0:T(8,128)(2,1)S(1)}, bf16[320,128]{1,0:T(8,128)(2,1)S(1)}, u32[]{:S(2)}, u32[]{:S(2)}) collective-permute-start(bf16[320,128]{1,0:T(8,128)(2,1)S(1)} %get-tuple-element.119), channel_id=1, source_target_pairs={{0,16},{4,20},{8,24},{12,28},{16,0},{20,4},{24,8},{28,12},{1,17},{... | collective-permute-start | bytes 245768 | tf_op jit(solution)/shard_map/ppermute | solution.py:773
  70.2 7.3 %collective-permute-start.15 = (bf16[320,128]{1,0:T(8,128)(2,1)S(1)}, bf16[320,128]{1,0:T(8,128)(2,1)S(1)}, u32[]{:S(2)}, u32[]{:S(2)}) collective-permute-start(bf16[320,128]{1,0:T(8,128)(2,1)S(1)} %pad_maximum_fusion.4), channel_id=1, source_target_pairs={{0,24},{4,28},{8,16},{12,20},{16,8},{20,12},{24,0},{28,4},{1,25},{... | collective-permute-start | bytes 245768 | tf_op jit(solution)/shard_map/ppermute | solution.py:773
  73.1 4.3 %collective-permute-start.16 = (bf16[2,128,128]{2,1,0:T(8,128)(2,1)S(1)}, bf16[2,128,128]{2,1,0:T(8,128)(2,1)S(1)}, u32[]{:S(2)}, u32[]{:S(2)}) collective-permute-start(bf16[2,128,128]{2,1,0:T(8,128)(2,1)S(1)} %fusion.14), channel_id=1, source_target_pairs={{0,4},{4,0},{8,12},{12,8},{16,20},{20,16},{24,28},{28,24},{1,5},{5... | collective-permute-start | bytes 196616 | tf_op jit(solution)/shard_map/ppermute | solution.py:773
  74.2 12.3 %collective-permute-start.20 = (bf16[512,512]{1,0:T(8,128)(2,1)S(1)}, bf16[512,512]{1,0:T(8,128)(2,1)S(1)}, u32[]{:S(2)}, u32[]{:S(2)}) collective-permute-start(bf16[512,512]{1,0:T(8,128)(2,1)S(1)} %bitcast.40), channel_id=1, source_target_pairs={{0,2},{1,3},{2,0},{3,1},{4,6},{5,7},{6,4},{7,5},{8,10},{9,11},{10,... | collective-permute-start | bytes 1572872 | tf_op jit(solution)/shard_map/ppermute | solution.py:773
  77.7 6.4 %collective-permute-start.19 = (bf16[320,128]{1,0:T(8,128)(2,1)S(1)}, bf16[320,128]{1,0:T(8,128)(2,1)S(1)}, u32[]{:S(2)}, u32[]{:S(2)}) collective-permute-start(bf16[320,128]{1,0:T(8,128)(2,1)S(1)} %fusion.3), channel_id=1, source_target_pairs={{0,24},{4,28},{8,16},{12,20},{16,8},{20,12},{24,0},{28,4},{1,25},{... | collective-permute-start | bytes 245768 | tf_op jit(solution)/shard_map/ppermute | solution.py:773
  79.7 6.8 %collective-permute-start.18 = (bf16[320,128]{1,0:T(8,128)(2,1)S(1)}, bf16[320,128]{1,0:T(8,128)(2,1)S(1)}, u32[]{:S(2)}, u32[]{:S(2)}) collective-permute-start(bf16[320,128]{1,0:T(8,128)(2,1)S(1)} %fusion.3), channel_id=1, source_target_pairs={{0,16},{4,20},{8,24},{12,28},{16,0},{20,4},{24,8},{28,12},{1,17},{... | collective-permute-start | bytes 245768 | tf_op jit(solution)/shard_map/ppermute | solution.py:773
  80.6 5.8 %collective-permute-start.17 = (bf16[320,128]{1,0:T(8,128)(2,1)S(1)}, bf16[320,128]{1,0:T(8,128)(2,1)S(1)}, u32[]{:S(2)}, u32[]{:S(2)}) collective-permute-start(bf16[320,128]{1,0:T(8,128)(2,1)S(1)} %fusion.3), channel_id=1, source_target_pairs={{0,8},{4,12},{8,0},{12,4},{16,24},{20,28},{24,16},{28,20},{1,9},{5... | collective-permute-start | bytes 245768 | tf_op jit(solution)/shard_map/ppermute | solution.py:773
  86.5 8.3 %collective-permute-start.21 = (bf16[4,320,128]{2,1,0:T(8,128)(2,1)S(1)}, bf16[4,320,128]{2,1,0:T(8,128)(2,1)S(1)}, u32[]{:S(2)}, u32[]{:S(2)}) collective-permute-start(bf16[4,320,128]{2,1,0:T(8,128)(2,1)S(1)} %pad_maximum_fusion), channel_id=1, source_target_pairs={{0,4},{4,0},{8,12},{12,8},{16,20},{20,16},{24,28},{28,24},{1,5},{5... | collective-permute-start | bytes 983048 | tf_op jit(solution)/shard_map/ppermute | solution.py:773
  87.1 6.4 %collective-permute-start.24 = (bf16[2,128,128]{2,1,0:T(8,128)(2,1)S(1)}, bf16[2,128,128]{2,1,0:T(8,128)(2,1)S(1)}, u32[]{:S(2)}, u32[]{:S(2)}) collective-permute-start(bf16[2,128,128]{2,1,0:T(8,128)(2,1)S(1)} %add_convert_fusion.1), channel_id=1, source_target_pairs={{0,24},{4,28},{8,16},{12,20},{16,8},{20,12},{24,0},{28,4},{1,25},{... | collective-permute-start | bytes 196616 | tf_op jit(solution)/shard_map/ppermute | solution.py:773
  89.2 5.6 %collective-permute-start.23 = (bf16[2,128,128]{2,1,0:T(8,128)(2,1)S(1)}, bf16[2,128,128]{2,1,0:T(8,128)(2,1)S(1)}, u32[]{:S(2)}, u32[]{:S(2)}) collective-permute-start(bf16[2,128,128]{2,1,0:T(8,128)(2,1)S(1)} %add_convert_fusion.1), channel_id=1, source_target_pairs={{0,16},{4,20},{8,24},{12,28},{16,0},{20,4},{24,8},{28,12},{1,17},{... | collective-permute-start | bytes 196616 | tf_op jit(solution)/shard_map/ppermute | solution.py:773
  89.2 5.6 %collective-permute-start.22 = (bf16[2,128,128]{2,1,0:T(8,128)(2,1)S(1)}, bf16[2,128,128]{2,1,0:T(8,128)(2,1)S(1)}, u32[]{:S(2)}, u32[]{:S(2)}) collective-permute-start(bf16[2,128,128]{2,1,0:T(8,128)(2,1)S(1)} %add_convert_fusion.1), channel_id=1, source_target_pairs={{0,8},{4,12},{8,0},{12,4},{16,24},{20,28},{24,16},{28,20},{1,9},{5... | collective-permute-start | bytes 196616 | tf_op jit(solution)/shard_map/ppermute | solution.py:773
  94.9 1.4 %collective-permute-start.25 = (bf16[8,64,128]{2,1,0:T(8,128)(2,1)S(1)}, bf16[8,64,128]{2,1,0:T(8,128)(2,1)S(1)}, u32[]{:S(2)}, u32[]{:S(2)}) collective-permute-start(bf16[8,64,128]{2,1,0:T(8,128)(2,1)S(1)} %slice.138), channel_id=1, source_target_pairs={{0,1},{1,0},{2,3},{3,2},{4,5},{5,4},{6,7},{7,6},{8,9},{9,8},{10,11... | collective-permute-start | bytes 393224 | tf_op jit(solution)/shard_map/ppermute | solution.py:773

commit v4 on v3

--- a/solution.py
+++ b/solution.py
@@ -823,9 +823,11 @@
     high, beside = together(([swap(first, ROWS, m) for m in far], beside))
     pair, evens = together((pair, jnp.stack([first] + high)))
     low, high = swap(evens, ROWS, 1), [swap(pair, ROWS, m) for m in far]
-    low, high, beside = together((low, high, finish_inputs(*beside)))
+    other = swap(evens[:, m_first:], WIDTH, 1)
+    other = [other, swap(other, ROWS, 1)]
+    low, high, other, beside = together((low, high, other, finish_inputs(*beside)))
     second, first = jnp.concatenate([pair] + high), jnp.concatenate([evens, low])
-    return second, first, swap(first[:, m_first:], WIDTH, 1), beside
+    return second, first, jnp.concatenate(other), beside
 
 
 def local(inputs, w_first, w_second, w_gate, w_tower, norm_scale, norm_shift, w_head, domains, labels):

time: 98.6 us -> 98.7 us (level)
  starting transfers between devices: 28.2 us -> 29.7 us
  waiting for transfers between devices: 14.1 us -> 12.6 us
    ppermute x26 -> x27, starting transfers between devices: 28.2 us -> 29.7 us  [swap(): return lax.ppermute(value, axis, [(i, i ^ mask) for i in range(size)])]
    ppermute x26 -> x27, waiting for transfers between devices: 14.1 us -> 12.6 us  [swap(): return lax.ppermute(value, axis, [(i, i ^ mask) for i in range(size)])]
  transfers between devices with their start and end apart: 26 -> 27, of which waited for: 12 -> 10; matrix products, arithmetic and copies ran while one was open for 0% -> 0% of each run, Pallas kernels for 16% -> 16%
where the time goes in v4:
time: 98.7 us; the launch traced here: 98.5 us
  starting transfers between devices  29.7 us (30%)
  Pallas kernels  29.4 us (30%)
  blocking collectives  25 us (25%)
  waiting for transfers between devices  12.6 us (13%)
  between operations  1.09 us (1%)
    ppermute x27, starting transfers between devices, swap(): return lax.ppermute(value, axis, [(i, i ^ mask) for i in range(size)])  29.7 us
    pallas_call x9, Pallas kernels, staged(): pl.pallas_call(kernel, out_shape=[o.what if isinstance(o, Near) else pltp...  29.4 us
    all_to_all x1, blocking collectives, local(): stats = lax.all_to_all(message, BOTH, 0, 0, tiled=True)  14.1 us
    ppermute x27, waiting for transfers between devices, swap(): return lax.ppermute(value, axis, [(i, i ^ mask) for i in range(size)])  12.6 us
    all_to_all x1, blocking collectives, local(): sums = lax.all_to_all(message, BOTH, 0, 0, tiled=True)  10.9 us
  transfers between devices with their start and end apart: 27, of which 10 were waited for; matrix products, arithmetic and copies ran while one was open for 0% of the time, Pallas kernels for 16%

profile of v4, /device:TPU:0, one launch (start us, length us, event | category | flops | bytes accessed | tf_op | source)
XLA Modules:
  0.0 98.5 jit_solution(15261438325004435257)
XLA Ops:
  0.6 0.5 collective-permute-start
  1.2 0.1 collective-permute-start.1
  1.2 2.2 %prepare.1 = (bf16[512,512]{1,0:T(8,128)(2,1)S(1)}, bf16[536,512]{1,0:T(8,128)(2,1)S(1)}, bf16[2,256,256]{2,1,0:T(8,128)(2,1)S(1)}, bf16[3,128,256]{2,1,0:T(8,128)(2,1)S(1)}) custom-call(bf16[2,512,256]{2,1,0:T(8,128)(2,1)} %refs_19_.1, bf16[24,512]{1,0:T(8,128)(2,1)} %bitcast.38, bf16[2,256,256]{2,1,0:T(8,128)(2,1)} %refs_10_.1, ...), custom_call_target="tpu_custom_call" | custom-call | tf_op jit(solution)/shard_map/prepare/pallas_call | solution.py:139
  3.5 2.2 %forward_send.1 = bf16[1,384,512]{2,1,0:T(8,128)(2,1)S(1)} custom-call(bf16[512,512]{1,0:T(8,128)(2,1)S(1)} %get-tuple-element.81.refs_1_.refs_0_, bf16[536,512]{1,0:T(8,128)(2,1)S(1)} %get-tuple-element.82.refs_2_.refs_1_, bf16[2,512,256]{2,1,0:T(8,128)(2,1)S(1)} %collective-permute-done.refs_3_.refs_2_.refs_20_, ...), custom_call_target="tpu_custom_call" | custom-call | tf_op jit(solution)/shard_map/forward_send/pallas_call | solution.py:139
  5.7 3.0 %collective-permute-start.2 = (bf16[1,384,512]{2,1,0:T(8,128)(2,1)S(1)}, bf16[1,384,512]{2,1,0:T(8,128)(2,1)S(1)}, u32[]{:S(2)}, u32[]{:S(2)}) collective-permute-start(bf16[1,384,512]{2,1,0:T(8,128)(2,1)S(1)} %forward_send.1), channel_id=1, source_target_pairs={{0,2},{1,3},{2,0},{3,1},{4,6},{5,7},{6,4},{7,5},{8,10},{9,11},{10,... | collective-permute-start | bytes 1179656 | tf_op jit(solution)/shard_map/ppermute | solution.py:773
  8.7 8.2 %forward_keep.1 = (bf16[2,1024,512]{2,1,0:T(8,128)(2,1)}, bf16[2,1024,512]{2,1,0:T(8,128)(2,1)}, bf16[2,1024,512]{2,1,0:T(8,128)(2,1)}, f32[2,24,512]{2,1,0:T(8,...) custom-call(bf16[2048,512]{1,0:T(8,128)(2,1)} %refs_14_.1, ...), custom_call_target="tpu_custom_call" | custom-call | tf_op jit(solution)/shard_map/forward_keep/pallas_call | solution.py:139
  16.9 1.1 %collective-permute-done.2.refs_2_ = bf16[1,384,512]{2,1,0:T(8,128)(2,1)S(1)} collective-permute-done((bf16[1,384,512]{2,1,0:T(8,128)(2,1)S(1)}, bf16[1,384,512]{2,1,0:T(8,128)(2,1)S(1)}, u32[]{:S(2)}, u32[]{:S(2)}) %collective-permute-start.2) | collective-permute-done | bytes 393248 | tf_op jit(solution)/shard_map/ppermute | solution.py:773
  18.0 1.1 %combine.1 = (f32[384,512]{1,0:T(8,128)S(1)}, bf16[400,512]{1,0:T(8,128)(2,1)S(1)}, f32[256,128]{1,0:T(8,128)S(1)}) custom-call(f32[1,384,512]{2,1,0:T(8,128)S(1)} %get-tuple-element.85.refs_0_, s32[2,512]{1,0:T(2,128)S(1)} %pad_add_fusion.refs_1_.refs_2_.refs_3_, bf16[1,384,512]{2,1,0:T(8,128)(2,1)S(1)} %collective-permute-done.2.refs_2_), custom_call_target="tpu_custom_call" | custom-call | tf_op jit(solution)/shard_map/combine/pallas_call | solution.py:139
  19.1 14.1 %all_to_all.23 = f32[32,8,128]{2,1,0:T(8,128)S(1)} all-to-all(f32[32,8,128]{2,1,0:T(8,128)S(1)} %bitcast.36), channel_id=1, replica_groups=mesh['rows'=8,'width'=4] {'rows','width'}, dimensions={0} | all-to-all | bytes 262144 | tf_op jit(solution)/shard_map/all_to_all | solution.py:857
  33.2 0.4 collective-permute-start.3
  33.7 1.5 %normalise.1 = (f32[24,128]{1,0:T(8,128)S(1)}, f32[256,128]{1,0:T(8,128)S(1)}) custom-call(f32[256,128]{1,0:T(8,128)S(1)} %bitcast.35, f32[384,512]{1,0:T(8,128)S(1)} %get-tuple-element.89.refs_1_.refs_2_, s32[2,512]{1,0:T(2,128)S(1)} %pad_add_fusion.refs_1_.refs_2_.refs_3_, f32[3,128]{1,0:T(4,128)S(1)} %copy-done.1, f32[3,128]{1,0:T(4,128)S(1)} %copy-done.2, ...), custom_call_target="tpu_custom_call" | custom-call | tf_op jit(solution)/shard_map/normalise/pallas_call | solution.py:139
  35.2 10.9 %all_to_all.24 = f32[32,8,128]{2,1,0:T(8,128)S(1)} all-to-all(f32[32,8,128]{2,1,0:T(8,128)S(1)} %bitcast.37), channel_id=1, replica_groups=mesh['rows'=8,'width'=4] {'rows','width'}, dimensions={0} | all-to-all | bytes 262144 | tf_op jit(solution)/shard_map/all_to_all | solution.py:861
  46.1 8.5 %backward.1 = (f32[3,128]{1,0:T(4,128)}, f32[3,128]{1,0:T(4,128)}, f32[1,1]{1,0:T(1,128)}, bf16[8,128,128]{2,1,0:T(8,128)(2,1)S(1)}, bf16[8,256,128]{2,1,0:T(8,1...) custom-call(f32[256,128]{1,0:T(8,128)S(1)} %bitcast.34, ...), custom_call_target="tpu_custom_call" | custom-call | tf_op jit(solution)/shard_map/backward/pallas_call | solution.py:139
  54.6 0.3 collective-permute-start.4
  54.9 1.7 %collective-permute-done.4 = bf16[8,256,128]{2,1,0:T(8,128)(2,1)S(1)} collective-permute-done((bf16[8,256,128]{2,1,0:T(8,128)(2,1)S(1)}, bf16[8,256,128]{2,1,0:T(8,128)(2,1)S(1)}, u32[]{:S(2)}, u32[]{:S(2)}) %collective-permute-start.4) | collective-permute-done | bytes 524320 | tf_op jit(solution)/shard_map/ppermute | solution.py:773
  56.6 0.2 collective-permute-start.10
  56.8 0.3 collective-permute-start.5
  57.2 1.6 %collective-permute-start.6 = (bf16[4,256,128]{2,1,0:T(8,128)(2,1)S(1)}, bf16[4,256,128]{2,1,0:T(8,128)(2,1)S(1)}, u32[]{:S(2)}, u32[]{:S(2)}) collective-permute-start(bf16[4,256,128]{2,1,0:T(8,128)(2,1)S(1)} %add_convert_fusion), channel_id=1, source_target_pairs={{0,4},{4,0},{8,12},{12,8},{16,20},{20,16},{24,28},{28,24},{1,5},{5... | collective-permute-start | bytes 786440 | tf_op jit(solution)/shard_map/ppermute | solution.py:773
  58.8 0.4 collective-permute-start.11
  59.2 1.4 %collective-permute-start.9 = (bf16[2,128,128]{2,1,0:T(8,128)(2,1)S(1)}, bf16[2,128,128]{2,1,0:T(8,128)(2,1)S(1)}, u32[]{:S(2)}, u32[]{:S(2)}) collective-permute-start(bf16[2,128,128]{2,1,0:T(8,128)(2,1)S(1)} %get-tuple-element.157), channel_id=1, source_target_pairs={{0,24},{4,28},{8,16},{12,20},{16,8},{20,12},{24,0},{28,4},{1,25},{... | collective-permute-start | bytes 196616 | tf_op jit(solution)/shard_map/ppermute | solution.py:773
  60.6 0.8 collective-permute-start.8
  61.4 2.3 %collective-permute-start.7 = (bf16[2,128,128]{2,1,0:T(8,128)(2,1)S(1)}, bf16[2,128,128]{2,1,0:T(8,128)(2,1)S(1)}, u32[]{:S(2)}, u32[]{:S(2)}) collective-permute-start(bf16[2,128,128]{2,1,0:T(8,128)(2,1)S(1)} %get-tuple-element.159), channel_id=1, source_target_pairs={{0,8},{4,12},{8,0},{12,4},{16,24},{20,28},{24,16},{28,20},{1,9},{5... | collective-permute-start | bytes 196616 | tf_op jit(solution)/shard_map/ppermute | solution.py:773
  63.7 0.4 collective-permute-done.11
  64.2 1.1 %collective-permute-start.12 = (bf16[4,64,128]{2,1,0:T(8,128)(2,1)S(1)}, bf16[4,64,128]{2,1,0:T(8,128)(2,1)S(1)}, u32[]{:S(2)}, u32[]{:S(2)}) collective-permute-start(bf16[4,64,128]{2,1,0:T(8,128)(2,1)S(1)} %slice.197), channel_id=1, source_target_pairs={{0,4},{4,0},{8,12},{12,8},{16,20},{20,16},{24,28},{28,24},{1,5},{5... | collective-permute-start | bytes 196616 | tf_op jit(solution)/shard_map/ppermute | solution.py:773
  65.2 2.1 %backward_inputs.1 = (f32[512,512]{1,0:T(8,128)S(1)}, bf16[1,512,512]{2,1,0:T(8,128)(2,1)S(1)}) custom-call(bf16[512,1024]{1,0:T(8,128)(2,1)S(1)} %get-tuple-element.110.refs_0_, bf16[24,512]{1,0:T(8,128)(2,1)S(1)} %bitcast.39, bf16[1024,1024]{1,0:T(8,128)(2,1)S(1)} %get-tuple-element.111.refs_2_, bf16[24,1024]{1,0:T(8,128)(2,1)S(1)} %get-tuple-element.112.refs_3_), custom_call_target="tpu_custom_call" | custom-call | tf_op jit(solution)/shard_map/backward_inputs/pallas_call | solution.py:139
  67.4 0.5 collective-permute-done.8
  67.8 0.6 collective-permute-done.12
  68.5 0.1 add_bitcast_fusion
  68.7 0.2 collective-permute-start.13
  68.9 1.3 %collective-permute-start.14 = (bf16[320,128]{1,0:T(8,128)(2,1)S(1)}, bf16[320,128]{1,0:T(8,128)(2,1)S(1)}, u32[]{:S(2)}, u32[]{:S(2)}) collective-permute-start(bf16[320,128]{1,0:T(8,128)(2,1)S(1)} %get-tuple-element.121), channel_id=1, source_target_pairs={{0,16},{4,20},{8,24},{12,28},{16,0},{20,4},{24,8},{28,12},{1,17},{... | collective-permute-start | bytes 245768 | tf_op jit(solution)/shard_map/ppermute | solution.py:773
  70.2 2.9 %collective-permute-start.15 = (bf16[320,128]{1,0:T(8,128)(2,1)S(1)}, bf16[320,128]{1,0:T(8,128)(2,1)S(1)}, u32[]{:S(2)}, u32[]{:S(2)}) collective-permute-start(bf16[320,128]{1,0:T(8,128)(2,1)S(1)} %pad_maximum_fusion.6), channel_id=1, source_target_pairs={{0,24},{4,28},{8,16},{12,20},{16,8},{20,12},{24,0},{28,4},{1,25},{... | collective-permute-start | bytes 245768 | tf_op jit(solution)/shard_map/ppermute | solution.py:773
  73.1 1.0 %collective-permute-start.16 = (bf16[2,128,128]{2,1,0:T(8,128)(2,1)S(1)}, bf16[2,128,128]{2,1,0:T(8,128)(2,1)S(1)}, u32[]{:S(2)}, u32[]{:S(2)}) collective-permute-start(bf16[2,128,128]{2,1,0:T(8,128)(2,1)S(1)} %fusion.14), channel_id=1, source_target_pairs={{0,4},{4,0},{8,12},{12,8},{16,20},{20,16},{24,28},{28,24},{1,5},{5... | collective-permute-start | bytes 196616 | tf_op jit(solution)/shard_map/ppermute | solution.py:773
  74.2 1.0 collective-permute-start.20
  75.1 2.3 %collective-permute-done.16 = bf16[2,128,128]{2,1,0:T(8,128)(2,1)S(1)} collective-permute-done((bf16[2,128,128]{2,1,0:T(8,128)(2,1)S(1)}, bf16[2,128,128]{2,1,0:T(8,128)(2,1)S(1)}, u32[]{:S(2)}, u32[]{:S(2)}) %collective-permute-start.16) | collective-permute-done | bytes 65568 | tf_op jit(solution)/shard_map/ppermute | solution.py:773
  77.4 0.1 collective-permute-done.14
  77.7 2.0 %collective-permute-start.19 = (bf16[320,128]{1,0:T(8,128)(2,1)S(1)}, bf16[320,128]{1,0:T(8,128)(2,1)S(1)}, u32[]{:S(2)}, u32[]{:S(2)}) collective-permute-start(bf16[320,128]{1,0:T(8,128)(2,1)S(1)} %fusion.3), channel_id=1, source_target_pairs={{0,24},{4,28},{8,16},{12,20},{16,8},{20,12},{24,0},{28,4},{1,25},{... | collective-permute-start | bytes 245768 | tf_op jit(solution)/shard_map/ppermute | solution.py:773
  79.7 1.0 collective-permute-start.18
  80.6 1.5 %collective-permute-start.17 = (bf16[320,128]{1,0:T(8,128)(2,1)S(1)}, bf16[320,128]{1,0:T(8,128)(2,1)S(1)}, u32[]{:S(2)}, u32[]{:S(2)}) collective-permute-start(bf16[320,128]{1,0:T(8,128)(2,1)S(1)} %fusion.3), channel_id=1, source_target_pairs={{0,8},{4,12},{8,0},{12,4},{16,24},{20,28},{24,16},{28,20},{1,9},{5... | collective-permute-start | bytes 245768 | tf_op jit(solution)/shard_map/ppermute | solution.py:773
  82.1 2.0 %collective-permute-done.19 = bf16[320,128]{1,0:T(8,128)(2,1)S(1)} collective-permute-done((bf16[320,128]{1,0:T(8,128)(2,1)S(1)}, bf16[320,128]{1,0:T(8,128)(2,1)S(1)}, u32[]{:S(2)}, u32[]{:S(2)}) %collective-permute-start.19) | collective-permute-done | bytes 81952 | tf_op jit(solution)/shard_map/ppermute | solution.py:773
  84.1 2.0 %collective-permute-done.18 = bf16[320,128]{1,0:T(8,128)(2,1)S(1)} collective-permute-done((bf16[320,128]{1,0:T(8,128)(2,1)S(1)}, bf16[320,128]{1,0:T(8,128)(2,1)S(1)}, u32[]{:S(2)}, u32[]{:S(2)}) %collective-permute-start.18) | collective-permute-done | bytes 81952 | tf_op jit(solution)/shard_map/ppermute | solution.py:773
  86.2 0.9 collective-permute-start.21
  87.1 2.0 %collective-permute-start.24 = (bf16[2,128,128]{2,1,0:T(8,128)(2,1)S(1)}, bf16[2,128,128]{2,1,0:T(8,128)(2,1)S(1)}, u32[]{:S(2)}, u32[]{:S(2)}) collective-permute-start(bf16[2,128,128]{2,1,0:T(8,128)(2,1)S(1)} %add_convert_fusion.1), channel_id=1, source_target_pairs={{0,24},{4,28},{8,16},{12,20},{16,8},{20,12},{24,0},{28,4},{1,25},{... | collective-permute-start | bytes 196616 | tf_op jit(solution)/shard_map/ppermute | solution.py:773
  89.2 2.4 %collective-permute-start.22 = (bf16[2,128,128]{2,1,0:T(8,128)(2,1)S(1)}, bf16[2,128,128]{2,1,0:T(8,128)(2,1)S(1)}, u32[]{:S(2)}, u32[]{:S(2)}) collective-permute-start(bf16[2,128,128]{2,1,0:T(8,128)(2,1)S(1)} %add_convert_fusion.1), channel_id=1, source_target_pairs={{0,8},{4,12},{8,0},{12,4},{16,24},{20,28},{24,16},{28,20},{1,9},{5... | collective-permute-start | bytes 196616 | tf_op jit(solution)/shard_map/ppermute | solution.py:773
  91.6 1.2 %collective-permute-start.26 = (bf16[4,64,128]{2,1,0:T(8,128)(2,1)S(1)}, bf16[4,64,128]{2,1,0:T(8,128)(2,1)S(1)}, u32[]{:S(2)}, u32[]{:S(2)}) collective-permute-start(bf16[4,64,128]{2,1,0:T(8,128)(2,1)S(1)} %collective-permute-done.25), channel_id=1, source_target_pairs={{0,4},{4,0},{8,12},{12,8},{16,20},{20,16},{24,28},{28,24},{1,5},{5... | collective-permute-start | bytes 196616 | tf_op jit(solution)/shard_map/ppermute | solution.py:773
  92.7 1.7 %finish_inputs.1 = f32[512,512]{1,0:T(8,128)} custom-call(f32[512,512]{1,0:T(8,128)S(1)} %get-tuple-element.137.refs_0_, bf16[512,512]{1,0:T(8,128)(2,1)S(1)} %collective-permute-done.20.refs_1_), custom_call_target="tpu_custom_call" | custom-call | tf_op jit(solution)/shard_map/finish_inputs/pallas_call | solution.py:139
  94.4 1.8 %collective-permute-done.23 = bf16[2,128,128]{2,1,0:T(8,128)(2,1)S(1)} collective-permute-done((bf16[2,128,128]{2,1,0:T(8,128)(2,1)S(1)}, bf16[2,128,128]{2,1,0:T(8,128)(2,1)S(1)}, u32[]{:S(2)}, u32[]{:S(2)}) %collective-permute-start.23) | collective-permute-done | bytes 65568 | tf_op jit(solution)/shard_map/ppermute | solution.py:773
  96.2 0.1 pad_maximum_fusion.refs_1_
  96.4 2.0 %finish_weights.1 = (f32[2,512,256]{2,1,0:T(8,128)}, f32[2,256,256]{2,1,0:T(8,128)}, f32[3,256,128]{2,1,0:T(8,128)}, f32[24,512]{1,0:T(8,128)}, f32[3,128]{1,0:T(4,128)}) custom-call(bf16[8,128,128]{2,1,0:T(8,128)(2,1)S(1)} %pad_maximum_fusion.2.refs_0_, bf16[8,320,128]{2,1,0:T(8,128)(2,1)S(1)} %pad_maximum_fusion.refs_1_, ...), custom_call_target="tpu_custom_call" | custom-call | tf_op jit(solution)/shard_map/finish_weights/pallas_call | solution.py:139
  (47 shorter events, 0.6 us)
Async XLA Ops:
  0.6 2.8 %collective-permute-start = (bf16[2,512,256]{2,1,0:T(8,128)(2,1)}, bf16[2,512,256]{2,1,0:T(8,128)(2,1)S(1)}, u32[]{:S(2)}, u32[]{:S(2)}) collective-permute-start(bf16[2,512,256]{2,1,0:T(8,128)(2,1)} %refs_19_.1), channel_id=1, source_target_pairs={{0,1},{1,0},{2,3},{3,2},{4,5},{5,4},{6,7},{7,6},{8,9},{9,8},{10,11... | collective-permute-start | bytes 1572872 | tf_op jit(solution)/shard_map/ppermute | solution.py:773
  1.2 2.3 %collective-permute-start.1 = (bf16[2,256,256]{2,1,0:T(8,128)(2,1)}, bf16[2,256,256]{2,1,0:T(8,128)(2,1)S(1)}, u32[]{:S(2)}, u32[]{:S(2)}) collective-permute-start(bf16[2,256,256]{2,1,0:T(8,128)(2,1)} %refs_10_.1), channel_id=1, source_target_pairs={{0,1},{1,0},{2,3},{3,2},{4,5},{5,4},{6,7},{7,6},{8,9},{9,8},{10,11... | collective-permute-start | bytes 786440 | tf_op jit(solution)/shard_map/ppermute | solution.py:773
  3.4 5.3 %copy-start.4 = (s32[512]{0:T(512)S(1)}, s32[512]{0:T(512)}, u32[]{:S(2)}) copy-start(s32[512]{0:T(512)} %param.19) | copy-start | bytes 6148
  3.4 5.3 %copy-start.5 = (s32[512]{0:T(512)S(1)}, s32[512]{0:T(512)}, u32[]{:S(2)}) copy-start(s32[512]{0:T(512)} %param.18) | copy-start | bytes 6148
  5.7 12.3 %collective-permute-start.2 = (bf16[1,384,512]{2,1,0:T(8,128)(2,1)S(1)}, bf16[1,384,512]{2,1,0:T(8,128)(2,1)S(1)}, u32[]{:S(2)}, u32[]{:S(2)}) collective-permute-start(bf16[1,384,512]{2,1,0:T(8,128)(2,1)S(1)} %forward_send.1), channel_id=1, source_target_pairs={{0,2},{1,3},{2,0},{3,1},{4,6},{5,7},{6,4},{7,5},{8,10},{9,11},{10,... | collective-permute-start | bytes 1179656 | tf_op jit(solution)/shard_map/ppermute | solution.py:773
  8.7 25.0 %copy-start.1 = (f32[3,128]{1,0:T(4,128)S(1)}, f32[3,128]{1,0:T(4,128)}, u32[]{:S(2)}) copy-start(f32[3,128]{1,0:T(4,128)} %refs_3_.3) | copy-start | bytes 4612
  8.7 25.0 %copy-start.2 = (f32[3,128]{1,0:T(4,128)S(1)}, f32[3,128]{1,0:T(4,128)}, u32[]{:S(2)}) copy-start(f32[3,128]{1,0:T(4,128)} %refs_4_.3) | copy-start | bytes 4612
  8.7 25.0 %copy-start.3 = (f32[3,128]{1,0:T(4,128)S(1)}, f32[3,128]{1,0:T(4,128)}, u32[]{:S(2)}) copy-start(f32[3,128]{1,0:T(4,128)} %refs_5_.2) | copy-start | bytes 4612
  33.2 12.9 %collective-permute-start.3 = (bf16[400,512]{1,0:T(8,128)(2,1)S(1)}, bf16[400,512]{1,0:T(8,128)(2,1)S(1)}, u32[]{:S(2)}, u32[]{:S(2)}) collective-permute-start(bf16[400,512]{1,0:T(8,128)(2,1)S(1)} %get-tuple-element.92), channel_id=1, source_target_pairs={{0,2},{1,3},{2,0},{3,1},{4,6},{5,7},{6,4},{7,5},{8,10},{9,11},{10,... | collective-permute-start | bytes 1228808 | tf_op jit(solution)/shard_map/ppermute | solution.py:773
  54.6 10.6 %copy-start = (bf16[3,512,8]{1,2,0:T(8,128)(2,1)S(1)}, bf16[3,512,8]{1,2,0:T(8,128)(2,1)}, u32[]{:S(2)}) copy-start(bf16[3,512,8]{1,2,0:T(8,128)(2,1)} %param.13) | copy-start | bytes 73732
  54.6 2.0 %collective-permute-start.4 = (bf16[8,256,128]{2,1,0:T(8,128)(2,1)S(1)}, bf16[8,256,128]{2,1,0:T(8,128)(2,1)S(1)}, u32[]{:S(2)}, u32[]{:S(2)}) collective-permute-start(bf16[8,256,128]{2,1,0:T(8,128)(2,1)S(1)} %get-tuple-element.100), channel_id=1, source_target_pairs={{0,1},{1,0},{2,3},{3,2},{4,5},{5,4},{6,7},{7,6},{8,9},{9,8},{10,11... | collective-permute-start | bytes 1572872 | tf_op jit(solution)/shard_map/ppermute | solution.py:773
  56.6 2.1 %collective-permute-start.10 = (bf16[8,64,128]{2,1,0:T(8,128)(2,1)S(1)}, bf16[8,64,128]{2,1,0:T(8,128)(2,1)S(1)}, u32[]{:S(2)}, u32[]{:S(2)}) collective-permute-start(bf16[8,64,128]{2,1,0:T(8,128)(2,1)S(1)} %get-tuple-element.107), channel_id=1, source_target_pairs={{0,1},{1,0},{2,3},{3,2},{4,5},{5,4},{6,7},{7,6},{8,9},{9,8},{10,11... | collective-permute-start | bytes 393224 | tf_op jit(solution)/shard_map/ppermute | solution.py:773
  56.8 2.4 %collective-permute-start.5 = (bf16[8,128,128]{2,1,0:T(8,128)(2,1)S(1)}, bf16[8,128,128]{2,1,0:T(8,128)(2,1)S(1)}, u32[]{:S(2)}, u32[]{:S(2)}) collective-permute-start(bf16[8,128,128]{2,1,0:T(8,128)(2,1)S(1)} %get-tuple-element.103), channel_id=1, source_target_pairs={{0,1},{1,0},{2,3},{3,2},{4,5},{5,4},{6,7},{7,6},{8,9},{9,8},{10,11... | collective-permute-start | bytes 786440 | tf_op jit(solution)/shard_map/ppermute | solution.py:773
  57.2 10.2 %collective-permute-start.6 = (bf16[4,256,128]{2,1,0:T(8,128)(2,1)S(1)}, bf16[4,256,128]{2,1,0:T(8,128)(2,1)S(1)}, u32[]{:S(2)}, u32[]{:S(2)}) collective-permute-start(bf16[4,256,128]{2,1,0:T(8,128)(2,1)S(1)} %add_convert_fusion), channel_id=1, source_target_pairs={{0,4},{4,0},{8,12},{12,8},{16,20},{20,16},{24,28},{28,24},{1,5},{5... | collective-permute-start | bytes 786440 | tf_op jit(solution)/shard_map/ppermute | solution.py:773
  58.8 5.3 %collective-permute-start.11 = (bf16[8,64,128]{2,1,0:T(8,128)(2,1)S(1)}, bf16[8,64,128]{2,1,0:T(8,128)(2,1)S(1)}, u32[]{:S(2)}, u32[]{:S(2)}) collective-permute-start(bf16[8,64,128]{2,1,0:T(8,128)(2,1)S(1)} %fusion), channel_id=1, source_target_pairs={{0,2},{1,3},{2,0},{3,1},{4,6},{5,7},{6,4},{7,5},{8,10},{9,11},{10,... | collective-permute-start | bytes 393224 | tf_op jit(solution)/shard_map/ppermute | solution.py:773
  59.2 8.2 %collective-permute-start.9 = (bf16[2,128,128]{2,1,0:T(8,128)(2,1)S(1)}, bf16[2,128,128]{2,1,0:T(8,128)(2,1)S(1)}, u32[]{:S(2)}, u32[]{:S(2)}) collective-permute-start(bf16[2,128,128]{2,1,0:T(8,128)(2,1)S(1)} %get-tuple-element.157), channel_id=1, source_target_pairs={{0,24},{4,28},{8,16},{12,20},{16,8},{20,12},{24,0},{28,4},{1,25},{... | collective-permute-start | bytes 196616 | tf_op jit(solution)/shard_map/ppermute | solution.py:773
  60.6 7.3 %collective-permute-start.8 = (bf16[2,128,128]{2,1,0:T(8,128)(2,1)S(1)}, bf16[2,128,128]{2,1,0:T(8,128)(2,1)S(1)}, u32[]{:S(2)}, u32[]{:S(2)}) collective-permute-start(bf16[2,128,128]{2,1,0:T(8,128)(2,1)S(1)} %get-tuple-element.158), channel_id=1, source_target_pairs={{0,16},{4,20},{8,24},{12,28},{16,0},{20,4},{24,8},{28,12},{1,17},{... | collective-permute-start | bytes 196616 | tf_op jit(solution)/shard_map/ppermute | solution.py:773
  61.4 6.5 %collective-permute-start.7 = (bf16[2,128,128]{2,1,0:T(8,128)(2,1)S(1)}, bf16[2,128,128]{2,1,0:T(8,128)(2,1)S(1)}, u32[]{:S(2)}, u32[]{:S(2)}) collective-permute-start(bf16[2,128,128]{2,1,0:T(8,128)(2,1)S(1)} %get-tuple-element.159), channel_id=1, source_target_pairs={{0,8},{4,12},{8,0},{12,4},{16,24},{20,28},{24,16},{28,20},{1,9},{5... | collective-permute-start | bytes 196616 | tf_op jit(solution)/shard_map/ppermute | solution.py:773
  64.2 4.3 %collective-permute-start.12 = (bf16[4,64,128]{2,1,0:T(8,128)(2,1)S(1)}, bf16[4,64,128]{2,1,0:T(8,128)(2,1)S(1)}, u32[]{:S(2)}, u32[]{:S(2)}) collective-permute-start(bf16[4,64,128]{2,1,0:T(8,128)(2,1)S(1)} %slice.197), channel_id=1, source_target_pairs={{0,4},{4,0},{8,12},{12,8},{16,20},{20,16},{24,28},{28,24},{1,5},{5... | collective-permute-start | bytes 196616 | tf_op jit(solution)/shard_map/ppermute | solution.py:773
  68.7 8.7 %collective-permute-start.13 = (bf16[320,128]{1,0:T(8,128)(2,1)S(1)}, bf16[320,128]{1,0:T(8,128)(2,1)S(1)}, u32[]{:S(2)}, u32[]{:S(2)}) collective-permute-start(bf16[320,128]{1,0:T(8,128)(2,1)S(1)} %get-tuple-element.120), channel_id=1, source_target_pairs={{0,8},{4,12},{8,0},{12,4},{16,24},{20,28},{24,16},{28,20},{1,9},{5... | collective-permute-start | bytes 245768 | tf_op jit(solution)/shard_map/ppermute | solution.py:773
  68.9 8.7 %collective-permute-start.14 = (bf16[320,128]{1,0:T(8,128)(2,1)S(1)}, bf16[320,128]{1,0:T(8,128)(2,1)S(1)}, u32[]{:S(2)}, u32[]{:S(2)}) collective-permute-start(bf16[320,128]{1,0:T(8,128)(2,1)S(1)} %get-tuple-element.121), channel_id=1, source_target_pairs={{0,16},{4,20},{8,24},{12,28},{16,0},{20,4},{24,8},{28,12},{1,17},{... | collective-permute-start | bytes 245768 | tf_op jit(solution)/shard_map/ppermute | solution.py:773
  70.2 7.3 %collective-permute-start.15 = (bf16[320,128]{1,0:T(8,128)(2,1)S(1)}, bf16[320,128]{1,0:T(8,128)(2,1)S(1)}, u32[]{:S(2)}, u32[]{:S(2)}) collective-permute-start(bf16[320,128]{1,0:T(8,128)(2,1)S(1)} %pad_maximum_fusion.6), channel_id=1, source_target_pairs={{0,24},{4,28},{8,16},{12,20},{16,8},{20,12},{24,0},{28,4},{1,25},{... | collective-permute-start | bytes 245768 | tf_op jit(solution)/shard_map/ppermute | solution.py:773
  73.1 4.3 %collective-permute-start.16 = (bf16[2,128,128]{2,1,0:T(8,128)(2,1)S(1)}, bf16[2,128,128]{2,1,0:T(8,128)(2,1)S(1)}, u32[]{:S(2)}, u32[]{:S(2)}) collective-permute-start(bf16[2,128,128]{2,1,0:T(8,128)(2,1)S(1)} %fusion.14), channel_id=1, source_target_pairs={{0,4},{4,0},{8,12},{12,8},{16,20},{20,16},{24,28},{28,24},{1,5},{5... | collective-permute-start | bytes 196616 | tf_op jit(solution)/shard_map/ppermute | solution.py:773
  74.2 12.0 %collective-permute-start.20 = (bf16[512,512]{1,0:T(8,128)(2,1)S(1)}, bf16[512,512]{1,0:T(8,128)(2,1)S(1)}, u32[]{:S(2)}, u32[]{:S(2)}) collective-permute-start(bf16[512,512]{1,0:T(8,128)(2,1)S(1)} %bitcast.40), channel_id=1, source_target_pairs={{0,2},{1,3},{2,0},{3,1},{4,6},{5,7},{6,4},{7,5},{8,10},{9,11},{10,... | collective-permute-start | bytes 1572872 | tf_op jit(solution)/shard_map/ppermute | solution.py:773
  77.7 6.4 %collective-permute-start.19 = (bf16[320,128]{1,0:T(8,128)(2,1)S(1)}, bf16[320,128]{1,0:T(8,128)(2,1)S(1)}, u32[]{:S(2)}, u32[]{:S(2)}) collective-permute-start(bf16[320,128]{1,0:T(8,128)(2,1)S(1)} %fusion.3), channel_id=1, source_target_pairs={{0,24},{4,28},{8,16},{12,20},{16,8},{20,12},{24,0},{28,4},{1,25},{... | collective-permute-start | bytes 245768 | tf_op jit(solution)/shard_map/ppermute | solution.py:773
  79.7 6.5 %collective-permute-start.18 = (bf16[320,128]{1,0:T(8,128)(2,1)S(1)}, bf16[320,128]{1,0:T(8,128)(2,1)S(1)}, u32[]{:S(2)}, u32[]{:S(2)}) collective-permute-start(bf16[320,128]{1,0:T(8,128)(2,1)S(1)} %fusion.3), channel_id=1, source_target_pairs={{0,16},{4,20},{8,24},{12,28},{16,0},{20,4},{24,8},{28,12},{1,17},{... | collective-permute-start | bytes 245768 | tf_op jit(solution)/shard_map/ppermute | solution.py:773
  80.6 5.5 %collective-permute-start.17 = (bf16[320,128]{1,0:T(8,128)(2,1)S(1)}, bf16[320,128]{1,0:T(8,128)(2,1)S(1)}, u32[]{:S(2)}, u32[]{:S(2)}) collective-permute-start(bf16[320,128]{1,0:T(8,128)(2,1)S(1)} %fusion.3), channel_id=1, source_target_pairs={{0,8},{4,12},{8,0},{12,4},{16,24},{20,28},{24,16},{28,20},{1,9},{5... | collective-permute-start | bytes 245768 | tf_op jit(solution)/shard_map/ppermute | solution.py:773
  86.2 10.0 %collective-permute-start.21 = (bf16[4,320,128]{2,1,0:T(8,128)(2,1)S(1)}, bf16[4,320,128]{2,1,0:T(8,128)(2,1)S(1)}, u32[]{:S(2)}, u32[]{:S(2)}) collective-permute-start(bf16[4,320,128]{2,1,0:T(8,128)(2,1)S(1)} %pad_maximum_fusion.1), channel_id=1, source_target_pairs={{0,4},{4,0},{8,12},{12,8},{16,20},{20,16},{24,28},{28,24},{1,5},{5... | collective-permute-start | bytes 983048 | tf_op jit(solution)/shard_map/ppermute | solution.py:773
  87.1 4.5 %collective-permute-start.25 = (bf16[4,64,128]{2,1,0:T(8,128)(2,1)S(1)}, bf16[4,64,128]{2,1,0:T(8,128)(2,1)S(1)}, u32[]{:S(2)}, u32[]{:S(2)}) collective-permute-start(bf16[4,64,128]{2,1,0:T(8,128)(2,1)S(1)} %slice.128), channel_id=1, source_target_pairs={{0,1},{1,0},{2,3},{3,2},{4,5},{5,4},{6,7},{7,6},{8,9},{9,8},{10,11... | collective-permute-start | bytes 196616 | tf_op jit(solution)/shard_map/ppermute | solution.py:773
  87.1 7.3 %collective-permute-start.24 = (bf16[2,128,128]{2,1,0:T(8,128)(2,1)S(1)}, bf16[2,128,128]{2,1,0:T(8,128)(2,1)S(1)}, u32[]{:S(2)}, u32[]{:S(2)}) collective-permute-start(bf16[2,128,128]{2,1,0:T(8,128)(2,1)S(1)} %add_convert_fusion.1), channel_id=1, source_target_pairs={{0,24},{4,28},{8,16},{12,20},{16,8},{20,12},{24,0},{28,4},{1,25},{... | collective-permute-start | bytes 196616 | tf_op jit(solution)/shard_map/ppermute | solution.py:773
  89.1 7.1 %collective-permute-start.23 = (bf16[2,128,128]{2,1,0:T(8,128)(2,1)S(1)}, bf16[2,128,128]{2,1,0:T(8,128)(2,1)S(1)}, u32[]{:S(2)}, u32[]{:S(2)}) collective-permute-start(bf16[2,128,128]{2,1,0:T(8,128)(2,1)S(1)} %add_convert_fusion.1), channel_id=1, source_target_pairs={{0,16},{4,20},{8,24},{12,28},{16,0},{20,4},{24,8},{28,12},{1,17},{... | collective-permute-start | bytes 196616 | tf_op jit(solution)/shard_map/ppermute | solution.py:773
  89.2 7.1 %collective-permute-start.22 = (bf16[2,128,128]{2,1,0:T(8,128)(2,1)S(1)}, bf16[2,128,128]{2,1,0:T(8,128)(2,1)S(1)}, u32[]{:S(2)}, u32[]{:S(2)}) collective-permute-start(bf16[2,128,128]{2,1,0:T(8,128)(2,1)S(1)} %add_convert_fusion.1), channel_id=1, source_target_pairs={{0,8},{4,12},{8,0},{12,4},{16,24},{20,28},{24,16},{28,20},{1,9},{5... | collective-permute-start | bytes 196616 | tf_op jit(solution)/shard_map/ppermute | solution.py:773
  91.6 4.7 %collective-permute-start.26 = (bf16[4,64,128]{2,1,0:T(8,128)(2,1)S(1)}, bf16[4,64,128]{2,1,0:T(8,128)(2,1)S(1)}, u32[]{:S(2)}, u32[]{:S(2)}) collective-permute-start(bf16[4,64,128]{2,1,0:T(8,128)(2,1)S(1)} %collective-permute-done.25), channel_id=1, source_target_pairs={{0,4},{4,0},{8,12},{12,8},{16,20},{20,16},{24,28},{28,24},{1,5},{5... | collective-permute-start | bytes 196616 | tf_op jit(solution)/shard_map/ppermute | solution.py:773

commit v5 on v4

--- a/solution.py
+++ b/solution.py
@@ -656,7 +656,7 @@
 
     ins = [Near(sums), Near(params), Near(tower), Near(marks)]
     ins += [Near(v) for v in low_towers]
-    ins += [Far(wtower), side_by_side(3), side_by_side(2), Far(w2[0]), Far(w2[1], moved=True), side_by_side(1)]
+    ins += [Near(wtower), side_by_side(3), side_by_side(2), Near(w2[0]), Far(w2[1], moved=True), side_by_side(1)]
     ins += [Far(inputs, (total_n, dim), row_blocks(list(range(ns)), own)), side_by_side(0), side_by_side(4)]
 
     def joined(refs, buf):

time: 98.7 us -> 98.5 us (level)
  no operation moved by 1% of the time
where the time goes in v5:
time: 98.5 us; the launch traced here: 98.3 us
  starting transfers between devices  29.6 us (30%)
  Pallas kernels  29.3 us (30%)
  blocking collectives  25 us (25%)
  waiting for transfers between devices  12.6 us (13%)
  between operations  1.11 us (1%)
    ppermute x27, starting transfers between devices, swap(): return lax.ppermute(value, axis, [(i, i ^ mask) for i in range(size)])  29.6 us
    pallas_call x9, Pallas kernels, staged(): pl.pallas_call(kernel, out_shape=[o.what if isinstance(o, Near) else pltp...  29.3 us
    all_to_all x1, blocking collectives, local(): stats = lax.all_to_all(message, BOTH, 0, 0, tiled=True)  14.1 us
    ppermute x27, waiting for transfers between devices, swap(): return lax.ppermute(value, axis, [(i, i ^ mask) for i in range(size)])  12.6 us
    all_to_all x1, blocking collectives, local(): sums = lax.all_to_all(message, BOTH, 0, 0, tiled=True)  10.9 us
  transfers between devices with their start and end apart: 27, of which 10 were waited for; matrix products, arithmetic and copies ran while one was open for 0% of the time, Pallas kernels for 16%

profile of v5, /device:TPU:0, one launch (start us, length us, event | category | flops | bytes accessed | tf_op | source)
XLA Modules:
  0.0 98.3 jit_solution(14252347437354414611)
XLA Ops:
  0.6 0.5 collective-permute-start
  1.2 0.1 collective-permute-start.1
  1.2 2.2 %prepare.1 = (bf16[512,512]{1,0:T(8,128)(2,1)S(1)}, bf16[536,512]{1,0:T(8,128)(2,1)S(1)}, bf16[2,256,256]{2,1,0:T(8,128)(2,1)S(1)}, bf16[3,128,256]{2,1,0:T(8,128)(2,1)S(1)}) custom-call(bf16[2,512,256]{2,1,0:T(8,128)(2,1)} %refs_19_.1, bf16[24,512]{1,0:T(8,128)(2,1)} %bitcast.38, bf16[2,256,256]{2,1,0:T(8,128)(2,1)} %refs_10_.1, ...), custom_call_target="tpu_custom_call" | custom-call | tf_op jit(solution)/shard_map/prepare/pallas_call | solution.py:139
  3.5 2.2 %forward_send.1 = bf16[1,384,512]{2,1,0:T(8,128)(2,1)S(1)} custom-call(bf16[512,512]{1,0:T(8,128)(2,1)S(1)} %get-tuple-element.81.refs_1_.refs_0_, bf16[536,512]{1,0:T(8,128)(2,1)S(1)} %get-tuple-element.82.refs_2_.refs_1_, bf16[2,512,256]{2,1,0:T(8,128)(2,1)S(1)} %collective-permute-done.refs_3_.refs_2_.refs_20_, ...), custom_call_target="tpu_custom_call" | custom-call | tf_op jit(solution)/shard_map/forward_send/pallas_call | solution.py:139
  5.7 3.0 %collective-permute-start.2 = (bf16[1,384,512]{2,1,0:T(8,128)(2,1)S(1)}, bf16[1,384,512]{2,1,0:T(8,128)(2,1)S(1)}, u32[]{:S(2)}, u32[]{:S(2)}) collective-permute-start(bf16[1,384,512]{2,1,0:T(8,128)(2,1)S(1)} %forward_send.1), channel_id=1, source_target_pairs={{0,2},{1,3},{2,0},{3,1},{4,6},{5,7},{6,4},{7,5},{8,10},{9,11},{10,... | collective-permute-start | bytes 1179656 | tf_op jit(solution)/shard_map/ppermute | solution.py:773
  8.7 8.2 %forward_keep.1 = (bf16[2,1024,512]{2,1,0:T(8,128)(2,1)}, bf16[2,1024,512]{2,1,0:T(8,128)(2,1)}, bf16[2,1024,512]{2,1,0:T(8,128)(2,1)}, f32[2,24,512]{2,1,0:T(8,...) custom-call(bf16[2048,512]{1,0:T(8,128)(2,1)} %refs_14_.1, ...), custom_call_target="tpu_custom_call" | custom-call | tf_op jit(solution)/shard_map/forward_keep/pallas_call | solution.py:139
  17.0 1.1 %collective-permute-done.2.refs_2_ = bf16[1,384,512]{2,1,0:T(8,128)(2,1)S(1)} collective-permute-done((bf16[1,384,512]{2,1,0:T(8,128)(2,1)S(1)}, bf16[1,384,512]{2,1,0:T(8,128)(2,1)S(1)}, u32[]{:S(2)}, u32[]{:S(2)}) %collective-permute-start.2) | collective-permute-done | bytes 393248 | tf_op jit(solution)/shard_map/ppermute | solution.py:773
  18.0 1.1 %combine.1 = (f32[384,512]{1,0:T(8,128)S(1)}, bf16[400,512]{1,0:T(8,128)(2,1)S(1)}, f32[256,128]{1,0:T(8,128)S(1)}) custom-call(f32[1,384,512]{2,1,0:T(8,128)S(1)} %get-tuple-element.85.refs_0_, s32[2,512]{1,0:T(2,128)S(1)} %pad_add_fusion.refs_1_.refs_2_.refs_3_, bf16[1,384,512]{2,1,0:T(8,128)(2,1)S(1)} %collective-permute-done.2.refs_2_), custom_call_target="tpu_custom_call" | custom-call | tf_op jit(solution)/shard_map/combine/pallas_call | solution.py:139
  19.1 14.1 %all_to_all.23 = f32[32,8,128]{2,1,0:T(8,128)S(1)} all-to-all(f32[32,8,128]{2,1,0:T(8,128)S(1)} %bitcast.36), channel_id=1, replica_groups=mesh['rows'=8,'width'=4] {'rows','width'}, dimensions={0} | all-to-all | bytes 262144 | tf_op jit(solution)/shard_map/all_to_all | solution.py:857
  33.2 0.4 collective-permute-start.3
  33.7 1.5 %normalise.1 = (f32[24,128]{1,0:T(8,128)S(1)}, f32[256,128]{1,0:T(8,128)S(1)}) custom-call(f32[256,128]{1,0:T(8,128)S(1)} %bitcast.35, f32[384,512]{1,0:T(8,128)S(1)} %get-tuple-element.89.refs_1_.refs_2_, s32[2,512]{1,0:T(2,128)S(1)} %pad_add_fusion.refs_1_.refs_2_.refs_3_, f32[3,128]{1,0:T(4,128)S(1)} %copy-done.3, f32[3,128]{1,0:T(4,128)S(1)} %copy-done.4, ...), custom_call_target="tpu_custom_call" | custom-call | tf_op jit(solution)/shard_map/normalise/pallas_call | solution.py:139
  35.2 10.9 %all_to_all.24 = f32[32,8,128]{2,1,0:T(8,128)S(1)} all-to-all(f32[32,8,128]{2,1,0:T(8,128)S(1)} %bitcast.37), channel_id=1, replica_groups=mesh['rows'=8,'width'=4] {'rows','width'}, dimensions={0} | all-to-all | bytes 262144 | tf_op jit(solution)/shard_map/all_to_all | solution.py:861
  46.1 8.4 %backward.1 = (f32[3,128]{1,0:T(4,128)}, f32[3,128]{1,0:T(4,128)}, f32[1,1]{1,0:T(1,128)}, bf16[8,128,128]{2,1,0:T(8,128)(2,1)S(1)}, bf16[8,256,128]{2,1,0:T(8,1...) custom-call(f32[256,128]{1,0:T(8,128)S(1)} %bitcast.34, ...), custom_call_target="tpu_custom_call" | custom-call | tf_op jit(solution)/shard_map/backward/pallas_call | solution.py:139
  54.5 0.2 collective-permute-start.4
  54.7 1.7 %collective-permute-done.4 = bf16[8,256,128]{2,1,0:T(8,128)(2,1)S(1)} collective-permute-done((bf16[8,256,128]{2,1,0:T(8,128)(2,1)S(1)}, bf16[8,256,128]{2,1,0:T(8,128)(2,1)S(1)}, u32[]{:S(2)}, u32[]{:S(2)}) %collective-permute-start.4) | collective-permute-done | bytes 524320 | tf_op jit(solution)/shard_map/ppermute | solution.py:773
  56.5 0.2 collective-permute-start.10
  56.7 0.3 collective-permute-start.5
  57.1 1.5 %collective-permute-start.6 = (bf16[4,256,128]{2,1,0:T(8,128)(2,1)S(1)}, bf16[4,256,128]{2,1,0:T(8,128)(2,1)S(1)}, u32[]{:S(2)}, u32[]{:S(2)}) collective-permute-start(bf16[4,256,128]{2,1,0:T(8,128)(2,1)S(1)} %add_convert_fusion), channel_id=1, source_target_pairs={{0,4},{4,0},{8,12},{12,8},{16,20},{20,16},{24,28},{28,24},{1,5},{5... | collective-permute-start | bytes 786440 | tf_op jit(solution)/shard_map/ppermute | solution.py:773
  58.6 0.4 collective-permute-start.11
  59.1 1.4 %collective-permute-start.9 = (bf16[2,128,128]{2,1,0:T(8,128)(2,1)S(1)}, bf16[2,128,128]{2,1,0:T(8,128)(2,1)S(1)}, u32[]{:S(2)}, u32[]{:S(2)}) collective-permute-start(bf16[2,128,128]{2,1,0:T(8,128)(2,1)S(1)} %get-tuple-element.157), channel_id=1, source_target_pairs={{0,24},{4,28},{8,16},{12,20},{16,8},{20,12},{24,0},{28,4},{1,25},{... | collective-permute-start | bytes 196616 | tf_op jit(solution)/shard_map/ppermute | solution.py:773
  60.4 0.9 collective-permute-start.8
  61.3 2.2 %collective-permute-start.7 = (bf16[2,128,128]{2,1,0:T(8,128)(2,1)S(1)}, bf16[2,128,128]{2,1,0:T(8,128)(2,1)S(1)}, u32[]{:S(2)}, u32[]{:S(2)}) collective-permute-start(bf16[2,128,128]{2,1,0:T(8,128)(2,1)S(1)} %get-tuple-element.159), channel_id=1, source_target_pairs={{0,8},{4,12},{8,0},{12,4},{16,24},{20,28},{24,16},{28,20},{1,9},{5... | collective-permute-start | bytes 196616 | tf_op jit(solution)/shard_map/ppermute | solution.py:773
  63.5 0.5 collective-permute-done.11
  64.0 1.1 %collective-permute-start.12 = (bf16[4,64,128]{2,1,0:T(8,128)(2,1)S(1)}, bf16[4,64,128]{2,1,0:T(8,128)(2,1)S(1)}, u32[]{:S(2)}, u32[]{:S(2)}) collective-permute-start(bf16[4,64,128]{2,1,0:T(8,128)(2,1)S(1)} %slice.197), channel_id=1, source_target_pairs={{0,4},{4,0},{8,12},{12,8},{16,20},{20,16},{24,28},{28,24},{1,5},{5... | collective-permute-start | bytes 196616 | tf_op jit(solution)/shard_map/ppermute | solution.py:773
  65.1 2.1 %backward_inputs.1 = (f32[512,512]{1,0:T(8,128)S(1)}, bf16[1,512,512]{2,1,0:T(8,128)(2,1)S(1)}) custom-call(bf16[512,1024]{1,0:T(8,128)(2,1)S(1)} %get-tuple-element.110.refs_0_, bf16[24,512]{1,0:T(8,128)(2,1)S(1)} %bitcast.39, bf16[1024,1024]{1,0:T(8,128)(2,1)S(1)} %get-tuple-element.111.refs_2_, bf16[24,1024]{1,0:T(8,128)(2,1)S(1)} %get-tuple-element.112.refs_3_), custom_call_target="tpu_custom_call" | custom-call | tf_op jit(solution)/shard_map/backward_inputs/pallas_call | solution.py:139
  67.2 0.5 collective-permute-done.8
  67.7 0.6 collective-permute-done.12
  68.4 0.1 add_bitcast_fusion
  68.6 0.2 collective-permute-start.13
  68.8 1.3 %collective-permute-start.14 = (bf16[320,128]{1,0:T(8,128)(2,1)S(1)}, bf16[320,128]{1,0:T(8,128)(2,1)S(1)}, u32[]{:S(2)}, u32[]{:S(2)}) collective-permute-start(bf16[320,128]{1,0:T(8,128)(2,1)S(1)} %get-tuple-element.121), channel_id=1, source_target_pairs={{0,16},{4,20},{8,24},{12,28},{16,0},{20,4},{24,8},{28,12},{1,17},{... | collective-permute-start | bytes 245768 | tf_op jit(solution)/shard_map/ppermute | solution.py:773
  70.1 2.9 %collective-permute-start.15 = (bf16[320,128]{1,0:T(8,128)(2,1)S(1)}, bf16[320,128]{1,0:T(8,128)(2,1)S(1)}, u32[]{:S(2)}, u32[]{:S(2)}) collective-permute-start(bf16[320,128]{1,0:T(8,128)(2,1)S(1)} %pad_maximum_fusion.6), channel_id=1, source_target_pairs={{0,24},{4,28},{8,16},{12,20},{16,8},{20,12},{24,0},{28,4},{1,25},{... | collective-permute-start | bytes 245768 | tf_op jit(solution)/shard_map/ppermute | solution.py:773
  73.0 1.0 %collective-permute-start.16 = (bf16[2,128,128]{2,1,0:T(8,128)(2,1)S(1)}, bf16[2,128,128]{2,1,0:T(8,128)(2,1)S(1)}, u32[]{:S(2)}, u32[]{:S(2)}) collective-permute-start(bf16[2,128,128]{2,1,0:T(8,128)(2,1)S(1)} %fusion.14), channel_id=1, source_target_pairs={{0,4},{4,0},{8,12},{12,8},{16,20},{20,16},{24,28},{28,24},{1,5},{5... | collective-permute-start | bytes 196616 | tf_op jit(solution)/shard_map/ppermute | solution.py:773
  74.0 1.0 %collective-permute-start.20 = (bf16[512,512]{1,0:T(8,128)(2,1)S(1)}, bf16[512,512]{1,0:T(8,128)(2,1)S(1)}, u32[]{:S(2)}, u32[]{:S(2)}) collective-permute-start(bf16[512,512]{1,0:T(8,128)(2,1)S(1)} %bitcast.40), channel_id=1, source_target_pairs={{0,2},{1,3},{2,0},{3,1},{4,6},{5,7},{6,4},{7,5},{8,10},{9,11},{10,... | collective-permute-start | bytes 1572872 | tf_op jit(solution)/shard_map/ppermute | solution.py:773
  75.0 2.3 %collective-permute-done.16 = bf16[2,128,128]{2,1,0:T(8,128)(2,1)S(1)} collective-permute-done((bf16[2,128,128]{2,1,0:T(8,128)(2,1)S(1)}, bf16[2,128,128]{2,1,0:T(8,128)(2,1)S(1)}, u32[]{:S(2)}, u32[]{:S(2)}) %collective-permute-start.16) | collective-permute-done | bytes 65568 | tf_op jit(solution)/shard_map/ppermute | solution.py:773
  77.3 0.1 collective-permute-done.14
  77.5 2.0 %collective-permute-start.19 = (bf16[320,128]{1,0:T(8,128)(2,1)S(1)}, bf16[320,128]{1,0:T(8,128)(2,1)S(1)}, u32[]{:S(2)}, u32[]{:S(2)}) collective-permute-start(bf16[320,128]{1,0:T(8,128)(2,1)S(1)} %fusion.3), channel_id=1, source_target_pairs={{0,24},{4,28},{8,16},{12,20},{16,8},{20,12},{24,0},{28,4},{1,25},{... | collective-permute-start | bytes 245768 | tf_op jit(solution)/shard_map/ppermute | solution.py:773
  79.5 1.0 collective-permute-start.18
  80.5 1.5 %collective-permute-start.17 = (bf16[320,128]{1,0:T(8,128)(2,1)S(1)}, bf16[320,128]{1,0:T(8,128)(2,1)S(1)}, u32[]{:S(2)}, u32[]{:S(2)}) collective-permute-start(bf16[320,128]{1,0:T(8,128)(2,1)S(1)} %fusion.3), channel_id=1, source_target_pairs={{0,8},{4,12},{8,0},{12,4},{16,24},{20,28},{24,16},{28,20},{1,9},{5... | collective-permute-start | bytes 245768 | tf_op jit(solution)/shard_map/ppermute | solution.py:773
  82.0 2.0 %collective-permute-done.19 = bf16[320,128]{1,0:T(8,128)(2,1)S(1)} collective-permute-done((bf16[320,128]{1,0:T(8,128)(2,1)S(1)}, bf16[320,128]{1,0:T(8,128)(2,1)S(1)}, u32[]{:S(2)}, u32[]{:S(2)}) %collective-permute-start.19) | collective-permute-done | bytes 81952 | tf_op jit(solution)/shard_map/ppermute | solution.py:773
  83.9 2.0 %collective-permute-done.18 = bf16[320,128]{1,0:T(8,128)(2,1)S(1)} collective-permute-done((bf16[320,128]{1,0:T(8,128)(2,1)S(1)}, bf16[320,128]{1,0:T(8,128)(2,1)S(1)}, u32[]{:S(2)}, u32[]{:S(2)}) %collective-permute-start.18) | collective-permute-done | bytes 81952 | tf_op jit(solution)/shard_map/ppermute | solution.py:773
  86.0 0.9 collective-permute-start.21
  87.0 2.1 %collective-permute-start.24 = (bf16[2,128,128]{2,1,0:T(8,128)(2,1)S(1)}, bf16[2,128,128]{2,1,0:T(8,128)(2,1)S(1)}, u32[]{:S(2)}, u32[]{:S(2)}) collective-permute-start(bf16[2,128,128]{2,1,0:T(8,128)(2,1)S(1)} %add_convert_fusion.1), channel_id=1, source_target_pairs={{0,24},{4,28},{8,16},{12,20},{16,8},{20,12},{24,0},{28,4},{1,25},{... | collective-permute-start | bytes 196616 | tf_op jit(solution)/shard_map/ppermute | solution.py:773
  89.0 2.4 %collective-permute-start.22 = (bf16[2,128,128]{2,1,0:T(8,128)(2,1)S(1)}, bf16[2,128,128]{2,1,0:T(8,128)(2,1)S(1)}, u32[]{:S(2)}, u32[]{:S(2)}) collective-permute-start(bf16[2,128,128]{2,1,0:T(8,128)(2,1)S(1)} %add_convert_fusion.1), channel_id=1, source_target_pairs={{0,8},{4,12},{8,0},{12,4},{16,24},{20,28},{24,16},{28,20},{1,9},{5... | collective-permute-start | bytes 196616 | tf_op jit(solution)/shard_map/ppermute | solution.py:773
  91.4 1.2 %collective-permute-start.26 = (bf16[4,64,128]{2,1,0:T(8,128)(2,1)S(1)}, bf16[4,64,128]{2,1,0:T(8,128)(2,1)S(1)}, u32[]{:S(2)}, u32[]{:S(2)}) collective-permute-start(bf16[4,64,128]{2,1,0:T(8,128)(2,1)S(1)} %collective-permute-done.25), channel_id=1, source_target_pairs={{0,4},{4,0},{8,12},{12,8},{16,20},{20,16},{24,28},{28,24},{1,5},{5... | collective-permute-start | bytes 196616 | tf_op jit(solution)/shard_map/ppermute | solution.py:773
  92.6 1.7 %finish_inputs.1 = f32[512,512]{1,0:T(8,128)} custom-call(f32[512,512]{1,0:T(8,128)S(1)} %get-tuple-element.137.refs_0_, bf16[512,512]{1,0:T(8,128)(2,1)S(1)} %collective-permute-done.20.refs_1_), custom_call_target="tpu_custom_call" | custom-call | tf_op jit(solution)/shard_map/finish_inputs/pallas_call | solution.py:139
  94.3 1.8 %collective-permute-done.23 = bf16[2,128,128]{2,1,0:T(8,128)(2,1)S(1)} collective-permute-done((bf16[2,128,128]{2,1,0:T(8,128)(2,1)S(1)}, bf16[2,128,128]{2,1,0:T(8,128)(2,1)S(1)}, u32[]{:S(2)}, u32[]{:S(2)}) %collective-permute-start.23) | collective-permute-done | bytes 65568 | tf_op jit(solution)/shard_map/ppermute | solution.py:773
  96.1 0.1 pad_maximum_fusion.refs_1_
  96.2 2.0 %finish_weights.1 = (f32[2,512,256]{2,1,0:T(8,128)}, f32[2,256,256]{2,1,0:T(8,128)}, f32[3,256,128]{2,1,0:T(8,128)}, f32[24,512]{1,0:T(8,128)}, f32[3,128]{1,0:T(4,128)}) custom-call(bf16[8,128,128]{2,1,0:T(8,128)(2,1)S(1)} %pad_maximum_fusion.2.refs_0_, bf16[8,320,128]{2,1,0:T(8,128)(2,1)S(1)} %pad_maximum_fusion.refs_1_, ...), custom_call_target="tpu_custom_call" | custom-call | tf_op jit(solution)/shard_map/finish_weights/pallas_call | solution.py:139
  (51 shorter events, 0.6 us)
Async XLA Ops:
  0.6 2.8 %collective-permute-start = (bf16[2,512,256]{2,1,0:T(8,128)(2,1)}, bf16[2,512,256]{2,1,0:T(8,128)(2,1)S(1)}, u32[]{:S(2)}, u32[]{:S(2)}) collective-permute-start(bf16[2,512,256]{2,1,0:T(8,128)(2,1)} %refs_19_.1), channel_id=1, source_target_pairs={{0,1},{1,0},{2,3},{3,2},{4,5},{5,4},{6,7},{7,6},{8,9},{9,8},{10,11... | collective-permute-start | bytes 1572872 | tf_op jit(solution)/shard_map/ppermute | solution.py:773
  1.2 2.3 %collective-permute-start.1 = (bf16[2,256,256]{2,1,0:T(8,128)(2,1)}, bf16[2,256,256]{2,1,0:T(8,128)(2,1)S(1)}, u32[]{:S(2)}, u32[]{:S(2)}) collective-permute-start(bf16[2,256,256]{2,1,0:T(8,128)(2,1)} %refs_10_.1), channel_id=1, source_target_pairs={{0,1},{1,0},{2,3},{3,2},{4,5},{5,4},{6,7},{7,6},{8,9},{9,8},{10,11... | collective-permute-start | bytes 786440 | tf_op jit(solution)/shard_map/ppermute | solution.py:773
  3.4 5.3 %copy-start.6 = (s32[512]{0:T(512)S(1)}, s32[512]{0:T(512)}, u32[]{:S(2)}) copy-start(s32[512]{0:T(512)} %param.19) | copy-start | bytes 6148
  3.4 5.3 %copy-start.7 = (s32[512]{0:T(512)S(1)}, s32[512]{0:T(512)}, u32[]{:S(2)}) copy-start(s32[512]{0:T(512)} %param.18) | copy-start | bytes 6148
  5.7 12.3 %collective-permute-start.2 = (bf16[1,384,512]{2,1,0:T(8,128)(2,1)S(1)}, bf16[1,384,512]{2,1,0:T(8,128)(2,1)S(1)}, u32[]{:S(2)}, u32[]{:S(2)}) collective-permute-start(bf16[1,384,512]{2,1,0:T(8,128)(2,1)S(1)} %forward_send.1), channel_id=1, source_target_pairs={{0,2},{1,3},{2,0},{3,1},{4,6},{5,7},{6,4},{7,5},{8,10},{9,11},{10,... | collective-permute-start | bytes 1179656 | tf_op jit(solution)/shard_map/ppermute | solution.py:773
  8.7 25.0 %copy-start.3 = (f32[3,128]{1,0:T(4,128)S(1)}, f32[3,128]{1,0:T(4,128)}, u32[]{:S(2)}) copy-start(f32[3,128]{1,0:T(4,128)} %refs_3_.3) | copy-start | bytes 4612
  8.7 25.0 %copy-start.4 = (f32[3,128]{1,0:T(4,128)S(1)}, f32[3,128]{1,0:T(4,128)}, u32[]{:S(2)}) copy-start(f32[3,128]{1,0:T(4,128)} %refs_4_.3) | copy-start | bytes 4612
  8.7 25.0 %copy-start.5 = (f32[3,128]{1,0:T(4,128)S(1)}, f32[3,128]{1,0:T(4,128)}, u32[]{:S(2)}) copy-start(f32[3,128]{1,0:T(4,128)} %refs_5_.2) | copy-start | bytes 4612
  16.9 29.2 %copy-start = (bf16[2,256,256]{2,1,0:T(8,128)(2,1)S(1)}, bf16[2,256,256]{2,1,0:T(8,128)(2,1)}, u32[]{:S(2)}) copy-start(bf16[2,256,256]{2,1,0:T(8,128)(2,1)} %refs_10_.1) | copy-start | bytes 786436
  16.9 29.2 %copy-start.1 = (bf16[3,256,128]{2,1,0:T(8,128)(2,1)S(1)}, bf16[3,256,128]{2,1,0:T(8,128)(2,1)}, u32[]{:S(2)}) copy-start(bf16[3,256,128]{2,1,0:T(8,128)(2,1)} %refs_5_.3) | copy-start | bytes 589828
  33.2 12.9 %collective-permute-start.3 = (bf16[400,512]{1,0:T(8,128)(2,1)S(1)}, bf16[400,512]{1,0:T(8,128)(2,1)S(1)}, u32[]{:S(2)}, u32[]{:S(2)}) collective-permute-start(bf16[400,512]{1,0:T(8,128)(2,1)S(1)} %get-tuple-element.92), channel_id=1, source_target_pairs={{0,2},{1,3},{2,0},{3,1},{4,6},{5,7},{6,4},{7,5},{8,10},{9,11},{10,... | collective-permute-start | bytes 1228808 | tf_op jit(solution)/shard_map/ppermute | solution.py:773
  54.5 10.6 %copy-start.2 = (bf16[3,512,8]{1,2,0:T(8,128)(2,1)S(1)}, bf16[3,512,8]{1,2,0:T(8,128)(2,1)}, u32[]{:S(2)}) copy-start(bf16[3,512,8]{1,2,0:T(8,128)(2,1)} %param.13) | copy-start | bytes 73732
  54.5 2.0 %collective-permute-start.4 = (bf16[8,256,128]{2,1,0:T(8,128)(2,1)S(1)}, bf16[8,256,128]{2,1,0:T(8,128)(2,1)S(1)}, u32[]{:S(2)}, u32[]{:S(2)}) collective-permute-start(bf16[8,256,128]{2,1,0:T(8,128)(2,1)S(1)} %get-tuple-element.100), channel_id=1, source_target_pairs={{0,1},{1,0},{2,3},{3,2},{4,5},{5,4},{6,7},{7,6},{8,9},{9,8},{10,11... | collective-permute-start | bytes 1572872 | tf_op jit(solution)/shard_map/ppermute | solution.py:773
  56.5 2.1 %collective-permute-start.10 = (bf16[8,64,128]{2,1,0:T(8,128)(2,1)S(1)}, bf16[8,64,128]{2,1,0:T(8,128)(2,1)S(1)}, u32[]{:S(2)}, u32[]{:S(2)}) collective-permute-start(bf16[8,64,128]{2,1,0:T(8,128)(2,1)S(1)} %get-tuple-element.107), channel_id=1, source_target_pairs={{0,1},{1,0},{2,3},{3,2},{4,5},{5,4},{6,7},{7,6},{8,9},{9,8},{10,11... | collective-permute-start | bytes 393224 | tf_op jit(solution)/shard_map/ppermute | solution.py:773
  56.7 2.4 %collective-permute-start.5 = (bf16[8,128,128]{2,1,0:T(8,128)(2,1)S(1)}, bf16[8,128,128]{2,1,0:T(8,128)(2,1)S(1)}, u32[]{:S(2)}, u32[]{:S(2)}) collective-permute-start(bf16[8,128,128]{2,1,0:T(8,128)(2,1)S(1)} %get-tuple-element.103), channel_id=1, source_target_pairs={{0,1},{1,0},{2,3},{3,2},{4,5},{5,4},{6,7},{7,6},{8,9},{9,8},{10,11... | collective-permute-start | bytes 786440 | tf_op jit(solution)/shard_map/ppermute | solution.py:773
  57.1 10.2 %collective-permute-start.6 = (bf16[4,256,128]{2,1,0:T(8,128)(2,1)S(1)}, bf16[4,256,128]{2,1,0:T(8,128)(2,1)S(1)}, u32[]{:S(2)}, u32[]{:S(2)}) collective-permute-start(bf16[4,256,128]{2,1,0:T(8,128)(2,1)S(1)} %add_convert_fusion), channel_id=1, source_target_pairs={{0,4},{4,0},{8,12},{12,8},{16,20},{20,16},{24,28},{28,24},{1,5},{5... | collective-permute-start | bytes 786440 | tf_op jit(solution)/shard_map/ppermute | solution.py:773
  58.6 5.3 %collective-permute-start.11 = (bf16[8,64,128]{2,1,0:T(8,128)(2,1)S(1)}, bf16[8,64,128]{2,1,0:T(8,128)(2,1)S(1)}, u32[]{:S(2)}, u32[]{:S(2)}) collective-permute-start(bf16[8,64,128]{2,1,0:T(8,128)(2,1)S(1)} %fusion), channel_id=1, source_target_pairs={{0,2},{1,3},{2,0},{3,1},{4,6},{5,7},{6,4},{7,5},{8,10},{9,11},{10,... | collective-permute-start | bytes 393224 | tf_op jit(solution)/shard_map/ppermute | solution.py:773
  59.1 8.2 %collective-permute-start.9 = (bf16[2,128,128]{2,1,0:T(8,128)(2,1)S(1)}, bf16[2,128,128]{2,1,0:T(8,128)(2,1)S(1)}, u32[]{:S(2)}, u32[]{:S(2)}) collective-permute-start(bf16[2,128,128]{2,1,0:T(8,128)(2,1)S(1)} %get-tuple-element.157), channel_id=1, source_target_pairs={{0,24},{4,28},{8,16},{12,20},{16,8},{20,12},{24,0},{28,4},{1,25},{... | collective-permute-start | bytes 196616 | tf_op jit(solution)/shard_map/ppermute | solution.py:773
  60.4 7.3 %collective-permute-start.8 = (bf16[2,128,128]{2,1,0:T(8,128)(2,1)S(1)}, bf16[2,128,128]{2,1,0:T(8,128)(2,1)S(1)}, u32[]{:S(2)}, u32[]{:S(2)}) collective-permute-start(bf16[2,128,128]{2,1,0:T(8,128)(2,1)S(1)} %get-tuple-element.158), channel_id=1, source_target_pairs={{0,16},{4,20},{8,24},{12,28},{16,0},{20,4},{24,8},{28,12},{1,17},{... | collective-permute-start | bytes 196616 | tf_op jit(solution)/shard_map/ppermute | solution.py:773
  61.3 6.5 %collective-permute-start.7 = (bf16[2,128,128]{2,1,0:T(8,128)(2,1)S(1)}, bf16[2,128,128]{2,1,0:T(8,128)(2,1)S(1)}, u32[]{:S(2)}, u32[]{:S(2)}) collective-permute-start(bf16[2,128,128]{2,1,0:T(8,128)(2,1)S(1)} %get-tuple-element.159), channel_id=1, source_target_pairs={{0,8},{4,12},{8,0},{12,4},{16,24},{20,28},{24,16},{28,20},{1,9},{5... | collective-permute-start | bytes 196616 | tf_op jit(solution)/shard_map/ppermute | solution.py:773
  64.0 4.3 %collective-permute-start.12 = (bf16[4,64,128]{2,1,0:T(8,128)(2,1)S(1)}, bf16[4,64,128]{2,1,0:T(8,128)(2,1)S(1)}, u32[]{:S(2)}, u32[]{:S(2)}) collective-permute-start(bf16[4,64,128]{2,1,0:T(8,128)(2,1)S(1)} %slice.197), channel_id=1, source_target_pairs={{0,4},{4,0},{8,12},{12,8},{16,20},{20,16},{24,28},{28,24},{1,5},{5... | collective-permute-start | bytes 196616 | tf_op jit(solution)/shard_map/ppermute | solution.py:773
  68.6 8.7 %collective-permute-start.13 = (bf16[320,128]{1,0:T(8,128)(2,1)S(1)}, bf16[320,128]{1,0:T(8,128)(2,1)S(1)}, u32[]{:S(2)}, u32[]{:S(2)}) collective-permute-start(bf16[320,128]{1,0:T(8,128)(2,1)S(1)} %get-tuple-element.120), channel_id=1, source_target_pairs={{0,8},{4,12},{8,0},{12,4},{16,24},{20,28},{24,16},{28,20},{1,9},{5... | collective-permute-start | bytes 245768 | tf_op jit(solution)/shard_map/ppermute | solution.py:773
  68.8 8.7 %collective-permute-start.14 = (bf16[320,128]{1,0:T(8,128)(2,1)S(1)}, bf16[320,128]{1,0:T(8,128)(2,1)S(1)}, u32[]{:S(2)}, u32[]{:S(2)}) collective-permute-start(bf16[320,128]{1,0:T(8,128)(2,1)S(1)} %get-tuple-element.121), channel_id=1, source_target_pairs={{0,16},{4,20},{8,24},{12,28},{16,0},{20,4},{24,8},{28,12},{1,17},{... | collective-permute-start | bytes 245768 | tf_op jit(solution)/shard_map/ppermute | solution.py:773
  70.1 7.3 %collective-permute-start.15 = (bf16[320,128]{1,0:T(8,128)(2,1)S(1)}, bf16[320,128]{1,0:T(8,128)(2,1)S(1)}, u32[]{:S(2)}, u32[]{:S(2)}) collective-permute-start(bf16[320,128]{1,0:T(8,128)(2,1)S(1)} %pad_maximum_fusion.6), channel_id=1, source_target_pairs={{0,24},{4,28},{8,16},{12,20},{16,8},{20,12},{24,0},{28,4},{1,25},{... | collective-permute-start | bytes 245768 | tf_op jit(solution)/shard_map/ppermute | solution.py:773
  73.0 4.3 %collective-permute-start.16 = (bf16[2,128,128]{2,1,0:T(8,128)(2,1)S(1)}, bf16[2,128,128]{2,1,0:T(8,128)(2,1)S(1)}, u32[]{:S(2)}, u32[]{:S(2)}) collective-permute-start(bf16[2,128,128]{2,1,0:T(8,128)(2,1)S(1)} %fusion.14), channel_id=1, source_target_pairs={{0,4},{4,0},{8,12},{12,8},{16,20},{20,16},{24,28},{28,24},{1,5},{5... | collective-permute-start | bytes 196616 | tf_op jit(solution)/shard_map/ppermute | solution.py:773
  74.0 12.0 %collective-permute-start.20 = (bf16[512,512]{1,0:T(8,128)(2,1)S(1)}, bf16[512,512]{1,0:T(8,128)(2,1)S(1)}, u32[]{:S(2)}, u32[]{:S(2)}) collective-permute-start(bf16[512,512]{1,0:T(8,128)(2,1)S(1)} %bitcast.40), channel_id=1, source_target_pairs={{0,2},{1,3},{2,0},{3,1},{4,6},{5,7},{6,4},{7,5},{8,10},{9,11},{10,... | collective-permute-start | bytes 1572872 | tf_op jit(solution)/shard_map/ppermute | solution.py:773
  77.5 6.4 %collective-permute-start.19 = (bf16[320,128]{1,0:T(8,128)(2,1)S(1)}, bf16[320,128]{1,0:T(8,128)(2,1)S(1)}, u32[]{:S(2)}, u32[]{:S(2)}) collective-permute-start(bf16[320,128]{1,0:T(8,128)(2,1)S(1)} %fusion.3), channel_id=1, source_target_pairs={{0,24},{4,28},{8,16},{12,20},{16,8},{20,12},{24,0},{28,4},{1,25},{... | collective-permute-start | bytes 245768 | tf_op jit(solution)/shard_map/ppermute | solution.py:773
  79.5 6.4 %collective-permute-start.18 = (bf16[320,128]{1,0:T(8,128)(2,1)S(1)}, bf16[320,128]{1,0:T(8,128)(2,1)S(1)}, u32[]{:S(2)}, u32[]{:S(2)}) collective-permute-start(bf16[320,128]{1,0:T(8,128)(2,1)S(1)} %fusion.3), channel_id=1, source_target_pairs={{0,16},{4,20},{8,24},{12,28},{16,0},{20,4},{24,8},{28,12},{1,17},{... | collective-permute-start | bytes 245768 | tf_op jit(solution)/shard_map/ppermute | solution.py:773
  80.5 5.5 %collective-permute-start.17 = (bf16[320,128]{1,0:T(8,128)(2,1)S(1)}, bf16[320,128]{1,0:T(8,128)(2,1)S(1)}, u32[]{:S(2)}, u32[]{:S(2)}) collective-permute-start(bf16[320,128]{1,0:T(8,128)(2,1)S(1)} %fusion.3), channel_id=1, source_target_pairs={{0,8},{4,12},{8,0},{12,4},{16,24},{20,28},{24,16},{28,20},{1,9},{5... | collective-permute-start | bytes 245768 | tf_op jit(solution)/shard_map/ppermute | solution.py:773
  86.0 10.0 %collective-permute-start.21 = (bf16[4,320,128]{2,1,0:T(8,128)(2,1)S(1)}, bf16[4,320,128]{2,1,0:T(8,128)(2,1)S(1)}, u32[]{:S(2)}, u32[]{:S(2)}) collective-permute-start(bf16[4,320,128]{2,1,0:T(8,128)(2,1)S(1)} %pad_maximum_fusion.1), channel_id=1, source_target_pairs={{0,4},{4,0},{8,12},{12,8},{16,20},{20,16},{24,28},{28,24},{1,5},{5... | collective-permute-start | bytes 983048 | tf_op jit(solution)/shard_map/ppermute | solution.py:773
  87.0 4.5 %collective-permute-start.25 = (bf16[4,64,128]{2,1,0:T(8,128)(2,1)S(1)}, bf16[4,64,128]{2,1,0:T(8,128)(2,1)S(1)}, u32[]{:S(2)}, u32[]{:S(2)}) collective-permute-start(bf16[4,64,128]{2,1,0:T(8,128)(2,1)S(1)} %slice.128), channel_id=1, source_target_pairs={{0,1},{1,0},{2,3},{3,2},{4,5},{5,4},{6,7},{7,6},{8,9},{9,8},{10,11... | collective-permute-start | bytes 196616 | tf_op jit(solution)/shard_map/ppermute | solution.py:773
  87.0 7.3 %collective-permute-start.24 = (bf16[2,128,128]{2,1,0:T(8,128)(2,1)S(1)}, bf16[2,128,128]{2,1,0:T(8,128)(2,1)S(1)}, u32[]{:S(2)}, u32[]{:S(2)}) collective-permute-start(bf16[2,128,128]{2,1,0:T(8,128)(2,1)S(1)} %add_convert_fusion.1), channel_id=1, source_target_pairs={{0,24},{4,28},{8,16},{12,20},{16,8},{20,12},{24,0},{28,4},{1,25},{... | collective-permute-start | bytes 196616 | tf_op jit(solution)/shard_map/ppermute | solution.py:773
  89.0 7.0 %collective-permute-start.23 = (bf16[2,128,128]{2,1,0:T(8,128)(2,1)S(1)}, bf16[2,128,128]{2,1,0:T(8,128)(2,1)S(1)}, u32[]{:S(2)}, u32[]{:S(2)}) collective-permute-start(bf16[2,128,128]{2,1,0:T(8,128)(2,1)S(1)} %add_convert_fusion.1), channel_id=1, source_target_pairs={{0,16},{4,20},{8,24},{12,28},{16,0},{20,4},{24,8},{28,12},{1,17},{... | collective-permute-start | bytes 196616 | tf_op jit(solution)/shard_map/ppermute | solution.py:773
  89.0 7.0 %collective-permute-start.22 = (bf16[2,128,128]{2,1,0:T(8,128)(2,1)S(1)}, bf16[2,128,128]{2,1,0:T(8,128)(2,1)S(1)}, u32[]{:S(2)}, u32[]{:S(2)}) collective-permute-start(bf16[2,128,128]{2,1,0:T(8,128)(2,1)S(1)} %add_convert_fusion.1), channel_id=1, source_target_pairs={{0,8},{4,12},{8,0},{12,4},{16,24},{20,28},{24,16},{28,20},{1,9},{5... | collective-permute-start | bytes 196616 | tf_op jit(solution)/shard_map/ppermute | solution.py:773
  91.4 4.7 %collective-permute-start.26 = (bf16[4,64,128]{2,1,0:T(8,128)(2,1)S(1)}, bf16[4,64,128]{2,1,0:T(8,128)(2,1)S(1)}, u32[]{:S(2)}, u32[]{:S(2)}) collective-permute-start(bf16[4,64,128]{2,1,0:T(8,128)(2,1)S(1)} %collective-permute-done.25), channel_id=1, source_target_pairs={{0,4},{4,0},{8,12},{12,8},{16,20},{20,16},{24,28},{28,24},{1,5},{5... | collective-permute-start | bytes 196616 | tf_op jit(solution)/shard_map/ppermute | solution.py:773
